TPU v7x, 32 devices: a whole 2x2x4 slice. The times are simulated.
32 devices in a mesh: row: 8 (over z, y), col: 4 (over x, core).
Axes of the slice: x: 2, y: 2, z: 4, core: 2. Of those that a mesh axis runs over, the one named last changes fastest.
Arguments:
- features: bfloat16 [8192, 256], P(('row', 'col')), may hold values from -6 to 6
- weight: bfloat16 [256, 256], replicated, may hold values from -0.375 to 0.375
- bias: float32 [256], replicated, may hold values from -3 to 3
- block_values: bfloat16 [8, 4, 32, 128, 128], P('row', 'col'), may hold values from -0.1875 to 0.1875
- block_target: int32 [8, 4, 32], P('row', 'col'), may hold values from 0 to 9
- block_source: int32 [8, 4, 32], P('row', 'col'), may hold values from 0 to 7
- block_count: int32 [8, 4], P('row', 'col'), may hold values from 4 to 32, as said below
- cotangent: bfloat16 [8192, 256], P(('row', 'col')), may hold values from -6 to 6
Outputs:
- output: bfloat16 [8192, 256], P(('row', 'col'))
- grad_inputs: bfloat16 [8192, 256], P(('row', 'col'))
- grad_weight: float32 [256, 256], replicated
- grad_bias: float32 [256], replicated
Inputs may be any that keep to these rules, and one draw needn't show every extreme that they name: `block_count`: slots at or after a device's count hold no adjacency block; some device uses all 32 slots.
All inputs are finite; a program needn't handle non-finite values.
Results may differ from a plain program's by a relative error of at most 0.006.
Values may be sent and summed in bfloat16 or wider, within the bound.
No kernel may reach another device: no remote copies, remote signals or barrier semaphores. Data moves between devices by JAX's collectives and lax.ppermute only.
A program may use at most 64 MiB of HBM per device.

v0:
```python
import math

import jax
import jax.numpy as jnp
from jax import lax
from jax.sharding import PartitionSpec as P

BLK = 128
HALF = 2
VB = 2


def shifted(block, axis, distance):
    devices = range(lax.axis_size(axis))
    route = [((i - distance) % len(devices), i) for i in devices]
    return lax.ppermute(block, axis, route)


def silu_slope(argument):
    sigmoid_value = jax.nn.sigmoid(argument)
    return sigmoid_value * (1.0 + argument * (1.0 - sigmoid_value))


def shards(
    features, weight, bias, block_values, block_target, block_source, block_count, cotangent
):
    span_count = 2 * HALF + 1
    slot_total = block_values.shape[2]
    group_size = min(slot_total, 32)
    group_total = slot_total // group_size
    columns = lax.axis_size("col")
    rows_own = features.shape[0]
    feature_width = features.shape[1]
    source_total = columns * VB
    dest_total = span_count * VB
    values_own = block_values[0, 0]
    target_own = block_target[0, 0]
    source_own = block_source[0, 0]
    live_count = block_count[0, 0]
    hidden = jnp.dot(features, weight, preferred_element_type=jnp.float32).astype(jnp.bfloat16)
    row_sources = lax.all_gather(hidden, "col", axis=0, tiled=True).reshape(
        source_total, BLK, feature_width
    )

    def slot_slice(slot_start):
        live_part = (slot_start + jnp.arange(group_size, dtype=jnp.int32) < live_count).astype(
            jnp.float32
        )
        return (values_own, target_own, source_own, live_part)

    def forward_group(group_index, totals):
        slot_start = group_index * group_size

        def forward_add_group(current):
            block_part, target_part, source_part, live_part = slot_slice(slot_start)
            picked = jnp.take(row_sources, source_part, axis=0)
            products = jnp.einsum(
                "sij,sjf->sif", block_part, picked, preferred_element_type=jnp.float32
            )
            selector = (
                target_part[None, :] == jnp.arange(dest_total, dtype=jnp.int32)[:, None]
            ).astype(jnp.float32) * live_part[None, :]
            return current + jnp.einsum(
                "ds,sif->dif", selector, products, precision=lax.Precision.HIGHEST
            )

        return lax.cond(slot_start < live_count, forward_add_group, lambda current: current, totals)

    partial_value = lax.fori_loop(
        0, group_total, forward_group, jnp.zeros((dest_total, BLK, feature_width), jnp.float32)
    )
    partial_value = partial_value.reshape(span_count, VB, BLK, feature_width)
    aggregate = partial_value[HALF]
    for distance in range(1, HALF + 1):
        aggregate = aggregate + shifted(partial_value[HALF + distance], "row", distance)
        aggregate = aggregate + shifted(partial_value[HALF - distance], "row", -distance)
    pre_value = aggregate.reshape(rows_own, feature_width) + bias[None, :]
    output = jax.nn.silu(pre_value).astype(jnp.bfloat16)
    grad_pre_exact = cotangent.astype(jnp.float32) * silu_slope(pre_value)
    grad_pre = grad_pre_exact.astype(jnp.bfloat16)
    local_grad = grad_pre.reshape(VB, BLK, feature_width)
    from_above = []
    behind = []
    for distance in range(1, HALF + 1):
        from_above.append(shifted(local_grad, "row", -distance))
        behind.append(shifted(local_grad, "row", distance))
    fetched = jnp.concatenate(behind[::-1] + [local_grad] + from_above, axis=0)

    def backward_group(group_index, totals):
        slot_start = group_index * group_size

        def backward_add_group(current):
            block_part, target_part, source_part, live_part = slot_slice(slot_start)
            picked = jnp.take(fetched, target_part, axis=0)
            products = jnp.einsum(
                "sji,sjf->sif", block_part, picked, preferred_element_type=jnp.float32
            )
            selector = (
                source_part[None, :] == jnp.arange(source_total, dtype=jnp.int32)[:, None]
            ).astype(jnp.float32) * live_part[None, :]
            return current + jnp.einsum(
                "bs,sif->bif", selector, products, precision=lax.Precision.HIGHEST
            )

        return lax.cond(
            slot_start < live_count, backward_add_group, lambda current: current, totals
        )

    source_terms = lax.fori_loop(
        0, group_total, backward_group, jnp.zeros((source_total, BLK, feature_width), jnp.float32)
    )
    source_terms = source_terms.reshape(source_total * BLK, feature_width)
    grad_source = lax.psum_scatter(source_terms, "col", scatter_dimension=0, tiled=True).astype(
        jnp.bfloat16
    )
    grad_inputs = lax.dot_general(
        grad_source, weight, (((1,), (1,)), ((), ())), preferred_element_type=jnp.float32
    ).astype(jnp.bfloat16)
    weight_term = lax.dot_general(
        features, grad_source, (((0,), (0,)), ((), ())), preferred_element_type=jnp.float32
    )
    bias_term = jnp.sum(grad_pre_exact, axis=0)
    weight_total, bias_total = lax.psum((weight_term, bias_term), ("row", "col"))
    normalizer = 1.0 / math.sqrt(rows_own * lax.axis_size("row") * columns)
    return (output, grad_inputs, weight_total * normalizer, bias_total * normalizer)


def solution(mesh):
    return jax.shard_map(
        shards,
        mesh=mesh,
        in_specs=(
            P(("row", "col"), None),
            P(),
            P(),
            P("row", "col", None, None, None),
            P("row", "col", None),
            P("row", "col", None),
            P("row", "col"),
            P(("row", "col"), None),
        ),
        out_specs=(P(("row", "col"), None), P(("row", "col"), None), P(), P()),
        check_vma=False,
    )
```

profile of v0, /device:TPU:0, one launch (start us, length us, event | category | flops | bytes accessed | tf_op | source)
XLA Modules:
  0.0 266.1 jit_solution(7528853167038637843)
XLA Ops:
  7.2 0.8 copy-done
  8.1 1.1 convolution_convert_fusion.1
  9.2 8.6 %all_gather.3 = bf16[1024,256]{1,0:T(8,128)(2,1)S(1)} all-gather(bf16[256,256]{1,0:T(8,128)(2,1)S(1)} %convolution_convert_fusion.1), channel_id=1, replica_groups=mesh['row'=8,'col'=4] {'col'}, dimensions={0}, use_global_device_ids=true | all-gather | bytes 655360 | tf_op jit(solution)/shard_map/all_gather | solution.py:41
  18.7 16.9 %conditional.2 = (f32[10,128,256]{2,0,1:T(8,128)S(1)}) conditional(s32[]{:T(128)} %convert_element_type.40, f32[10,128,256]{2,0,1:T(8,128)S(1)} %broadcast_in_dim.33, (s32[1,1,32]{2,1,0:T(1,128)S(1)}, s32[]{:T(128)}, s32[1,1,32]{2,1,0:T(1,128)S(1)}, bf16[1024,256]{1,0:T(8,128)(2,1)S(1)}, bf16[32,128,128]{2,1,0:T(8,128)(2,1)}, ...), branch_computations={%region_0.1_spmd, %region_1.2_spmd} | conditional | flops 395642848 | bytes 26743884 | solution.py:67
  19.4 2.0 gather_fusion
  21.5 4.6 %fusion.2 = f32[32,256,128]{2,1,0:T(8,128)} fusion(bf16[32,128,128]{2,1,0:T(8,128)(2,1)} %get-tuple-element.92, bf16[32,128,256]{2,1,0:T(8,128)(2,1)} %gather_fusion, pred[32]{0:T(512)(128)(4,1)S(1)} %get-tuple-element.113), kind=kOutput, calls=%fused_computation.4 | convolution fusion | flops 269484032 | bytes 7340064 | tf_op jit(solution)/shard_map/while/body/eval_jaxpr/cond/branch_1_fun/sij,sjf->sif/dot_general | solution.py:57
  26.1 5.5 %copy.17 = f32[32,256,128]{1,0,2:T(8,128)} copy(f32[32,256,128]{2,1,0:T(8,128)} %fusion.2) | data formatting | bytes 8388608 | tf_op jit(solution)/shard_map/while/body/eval_jaxpr/cond/branch_1_fun/sij,sjf->sif/dot_general | solution.py:57
  31.6 4.0 %fusion.5 = f32[10,128,256]{2,0,1:T(8,128)S(1)} fusion(f32[10,128,256]{2,0,1:T(8,128)S(1)} %get-tuple-element.79, f32[32,256,128]{1,0,2:T(8,128)} %copy.17, f32[32]{0:T(128)S(1)} %get-tuple-element.114, s32[32]{0:T(128)S(1)} %bitcast.60), kind=kOutput, calls=%fused_computation.7 | convolution fusion | flops 126157440 | bytes 6816000 | tf_op jit(solution)/shard_map/while/body/eval_jaxpr/cond/branch_1_fun/ds,sif->dif/dot_general | solution.py:63
  36.0 1.6 collective-permute-start
  37.6 3.2 %collective-permute-start.1 = (f32[2,128,256]{2,0,1:T(2,128)S(1)}, f32[2,128,256]{2,0,1:T(2,128)S(1)}, u32[]{:S(2)}, u32[]{:S(2)}) collective-permute-start(f32[2,128,256]{2,0,1:T(2,128)S(1)} %get-tuple-element.120), channel_id=1, source_target_pairs={{4,0},{8,4},{12,8},{16,12},{20,16},{24,20},{28,24},{0,28},{5,1},{9... | collective-permute-start | bytes 786440 | tf_op jit(solution)/shard_map/ppermute | solution.py:16
  40.8 3.8 %collective-permute-start.3 = (f32[2,128,256]{2,0,1:T(2,128)S(1)}, f32[2,128,256]{2,0,1:T(2,128)S(1)}, u32[]{:S(2)}, u32[]{:S(2)}) collective-permute-start(f32[2,128,256]{2,0,1:T(2,128)S(1)} %get-tuple-element.118), channel_id=1, source_target_pairs={{8,0},{12,4},{16,8},{20,12},{24,16},{28,20},{0,24},{4,28},{9,1},{1... | collective-permute-start | bytes 786440 | tf_op jit(solution)/shard_map/ppermute | solution.py:16
  44.6 4.7 %collective-permute-done = f32[2,128,256]{2,0,1:T(2,128)S(1)} collective-permute-done((f32[2,128,256]{2,0,1:T(2,128)S(1)}, f32[2,128,256]{2,0,1:T(2,128)S(1)}, u32[]{:S(2)}, u32[]{:S(2)}) %collective-permute-start) | collective-permute-done | bytes 262176 | tf_op jit(solution)/shard_map/ppermute | solution.py:16
  49.3 2.2 collective-permute-done.1
  51.5 4.0 %collective-permute-done.2 = f32[2,128,256]{2,0,1:T(2,128)S(1)} collective-permute-done((f32[2,128,256]{2,0,1:T(2,128)S(1)}, f32[2,128,256]{2,0,1:T(2,128)S(1)}, u32[]{:S(2)}, u32[]{:S(2)}) %collective-permute-start.2) | collective-permute-done | bytes 262176 | tf_op jit(solution)/shard_map/ppermute | solution.py:16
  55.4 2.7 collective-permute-done.3
  58.4 0.8 fusion.39
  59.2 1.6 collective-permute-start.4
  60.9 4.6 %collective-permute-start.6 = (bf16[2,128,256]{2,1,0:T(8,128)(2,1)S(1)}, bf16[2,128,256]{2,1,0:T(8,128)(2,1)S(1)}, u32[]{:S(2)}, u32[]{:S(2)}) collective-permute-start(bf16[2,128,256]{2,1,0:T(8,128)(2,1)S(1)} %bitcast.57), channel_id=1, source_target_pairs={{4,0},{8,4},{12,8},{16,12},{20,16},{24,20},{28,24},{0,28},{5,1},{9... | collective-permute-start | bytes 393224 | tf_op jit(solution)/shard_map/ppermute | solution.py:16
  65.5 0.9 collective-permute-start.7
  67.6 3.2 %collective-permute-done.5 = bf16[2,128,256]{2,1,0:T(8,128)(2,1)S(1)} collective-permute-done((bf16[2,128,256]{2,1,0:T(8,128)(2,1)S(1)}, bf16[2,128,256]{2,1,0:T(8,128)(2,1)S(1)}, u32[]{:S(2)}, u32[]{:S(2)}) %collective-permute-start.5) | collective-permute-done | bytes 131104 | tf_op jit(solution)/shard_map/ppermute | solution.py:16
  73.6 15.9 %conditional.3 = (f32[8,128,256]{2,0,1:T(8,128)S(1)}) conditional(s32[]{:T(128)} %convert_element_type.40, f32[8,128,256]{2,0,1:T(8,128)S(1)} %broadcast_in_dim.34, (s32[1,1,32]{2,1,0:T(1,128)S(1)}, s32[]{:T(128)}, s32[1,1,32]{2,1,0:T(1,128)S(1)}, bf16[10,128,256]{2,1,0:T(8,128)(2,1)}, bf16[32,128,128]{2,1,0:T(8,128)(2,1)}, ...), branch_computations={%region_2.3_spmd, %region_3.4_spmd} | conditional | flops 370411360 | bytes 26219596 | solution.py:105
  74.3 1.8 gather_fusion.1
  76.0 4.0 %fusion.19 = f32[32,256,128]{2,1,0:T(8,128)} fusion(bf16[32,128,128]{2,1,0:T(8,128)(2,1)} %get-tuple-element.98, bf16[32,128,256]{2,1,0:T(8,128)(2,1)S(1)} %gather_fusion.1, pred[32]{0:T(512)(128)(4,1)S(1)} %get-tuple-element.115), kind=kOutput, calls=%fused_computation.25 | convolution fusion | flops 269484032 | bytes 7340064 | tf_op jit(solution)/shard_map/while/body/eval_jaxpr/cond/branch_1_fun/sji,sjf->sif/dot_general | solution.py:95
  80.1 5.5 %copy.18 = f32[32,256,128]{1,0,2:T(8,128)} copy(f32[32,256,128]{2,1,0:T(8,128)} %fusion.19) | data formatting | bytes 8388608 | tf_op jit(solution)/shard_map/while/body/eval_jaxpr/cond/branch_1_fun/sji,sjf->sif/dot_general | solution.py:95
  85.6 3.9 %fusion.22 = f32[8,128,256]{2,0,1:T(8,128)S(1)} fusion(f32[8,128,256]{2,0,1:T(8,128)S(1)} %get-tuple-element.93, f32[32,256,128]{1,0,2:T(8,128)} %copy.18, f32[32]{0:T(128)S(1)} %get-tuple-element.116, s32[32]{0:T(128)S(1)} %bitcast.61), kind=kOutput, calls=%fused_computation.28 | convolution fusion | flops 100925952 | bytes 6291712 | tf_op jit(solution)/shard_map/while/body/eval_jaxpr/cond/branch_1_fun/bs,sif->bif/dot_general | solution.py:101
  89.4 1.3 copy.15
  90.8 38.7 %psum.15 = f32[256]{0:T(256)S(1)} all-reduce(f32[256]{0:T(256)S(1)} %get-tuple-element.111), channel_id=1, replica_groups=mesh['row'=8,'col'=4] {'row','col'}, use_global_device_ids=true, to_apply=%region_7.8 | all-reduce | flops 256 | bytes 2048 | tf_op jit(solution)/shard_map/psum | solution.py:123
  130.1 1.9 convolution_bitcast_fusion
  132.0 1.8 convolution_convert_fusion
  133.8 123.6 %all-reduce.2.cloned.1.call-done = f32[256,256]{0,1:T(8,128)} async-done(((f32[256,256]{0,1:T(8,128)}), f32[256,256]{0,1:T(8,128)}) %all-reduce.2.cloned.1.call-update) | async-done | bytes 262160 | tf_op jit(solution)/shard_map/psum | solution.py:123
  257.5 1.0 broadcast_multiply_fusion
  258.5 0.8 copy.16
  (38 shorter events, 7.0 us)
Async XLA Ops:
  7.2 0.9 copy-start
  7.2 11.5 %copy-start.3 = (s32[1,1,32]{2,1,0:T(1,128)S(1)}, s32[1,1,32]{2,1,0:T(1,128)}, u32[]{:S(2)}) copy-start(s32[1,1,32]{2,1,0:T(1,128)} %param.16) | copy-start | bytes 388
  7.2 11.5 %copy-start.4 = (s32[1,1,32]{2,1,0:T(1,128)S(1)}, s32[1,1,32]{2,1,0:T(1,128)}, u32[]{:S(2)}) copy-start(s32[1,1,32]{2,1,0:T(1,128)} %param.17) | copy-start | bytes 388
  7.2 122.9 %reduce-scatter.2.cloned.1.call-start = ((), (), s32[]{:S(2)}) async-start(), calls=%async_computation.1 | async-start | bytes 1310720 | tf_op jit(solution)/shard_map/reduce_scatter | solution.py:113
  35.6 22.8 %copy-start.2 = (bf16[256,256]{1,0:T(8,128)(2,1)S(1)}, bf16[256,256]{1,0:T(8,128)(2,1)}, u32[]{:S(2)}) copy-start(bf16[256,256]{1,0:T(8,128)(2,1)} %param.19) | copy-start | bytes 393220
  35.7 22.8 %copy-start.5 = (f32[256]{0:T(256)S(1)}, f32[256]{0:T(256)}, u32[]{:S(2)}) copy-start(f32[256]{0:T(256)} %param.14) | copy-start | bytes 3076
  36.0 13.3 %collective-permute-start = (f32[2,128,256]{2,0,1:T(2,128)S(1)}, f32[2,128,256]{2,0,1:T(2,128)S(1)}, u32[]{:S(2)}, u32[]{:S(2)}) collective-permute-start(f32[2,128,256]{2,0,1:T(2,128)S(1)} %get-tuple-element.117), channel_id=1, source_target_pairs={{28,0},{0,4},{4,8},{8,12},{12,16},{16,20},{20,24},{24,28},{29,1},{... | collective-permute-start | bytes 786440 | tf_op jit(solution)/shard_map/ppermute | solution.py:16
  37.6 13.9 %collective-permute-start.1 = (f32[2,128,256]{2,0,1:T(2,128)S(1)}, f32[2,128,256]{2,0,1:T(2,128)S(1)}, u32[]{:S(2)}, u32[]{:S(2)}) collective-permute-start(f32[2,128,256]{2,0,1:T(2,128)S(1)} %get-tuple-element.120), channel_id=1, source_target_pairs={{4,0},{8,4},{12,8},{16,12},{20,16},{24,20},{28,24},{0,28},{5,1},{9... | collective-permute-start | bytes 786440 | tf_op jit(solution)/shard_map/ppermute | solution.py:16
  40.8 14.7 %collective-permute-start.2 = (f32[2,128,256]{2,0,1:T(2,128)S(1)}, f32[2,128,256]{2,0,1:T(2,128)S(1)}, u32[]{:S(2)}, u32[]{:S(2)}) collective-permute-start(f32[2,128,256]{2,0,1:T(2,128)S(1)} %get-tuple-element.119), channel_id=1, source_target_pairs={{24,0},{28,4},{0,8},{4,12},{8,16},{12,20},{16,24},{20,28},{25,1},{... | collective-permute-start | bytes 786440 | tf_op jit(solution)/shard_map/ppermute | solution.py:16
  40.8 17.3 %collective-permute-start.3 = (f32[2,128,256]{2,0,1:T(2,128)S(1)}, f32[2,128,256]{2,0,1:T(2,128)S(1)}, u32[]{:S(2)}, u32[]{:S(2)}) collective-permute-start(f32[2,128,256]{2,0,1:T(2,128)S(1)} %get-tuple-element.118), channel_id=1, source_target_pairs={{8,0},{12,4},{16,8},{20,12},{24,16},{28,20},{0,24},{4,28},{9,1},{1... | collective-permute-start | bytes 786440 | tf_op jit(solution)/shard_map/ppermute | solution.py:16
  59.2 7.7 %collective-permute-start.4 = (bf16[2,128,256]{2,1,0:T(8,128)(2,1)S(1)}, bf16[2,128,256]{2,1,0:T(8,128)(2,1)S(1)}, u32[]{:S(2)}, u32[]{:S(2)}) collective-permute-start(bf16[2,128,256]{2,1,0:T(8,128)(2,1)S(1)} %bitcast.55), channel_id=1, source_target_pairs={{24,0},{28,4},{0,8},{4,12},{8,16},{12,20},{16,24},{20,28},{25,1},{... | collective-permute-start | bytes 393224 | tf_op jit(solution)/shard_map/ppermute | solution.py:16
  60.8 10.0 %collective-permute-start.5 = (bf16[2,128,256]{2,1,0:T(8,128)(2,1)S(1)}, bf16[2,128,256]{2,1,0:T(8,128)(2,1)S(1)}, u32[]{:S(2)}, u32[]{:S(2)}) collective-permute-start(bf16[2,128,256]{2,1,0:T(8,128)(2,1)S(1)} %bitcast.56), channel_id=1, source_target_pairs={{28,0},{0,4},{4,8},{8,12},{12,16},{16,20},{20,24},{24,28},{29,1},{... | collective-permute-start | bytes 393224 | tf_op jit(solution)/shard_map/ppermute | solution.py:16
  60.9 11.2 %collective-permute-start.6 = (bf16[2,128,256]{2,1,0:T(8,128)(2,1)S(1)}, bf16[2,128,256]{2,1,0:T(8,128)(2,1)S(1)}, u32[]{:S(2)}, u32[]{:S(2)}) collective-permute-start(bf16[2,128,256]{2,1,0:T(8,128)(2,1)S(1)} %bitcast.57), channel_id=1, source_target_pairs={{4,0},{8,4},{12,8},{16,12},{20,16},{24,20},{28,24},{0,28},{5,1},{9... | collective-permute-start | bytes 393224 | tf_op jit(solution)/shard_map/ppermute | solution.py:16
  65.5 7.3 %collective-permute-start.7 = (bf16[2,128,256]{2,1,0:T(8,128)(2,1)S(1)}, bf16[2,128,256]{2,1,0:T(8,128)(2,1)S(1)}, u32[]{:S(2)}, u32[]{:S(2)}) collective-permute-start(bf16[2,128,256]{2,1,0:T(8,128)(2,1)S(1)} %bitcast.58), channel_id=1, source_target_pairs={{8,0},{12,4},{16,8},{20,12},{24,16},{28,20},{0,24},{4,28},{9,1},{1... | collective-permute-start | bytes 393224 | tf_op jit(solution)/shard_map/ppermute | solution.py:16
  89.4 42.6 %copy-start.1 = (bf16[256,256]{1,0:T(8,128)(2,1)S(1)}, bf16[256,256]{1,0:T(8,128)(2,1)}, u32[]{:S(2)}) copy-start(bf16[256,256]{1,0:T(8,128)(2,1)} %param.13) | copy-start | bytes 393220
  90.8 166.7 %all-reduce.2.cloned.1.call-start = ((), (), s32[]{:S(2)}) async-start(), calls=%async_computation.2 | async-start | bytes 524288 | tf_op jit(solution)/shard_map/psum | solution.py:123
Sparse Core Ops, SparseCore 0:
  90.9 22.9 reduce-scatter.1
  132.1 125.3 all-reduce.1
where the time goes:
time: 267 us; the launch traced here: 266 us
  waiting for transfers between devices  141 us (53%)
  blocking collectives  47.3 us (18%)
  local copies, waits for them, and re-layouts  21.8 us (8%)
  matrix products  21.3 us (8%)
  starting transfers between devices  15.8 us (6%)
  between operations  14.8 us (6%)
  other arithmetic  3.98 us (1%)
    psum x1, waiting for transfers between devices, shards(): lax.psum((weight_term, bias_term), ('row', 'col'))  124 us
    psum x1, blocking collectives, shards(): lax.psum((weight_term, bias_term), ('row', 'col'))  38.7 us
    ppermute x8, waiting for transfers between devices, shifted(): return lax.ppermute(block, axis, route)  17.3 us
    ppermute x8, starting transfers between devices, shifted(): return lax.ppermute(block, axis, route)  15.8 us
    all_gather x1, blocking collectives, shards(): lax.all_gather(hidden, 'col', axis=0, tiled=True)  8.62 us
    dot_general x1, local copies, waits for them, and re-layouts, forward_add_group(): jnp.einsum('sij,sjf->sif', block_part, picked, preferred_element_type=jnp...  5.51 us
    dot_general x1, local copies, waits for them, and re-layouts, backward_add_group(): jnp.einsum('sji,sjf->sif', block_part, picked, preferred_element_type=jnp...  5.51 us
  transfers between devices with their start and end apart: 10, of which 7 were waited for; matrix products, arithmetic and copies ran while one was open for 2% of the time, Pallas kernels for 0%

commit v1 on v0

v1 whole, which is shorter than its diff:
```python
import functools
import math

import jax
import jax.numpy as jnp
from jax import lax
from jax.experimental import pallas as pl
from jax.experimental.pallas import tpu as pltpu
from jax.sharding import PartitionSpec as P

BLK = 128
HALF = 2
VB = 2
SPAN = 2 * HALF + 1
SLICE = 8
SLOT_GROUP = 8
VMEM = pltpu.VMEM
SMEM = pltpu.SMEM


def shifted(block, axis, distance):
    size = lax.axis_size(axis)
    return lax.ppermute(block, axis, [(i, (i + distance) % size) for i in range(size)])


def swapped(block, axis, bit):
    size = lax.axis_size(axis)
    return lax.ppermute(block, axis, [(i, i ^ bit) for i in range(size)])


def spec(space):
    return pl.BlockSpec(memory_space=space)


def call(body, outs, scratch, flops, spaces, name):
    return pl.pallas_call(
        body,
        out_shape=outs,
        in_specs=[spec(space) for space in spaces],
        out_specs=[spec(VMEM)] * len(outs),
        scratch_shapes=scratch,
        name=name,
        cost_estimate=pl.CostEstimate(flops=flops, bytes_accessed=2**20, transcendentals=0),
        compiler_params=pltpu.CompilerParams(vmem_limit_bytes=16 * 2**20),
    )


def for_slots(slot_total, live, step):
    for start in range(0, slot_total, SLOT_GROUP):

        @pl.when(start < live)
        def _group():
            for slot in range(start, min(start + SLOT_GROUP, slot_total)):
                step(slot)


def forward_kernel(
    count, target, source, values, own, near, across, far,
    mine, down2, down1, up1, up2, table, totals,
):
    column = lax.axis_index("col")
    live = count[0, 0]
    for relative, part in enumerate((own, near, across, far)):
        for block in range(VB):
            table[relative * VB + block] = part[block * BLK : (block + 1) * BLK, :]
    totals[...] = jnp.zeros_like(totals)

    def step(slot):
        block = source[0, 0, slot]
        place = ((block // VB) ^ column) * VB + lax.rem(block, VB)
        goal = jnp.where(slot < live, target[0, 0, slot], SPAN * VB)
        totals[goal] += jnp.dot(
            values[0, 0, slot], table[place], preferred_element_type=jnp.float32
        )

    for_slots(values.shape[2], live, step)
    for offset, out in enumerate((down2, down1, mine, up1, up2)):
        for block in range(VB):
            out[block * BLK : (block + 1) * BLK, :] = totals[offset * VB + block].astype(out.dtype)


def middle_kernel(
    mine, from_up2, from_up1, from_down1, from_down2, weight, bias, cotangent,
    output, grad_out, message,
):
    total = mine[...]
    for part in (from_up2, from_up1, from_down1, from_down2):
        total = total + part[...].astype(jnp.float32)
    high = total.astype(jnp.bfloat16)
    low = (total - high.astype(jnp.float32)).astype(jnp.bfloat16)
    kernel = weight[...]
    pre = jnp.dot(high, kernel, preferred_element_type=jnp.float32)
    pre = pre + jnp.dot(low, kernel, preferred_element_type=jnp.float32) + bias[...]
    gate = 1.0 / (1.0 + jnp.exp(-pre))
    output[...] = (pre * gate).astype(jnp.bfloat16)
    exact = cotangent[...].astype(jnp.float32) * (gate * (1.0 + pre * (1.0 - gate)))
    grad = exact.astype(jnp.bfloat16)
    grad_out[...] = lax.dot_general(
        kernel, grad, (((1,), (1,)), ((), ())), preferred_element_type=jnp.float32
    ).astype(jnp.bfloat16)
    weight_term = lax.dot_general(
        high, grad, (((0,), (0,)), ((), ())), preferred_element_type=jnp.float32
    )
    bias_term = jnp.sum(exact, axis=0, keepdims=True)
    bias_high = bias_term.astype(jnp.bfloat16).astype(jnp.float32)
    lines = lax.broadcasted_iota(jnp.int32, (SLICE, bias_term.shape[1]), 0)
    tail = jnp.where(lines == 0, bias_high, jnp.where(lines == 1, bias_term - bias_high, 0.0))
    for index in range(message.shape[0]):
        rows = weight_term[index * SLICE : (index + 1) * SLICE, :]
        message[index] = jnp.concatenate([rows, tail], axis=0).astype(jnp.bfloat16)


def backward_kernel(
    count, target, source, values, from_down2, from_down1, local, from_up1, from_up2,
    mine, near, across, far, table, totals,
):
    column = lax.axis_index("col")
    live = count[0, 0]
    for offset, part in enumerate((from_down2, from_down1, local, from_up1, from_up2)):
        for block in range(VB):
            table[offset * VB + block] = part[:, block * BLK : (block + 1) * BLK]
    totals[...] = jnp.zeros_like(totals)

    def step(slot):
        goal = jnp.where(slot < live, source[0, 0, slot], totals.shape[0] - 1)
        totals[goal] += jnp.dot(
            table[target[0, 0, slot]], values[0, 0, slot], preferred_element_type=jnp.float32
        )

    for_slots(values.shape[2], live, step)
    for relative, out in enumerate((mine, near, across, far)):
        for block in range(VB):
            out[:, block * BLK : (block + 1) * BLK] = totals[
                (column ^ relative) * VB + block
            ].astype(out.dtype)


def slice_kernel(scale, received, part, bias_out):
    total = jnp.sum(received[...].astype(jnp.float32), axis=0) * scale
    part[...] = jnp.broadcast_to(total[:SLICE].astype(jnp.bfloat16)[None], part.shape)
    bias_out[...] = total[SLICE : SLICE + 1] + total[SLICE + 1 : SLICE + 2]


def last_kernel(mine, near, across, far, grad_inputs):
    total = mine[...]
    for part in (near, across, far):
        total = total + part[...].astype(jnp.float32)
    grad_inputs[...] = total.T.astype(jnp.bfloat16)


def shards(
    features, weight, bias, block_values, block_target, block_source, block_count, cotangent
):
    columns = lax.axis_size("col")
    assert columns == 4
    rows = lax.axis_size("row")
    own_rows, width = features.shape
    slots = block_values.shape[2]
    sources = columns * VB
    bf16, f32 = jnp.bfloat16, jnp.float32

    near = swapped(features, "col", 1)
    across = swapped(features, "col", 2)
    far = swapped(across, "col", 1)
    whole = jax.ShapeDtypeStruct((own_rows, width), bf16)
    wide = jax.ShapeDtypeStruct((own_rows, width), f32)
    mine, down2, down1, up1, up2 = call(
        forward_kernel,
        [wide] + [whole] * 4,
        [
            pltpu.VMEM((sources, BLK, width), bf16),
            pltpu.VMEM((SPAN * VB + 1, BLK, width), f32),
        ],
        2 * slots * BLK * BLK * width,
        [SMEM] * 3 + [VMEM] * 5,
        "aggregate_terms",
    )(block_count, block_target, block_source, block_values, features, near, across, far)

    from_up2 = shifted(down2, "row", -2)
    from_down2 = shifted(up2, "row", 2)
    from_up1 = shifted(down1, "row", -1)
    from_down1 = shifted(up1, "row", 1)
    flipped = jax.ShapeDtypeStruct((width, own_rows), bf16)
    slices = width // SLICE
    output, grad_out, message = call(
        middle_kernel,
        [whole, flipped, jax.ShapeDtypeStruct((slices, 2 * SLICE, width), bf16)],
        [],
        2 * 4 * own_rows * width * width,
        [VMEM] * 8,
        "pointwise_and_weight",
    )(mine, from_up2, from_up1, from_down1, from_down2, weight, bias[None, :], cotangent)

    grad_up2 = shifted(grad_out, "row", -2)
    grad_down2 = shifted(grad_out, "row", 2)
    grad_up1 = shifted(grad_out, "row", -1)
    grad_down1 = shifted(grad_out, "row", 1)
    mine, near, across, far = call(
        backward_kernel,
        [jax.ShapeDtypeStruct((width, own_rows), f32)] + [flipped] * 3,
        [
            pltpu.VMEM((SPAN * VB, width, BLK), bf16),
            pltpu.VMEM((sources + 1, width, BLK), f32),
        ],
        2 * slots * BLK * BLK * width,
        [SMEM] * 3 + [VMEM] * 6,
        "source_terms",
    )(
        block_count, block_target, block_source, block_values,
        grad_down2, grad_down1, grad_out, grad_up1, grad_up2,
    )
    near = swapped(near, "col", 1)
    across = swapped(across, "col", 2)
    far = swapped(far, "col", 3)

    scale = 1.0 / math.sqrt(own_rows * rows * columns)
    everyone = ("row", "col")
    if slices == rows * columns:
        received = lax.all_to_all(message, everyone, 0, 0, tiled=True)
        part, bias_total = call(
            functools.partial(slice_kernel, scale),
            [
                jax.ShapeDtypeStruct((slices, SLICE, width), bf16),
                jax.ShapeDtypeStruct((1, width), f32),
            ],
            [],
            slices * SLICE * width,
            [VMEM],
            "weight_slice",
        )(received)
        weight_total = lax.all_to_all(part, everyone, 0, 0, tiled=True)
        weight_total = weight_total.reshape(width, width).astype(f32)
        bias_total = bias_total[0]
    else:
        summed = lax.psum(message.astype(f32), everyone) * scale
        weight_total = summed[:, :SLICE].reshape(width, width)
        bias_total = summed[0, SLICE] + summed[0, SLICE + 1]

    grad_inputs = call(
        last_kernel, [whole], [], own_rows * width * 4, [VMEM] * 4, "source_sum"
    )(mine, near, across, far)[0]
    return (output, grad_inputs, weight_total, bias_total)


def solution(mesh):
    return jax.shard_map(
        shards,
        mesh=mesh,
        in_specs=(
            P(("row", "col"), None),
            P(),
            P(),
            P("row", "col", None, None, None),
            P("row", "col", None),
            P("row", "col", None),
            P("row", "col"),
            P(("row", "col"), None),
        ),
        out_specs=(P(("row", "col"), None), P(("row", "col"), None), P(), P()),
        check_vma=False,
    )
```

time: 267 us -> 63.3 us (0.24)
  waiting for transfers between devices: 141 us -> 22.3 us
  blocking collectives: 47.3 us -> 0 us
  matrix products: 21.3 us -> 0 us
  local copies, waits for them, and re-layouts: 21.8 us -> 2.81 us
  starting transfers between devices: 15.8 us -> 29.8 us
  between operations: 14.8 us -> 1.4 us
  Pallas kernels: 0 us -> 6.18 us
  other arithmetic: 3.98 us -> 0.72 us
    psum x1 -> x0, waiting for transfers between devices: 124 us -> none  [shards(): lax.psum((weight_term, bias_term), ('row', 'col'))]
    psum x1 -> x0, blocking collectives: 38.7 us -> none  [shards(): lax.psum((weight_term, bias_term), ('row', 'col'))]
    dot_general x7 -> x0, matrix products: 21.3 us -> none  [the longest x1 4.65 us: forward_add_group(): jnp.einsum('sij,sjf->sif', block_part, picked, preferred_element_type=jnp...]
    dot_general x2 -> x0, local copies, waits for them, and re-layouts: 11 us -> none  [the longest x1 5.51 us: forward_add_group(): jnp.einsum('sij,sjf->sif', block_part, picked, preferred_element_type=jnp...]
    all_to_all x0 -> x2, starting transfers between devices: none -> 9.82 us  [the longest x1 5.45 us: shards(): weight_total = lax.all_to_all(part, everyone, 0, 0, tiled=True)]
    all_gather x1 -> x0, blocking collectives: 8.62 us -> none  [shards(): lax.all_gather(hidden, 'col', axis=0, tiled=True)]
    pallas_call x0 -> x5, Pallas kernels: none -> 6.18 us  [the longest x1 1.68 us: shards(): call(backward_kernel, [jax.ShapeDtypeStruct((width, own_rows), f32)] + [f...]
    ppermute x8 -> x14, starting transfers between devices: 15.8 us -> 20 us  [the longest x8 15 us: shifted(): lax.ppermute(block, axis, [(i, (i + distance) % size) for i in range(size)])]
  transfers between devices with their start and end apart: 10 -> 16, of which waited for: 7 -> 9; matrix products, arithmetic and copies ran while one was open for 2% -> 0% of each run, Pallas kernels for 0% -> 5%
where the time goes in v1:
time: 63.3 us; the launch traced here: 63.1 us
  starting transfers between devices  29.8 us (47%)
  waiting for transfers between devices  22.3 us (35%)
  Pallas kernels  6.18 us (10%)
  local copies, waits for them, and re-layouts  2.81 us (4%)
  between operations  1.4 us (2%)
  other arithmetic  0.72 us (1%)
    ppermute x8, starting transfers between devices, shifted(): lax.ppermute(block, axis, [(i, (i + distance) % size) for i in range(size)])  15 us
    ppermute x6, waiting for transfers between devices, swapped(): return lax.ppermute(block, axis, [(i, i ^ bit) for i in range(size)])  11 us
    ppermute x8, waiting for transfers between devices, shifted(): lax.ppermute(block, axis, [(i, (i + distance) % size) for i in range(size)])  9.18 us
    all_to_all x1, starting transfers between devices, shards(): weight_total = lax.all_to_all(part, everyone, 0, 0, tiled=True)  5.45 us
    ppermute x6, starting transfers between devices, swapped(): return lax.ppermute(block, axis, [(i, i ^ bit) for i in range(size)])  4.94 us
    all_to_all x1, starting transfers between devices, shards(): received = lax.all_to_all(message, everyone, 0, 0, tiled=True)  4.37 us
    unnamed x16, local copies, waits for them, and re-layouts  2.81 us
    all_to_all x1, waiting for transfers between devices, shards(): received = lax.all_to_all(message, everyone, 0, 0, tiled=True)  2.1 us
  transfers between devices with their start and end apart: 16, of which 9 were waited for; matrix products, arithmetic and copies ran while one was open for 0% of the time, Pallas kernels for 5%

profile of v1, /device:TPU:0, one launch (start us, length us, event | category | flops | bytes accessed | tf_op | source)
XLA Modules:
  0.0 63.1 jit_solution(7480823542149807145)
XLA Ops:
  0.7 3.0 %collective-permute-start.1 = (bf16[256,256]{1,0:T(8,128)(2,1)}, bf16[256,256]{1,0:T(8,128)(2,1)S(1)}, u32[]{:S(2)}, u32[]{:S(2)}) collective-permute-start(bf16[256,256]{1,0:T(8,128)(2,1)} %own.1), channel_id=1, source_target_pairs={{0,2},{1,3},{2,0},{3,1},{4,6},{5,7},{6,4},{7,5},{8,10},{9,11},{10,... | collective-permute-start | bytes 393224 | tf_op jit(solution)/shard_map/ppermute | solution.py:28
  3.7 0.0 collective-permute-start
  3.7 3.7 %collective-permute-done.1.across = bf16[256,256]{1,0:T(8,128)(2,1)S(1)} collective-permute-done((bf16[256,256]{1,0:T(8,128)(2,1)}, bf16[256,256]{1,0:T(8,128)(2,1)S(1)}, u32[]{:S(2)}, u32[]{:S(2)}) %collective-permute-start.1) | collective-permute-done | bytes 131104 | tf_op jit(solution)/shard_map/ppermute | solution.py:28
  8.0 0.7 %collective-permute-done.2.far = bf16[256,256]{1,0:T(8,128)(2,1)S(1)} collective-permute-done((bf16[256,256]{1,0:T(8,128)(2,1)S(1)}, bf16[256,256]{1,0:T(8,128)(2,1)S(1)}, u32[]{:S(2)}, u32[]{:S(2)}) %collective-permute-start.2) | collective-permute-done | bytes 131104 | tf_op jit(solution)/shard_map/ppermute | solution.py:28
  8.7 1.2 %copy-done = bf16[1,1,32,128,128]{4,3,2,1,0:T(8,128)(2,1)S(1)} copy-done((bf16[1,1,32,128,128]{4,3,2,1,0:T(8,128)(2,1)S(1)}, bf16[1,1,32,128,128]{4,3,2,1,0:T(8,128)(2,1)}, u32[]{:S(2)}) %copy-start) | copy-done | bytes 1048600
  9.9 0.9 %copy-done.2 = bf16[256,256]{1,0:T(8,128)(2,1)S(1)} copy-done((bf16[256,256]{1,0:T(8,128)(2,1)S(1)}, bf16[256,256]{1,0:T(8,128)(2,1)}, u32[]{:S(2)}) %copy-start.2) | copy-done | bytes 131096
  10.9 1.7 %aggregate_terms.1 = (f32[256,256]{1,0:T(8,128)S(1)}, bf16[256,256]{1,0:T(8,128)(2,1)S(1)}, bf16[256,256]{1,0:T(8,128)(2,1)S(1)}, bf16[256,256]{1,0:T(8,128)(2,1)S(1)}, bf16[256,256]{1,0:T(8,128)(2,1)S(1)}) custom-call(s32[1,1]{1,0:T(1,128)S(6)} %copy.12.count, s32[1,1,32]{2,1,0:T(1,128)S(1)} %copy-done.5, s32[1,1,32]{2,1,0:T(1,128)S(1)} %copy-done.6, ...), custom_call_target="tpu_custom_call" | custom-call | flops 268435456 | bytes 1048576 | tf_op jit(solution)/shard_map/aggregate_terms/pallas_call | solution.py:167
  12.5 3.6 %collective-permute-start.3 = (bf16[256,256]{1,0:T(8,128)(2,1)S(1)}, bf16[256,256]{1,0:T(8,128)(2,1)S(1)}, u32[]{:S(2)}, u32[]{:S(2)}) collective-permute-start(bf16[256,256]{1,0:T(8,128)(2,1)S(1)} %get-tuple-element.19), channel_id=1, source_target_pairs={{0,24},{4,28},{8,0},{12,4},{16,8},{20,12},{24,16},{28,20},{1,25},{... | collective-permute-start | bytes 393224 | tf_op jit(solution)/shard_map/ppermute | solution.py:23
  16.1 1.4 %collective-permute-start.4 = (bf16[256,256]{1,0:T(8,128)(2,1)S(1)}, bf16[256,256]{1,0:T(8,128)(2,1)S(1)}, u32[]{:S(2)}, u32[]{:S(2)}) collective-permute-start(bf16[256,256]{1,0:T(8,128)(2,1)S(1)} %get-tuple-element.20), channel_id=1, source_target_pairs={{0,28},{4,0},{8,4},{12,8},{16,12},{20,16},{24,20},{28,24},{1,29},{... | collective-permute-start | bytes 393224 | tf_op jit(solution)/shard_map/ppermute | solution.py:23
  17.5 0.6 collective-permute-start.5
  18.2 1.0 %collective-permute-start.6 = (bf16[256,256]{1,0:T(8,128)(2,1)S(1)}, bf16[256,256]{1,0:T(8,128)(2,1)S(1)}, u32[]{:S(2)}, u32[]{:S(2)}) collective-permute-start(bf16[256,256]{1,0:T(8,128)(2,1)S(1)} %get-tuple-element.22), channel_id=1, source_target_pairs={{0,8},{4,12},{8,16},{12,20},{16,24},{20,28},{24,0},{28,4},{1,9},{5... | collective-permute-start | bytes 393224 | tf_op jit(solution)/shard_map/ppermute | solution.py:23
  19.1 1.0 %collective-permute-done.3.from_up2 = bf16[256,256]{1,0:T(8,128)(2,1)S(1)} collective-permute-done((bf16[256,256]{1,0:T(8,128)(2,1)S(1)}, bf16[256,256]{1,0:T(8,128)(2,1)S(1)}, u32[]{:S(2)}, u32[]{:S(2)}) %collective-permute-start.3) | collective-permute-done | bytes 131104 | tf_op jit(solution)/shard_map/ppermute | solution.py:23
  20.1 2.8 %collective-permute-done.4.from_up1 = bf16[256,256]{1,0:T(8,128)(2,1)S(1)} collective-permute-done((bf16[256,256]{1,0:T(8,128)(2,1)S(1)}, bf16[256,256]{1,0:T(8,128)(2,1)S(1)}, u32[]{:S(2)}, u32[]{:S(2)}) %collective-permute-start.4) | collective-permute-done | bytes 131104 | tf_op jit(solution)/shard_map/ppermute | solution.py:23
  22.9 3.7 %collective-permute-done.5.from_down1 = bf16[256,256]{1,0:T(8,128)(2,1)S(1)} collective-permute-done((bf16[256,256]{1,0:T(8,128)(2,1)S(1)}, bf16[256,256]{1,0:T(8,128)(2,1)S(1)}, u32[]{:S(2)}, u32[]{:S(2)}) %collective-permute-start.5) | collective-permute-done | bytes 131104 | tf_op jit(solution)/shard_map/ppermute | solution.py:23
  26.6 0.7 %copy-done.7 = f32[256]{0:T(256)S(1)} copy-done((f32[256]{0:T(256)S(1)}, f32[256]{0:T(256)}, u32[]{:S(2)}) %copy-start.7) | copy-done | bytes 1048
  27.3 1.3 %pointwise_and_weight.1 = (bf16[256,256]{1,0:T(8,128)(2,1)}, bf16[256,256]{1,0:T(8,128)(2,1)S(1)}, bf16[32,16,256]{2,1,0:T(8,128)(2,1)}) custom-call(f32[256,256]{1,0:T(8,128)S(1)} %get-tuple-element.18.mine, bf16[256,256]{1,0:T(8,128)(2,1)S(1)} %collective-permute-done.3.from_up2, bf16[256,256]{1,0:T(8,128)(2,1)S(1)} %collective-permute-done.4.from_up1, ...), custom_call_target="tpu_custom_call" | custom-call | flops 134217728 | bytes 1048576 | tf_op jit(solution)/shard_map/pointwise_and_weight/pallas_call | solution.py:185
  28.6 4.4 %all-to-all-start = ((bf16[32,16,256]{2,1,0:T(8,128)(2,1)}), bf16[32,16,256]{2,1,0:T(8,128)(2,1)S(1)}, u32[]{:S(2)}, u32[]{:S(2)}) async-start(bf16[32,16,256]{2,1,0:T(8,128)(2,1)} %get-tuple-element.29), calls=%async_computation | async-start | bytes 524288 | tf_op jit(solution)/shard_map/all_to_all | solution.py:219
  33.0 3.7 %collective-permute-start.10 = (bf16[256,256]{1,0:T(8,128)(2,1)S(1)}, bf16[256,256]{1,0:T(8,128)(2,1)S(1)}, u32[]{:S(2)}, u32[]{:S(2)}) collective-permute-start(bf16[256,256]{1,0:T(8,128)(2,1)S(1)} %get-tuple-element.24.local), channel_id=1, source_target_pairs={{0,24},{4,28},{8,0},{12,4},{16,8},{20,12},{24,16},{28,20},{1,25},{... | collective-permute-start | bytes 393224 | tf_op jit(solution)/shard_map/ppermute | solution.py:23
  36.7 1.5 %collective-permute-start.8 = (bf16[256,256]{1,0:T(8,128)(2,1)S(1)}, bf16[256,256]{1,0:T(8,128)(2,1)S(1)}, u32[]{:S(2)}, u32[]{:S(2)}) collective-permute-start(bf16[256,256]{1,0:T(8,128)(2,1)S(1)} %get-tuple-element.24.local), channel_id=1, source_target_pairs={{0,4},{4,8},{8,12},{12,16},{16,20},{20,24},{24,28},{28,0},{1,5},{5... | collective-permute-start | bytes 393224 | tf_op jit(solution)/shard_map/ppermute | solution.py:23
  38.2 3.3 %collective-permute-start.9 = (bf16[256,256]{1,0:T(8,128)(2,1)S(1)}, bf16[256,256]{1,0:T(8,128)(2,1)S(1)}, u32[]{:S(2)}, u32[]{:S(2)}) collective-permute-start(bf16[256,256]{1,0:T(8,128)(2,1)S(1)} %get-tuple-element.24.local), channel_id=1, source_target_pairs={{0,28},{4,0},{8,4},{12,8},{16,12},{20,16},{24,20},{28,24},{1,29},{... | collective-permute-start | bytes 393224 | tf_op jit(solution)/shard_map/ppermute | solution.py:23
  41.4 2.1 %all-to-all-done.received = bf16[32,16,256]{2,1,0:T(8,128)(2,1)S(1)} async-done(((bf16[32,16,256]{2,1,0:T(8,128)(2,1)}), bf16[32,16,256]{2,1,0:T(8,128)(2,1)S(1)}, u32[]{:S(2)}, u32[]{:S(2)}) %all-to-all-start) | async-done | bytes 262176 | tf_op jit(solution)/shard_map/all_to_all | solution.py:219
  43.5 0.7 %weight_slice.1 = (bf16[32,8,256]{2,1,0:T(8,128)(2,1)}, f32[1,256]{1,0:T(1,128)}) custom-call(bf16[32,16,256]{2,1,0:T(8,128)(2,1)S(1)} %all-to-all-done.received), custom_call_target="tpu_custom_call" | custom-call | flops 65536 | bytes 1048576 | tf_op jit(solution)/shard_map/weight_slice/pallas_call | solution.py:220
  44.2 5.4 %all-to-all-start.1 = ((bf16[32,8,256]{2,1,0:T(8,128)(2,1)}), bf16[32,8,256]{2,1,0:T(8,128)(2,1)S(1)}, u32[]{:S(2)}, u32[]{:S(2)}) async-start(bf16[32,8,256]{2,1,0:T(8,128)(2,1)} %get-tuple-element.30), calls=%async_computation.1 | async-start | bytes 262144 | tf_op jit(solution)/shard_map/all_to_all | solution.py:231
  49.7 1.7 %collective-permute-done.8.from_down1 = bf16[256,256]{1,0:T(8,128)(2,1)S(1)} collective-permute-done((bf16[256,256]{1,0:T(8,128)(2,1)S(1)}, bf16[256,256]{1,0:T(8,128)(2,1)S(1)}, u32[]{:S(2)}, u32[]{:S(2)}) %collective-permute-start.8) | collective-permute-done | bytes 131104 | tf_op jit(solution)/shard_map/ppermute | solution.py:23
  51.4 1.7 %source_terms.1 = (f32[256,256]{1,0:T(8,128)S(1)}, bf16[256,256]{1,0:T(8,128)(2,1)S(1)}, bf16[256,256]{1,0:T(8,128)(2,1)S(1)}, bf16[256,256]{1,0:T(8,128)(2,1)S(1)}) custom-call(s32[1,1]{1,0:T(1,128)S(6)} %copy.12.count, s32[1,1,32]{2,1,0:T(1,128)S(1)} %copy-done.5, s32[1,1,32]{2,1,0:T(1,128)S(1)} %copy-done.6, bf16[1,1,32,128,128]{4,3,2,1,0:T(8,128)(2,1)S(1)} %copy-done.1, ...), custom_call_target="tpu_custom_call" | custom-call | flops 268435456 | bytes 1048576 | tf_op jit(solution)/shard_map/source_terms/pallas_call | solution.py:198
  53.1 0.1 collective-permute-start.11
  53.2 1.5 %collective-permute-start.12 = (bf16[256,256]{1,0:T(8,128)(2,1)S(1)}, bf16[256,256]{1,0:T(8,128)(2,1)S(1)}, u32[]{:S(2)}, u32[]{:S(2)}) collective-permute-start(bf16[256,256]{1,0:T(8,128)(2,1)S(1)} %get-tuple-element.27), channel_id=1, source_target_pairs={{0,2},{1,3},{2,0},{3,1},{4,6},{5,7},{6,4},{7,5},{8,10},{9,11},{10,... | collective-permute-start | bytes 393224 | tf_op jit(solution)/shard_map/ppermute | solution.py:28
  54.7 0.3 collective-permute-start.13
  55.0 4.6 %collective-permute-done.12.across = bf16[256,256]{1,0:T(8,128)(2,1)S(1)} collective-permute-done((bf16[256,256]{1,0:T(8,128)(2,1)S(1)}, bf16[256,256]{1,0:T(8,128)(2,1)S(1)}, u32[]{:S(2)}, u32[]{:S(2)}) %collective-permute-start.12) | collective-permute-done | bytes 131104 | tf_op jit(solution)/shard_map/ppermute | solution.py:28
  59.6 2.0 %collective-permute-done.13.far = bf16[256,256]{1,0:T(8,128)(2,1)S(1)} collective-permute-done((bf16[256,256]{1,0:T(8,128)(2,1)S(1)}, bf16[256,256]{1,0:T(8,128)(2,1)S(1)}, u32[]{:S(2)}, u32[]{:S(2)}) %collective-permute-start.13) | collective-permute-done | bytes 131104 | tf_op jit(solution)/shard_map/ppermute | solution.py:28
  61.6 0.8 %source_sum.1 = bf16[256,256]{1,0:T(8,128)(2,1)} custom-call(f32[256,256]{1,0:T(8,128)S(1)} %get-tuple-element.25.mine, bf16[256,256]{1,0:T(8,128)(2,1)S(1)} %collective-permute-done.11.near, bf16[256,256]{1,0:T(8,128)(2,1)S(1)} %collective-permute-done.12.across, bf16[256,256]{1,0:T(8,128)(2,1)S(1)} %collective-permute-done.13.far), custom_call_target="tpu_custom_call" | custom-call | flops 262144 | bytes 1048576 | tf_op jit(solution)/shard_map/source_sum/pallas_call | solution.py:239
  62.4 0.7 %bitcast_convert_fusion = f32[256,256]{1,0:T(8,128)} fusion(bf16[32,8,256]{2,1,0:T(8,128)(2,1)S(1)} %all-to-all-done.1), kind=kLoop, calls=%fused_computation | loop fusion | flops 65536 | bytes 393216 | tf_op jit(solution)/shard_map/convert_element_type | solution.py:232
  (22 shorter events, 0.0 us)
Async XLA Ops:
  0.6 8.1 %copy-start.5 = (s32[1,1,32]{2,1,0:T(1,128)S(1)}, s32[1,1,32]{2,1,0:T(1,128)}, u32[]{:S(2)}) copy-start(s32[1,1,32]{2,1,0:T(1,128)} %target.3) | copy-start | bytes 388
  0.6 8.1 %copy-start.6 = (s32[1,1,32]{2,1,0:T(1,128)S(1)}, s32[1,1,32]{2,1,0:T(1,128)}, u32[]{:S(2)}) copy-start(s32[1,1,32]{2,1,0:T(1,128)} %source.3) | copy-start | bytes 388
  0.7 6.7 %collective-permute-start.1 = (bf16[256,256]{1,0:T(8,128)(2,1)}, bf16[256,256]{1,0:T(8,128)(2,1)S(1)}, u32[]{:S(2)}, u32[]{:S(2)}) collective-permute-start(bf16[256,256]{1,0:T(8,128)(2,1)} %own.1), channel_id=1, source_target_pairs={{0,2},{1,3},{2,0},{3,1},{4,6},{5,7},{6,4},{7,5},{8,10},{9,11},{10,... | collective-permute-start | bytes 393224 | tf_op jit(solution)/shard_map/ppermute | solution.py:28
  3.7 4.4 %collective-permute-start = (bf16[256,256]{1,0:T(8,128)(2,1)}, bf16[256,256]{1,0:T(8,128)(2,1)S(1)}, u32[]{:S(2)}, u32[]{:S(2)}) collective-permute-start(bf16[256,256]{1,0:T(8,128)(2,1)} %own.1), channel_id=1, source_target_pairs={{0,1},{1,0},{2,3},{3,2},{4,5},{5,4},{6,7},{7,6},{8,9},{9,8},{10,11... | collective-permute-start | bytes 393224 | tf_op jit(solution)/shard_map/ppermute | solution.py:28
  7.4 1.3 %collective-permute-start.2 = (bf16[256,256]{1,0:T(8,128)(2,1)S(1)}, bf16[256,256]{1,0:T(8,128)(2,1)S(1)}, u32[]{:S(2)}, u32[]{:S(2)}) collective-permute-start(bf16[256,256]{1,0:T(8,128)(2,1)S(1)} %collective-permute-done.1.across), channel_id=1, source_target_pairs={{0,1},{1,0},{2,3},{3,2},{4,5},{5,4},{6,7},{7,6},{8,9},{9,8},{10,11... | collective-permute-start | bytes 393224 | tf_op jit(solution)/shard_map/ppermute | solution.py:28
  8.7 1.2 %copy-start = (bf16[1,1,32,128,128]{4,3,2,1,0:T(8,128)(2,1)S(1)}, bf16[1,1,32,128,128]{4,3,2,1,0:T(8,128)(2,1)}, u32[]{:S(2)}) copy-start(bf16[1,1,32,128,128]{4,3,2,1,0:T(8,128)(2,1)} %values.3) | copy-start | bytes 3145732
  9.9 0.9 %copy-start.2 = (bf16[256,256]{1,0:T(8,128)(2,1)S(1)}, bf16[256,256]{1,0:T(8,128)(2,1)}, u32[]{:S(2)}) copy-start(bf16[256,256]{1,0:T(8,128)(2,1)} %own.1) | copy-start | bytes 393220
  10.8 15.8 %copy-start.3 = (bf16[256,256]{1,0:T(8,128)(2,1)S(1)}, bf16[256,256]{1,0:T(8,128)(2,1)}, u32[]{:S(2)}) copy-start(bf16[256,256]{1,0:T(8,128)(2,1)} %weight.1) | copy-start | bytes 393220
  10.9 15.8 %copy-start.4 = (bf16[256,256]{1,0:T(8,128)(2,1)S(1)}, bf16[256,256]{1,0:T(8,128)(2,1)}, u32[]{:S(2)}) copy-start(bf16[256,256]{1,0:T(8,128)(2,1)} %cotangent.1) | copy-start | bytes 393220
  12.5 7.5 %collective-permute-start.3 = (bf16[256,256]{1,0:T(8,128)(2,1)S(1)}, bf16[256,256]{1,0:T(8,128)(2,1)S(1)}, u32[]{:S(2)}, u32[]{:S(2)}) collective-permute-start(bf16[256,256]{1,0:T(8,128)(2,1)S(1)} %get-tuple-element.19), channel_id=1, source_target_pairs={{0,24},{4,28},{8,0},{12,4},{16,8},{20,12},{24,16},{28,20},{1,25},{... | collective-permute-start | bytes 393224 | tf_op jit(solution)/shard_map/ppermute | solution.py:23
  16.1 6.8 %collective-permute-start.4 = (bf16[256,256]{1,0:T(8,128)(2,1)S(1)}, bf16[256,256]{1,0:T(8,128)(2,1)S(1)}, u32[]{:S(2)}, u32[]{:S(2)}) collective-permute-start(bf16[256,256]{1,0:T(8,128)(2,1)S(1)} %get-tuple-element.20), channel_id=1, source_target_pairs={{0,28},{4,0},{8,4},{12,8},{16,12},{20,16},{24,20},{28,24},{1,29},{... | collective-permute-start | bytes 393224 | tf_op jit(solution)/shard_map/ppermute | solution.py:23
  17.5 9.1 %collective-permute-start.5 = (bf16[256,256]{1,0:T(8,128)(2,1)S(1)}, bf16[256,256]{1,0:T(8,128)(2,1)S(1)}, u32[]{:S(2)}, u32[]{:S(2)}) collective-permute-start(bf16[256,256]{1,0:T(8,128)(2,1)S(1)} %get-tuple-element.21), channel_id=1, source_target_pairs={{0,4},{4,8},{8,12},{12,16},{16,20},{20,24},{24,28},{28,0},{1,5},{5... | collective-permute-start | bytes 393224 | tf_op jit(solution)/shard_map/ppermute | solution.py:23
  18.2 8.5 %collective-permute-start.6 = (bf16[256,256]{1,0:T(8,128)(2,1)S(1)}, bf16[256,256]{1,0:T(8,128)(2,1)S(1)}, u32[]{:S(2)}, u32[]{:S(2)}) collective-permute-start(bf16[256,256]{1,0:T(8,128)(2,1)S(1)} %get-tuple-element.22), channel_id=1, source_target_pairs={{0,8},{4,12},{8,16},{12,20},{16,24},{20,28},{24,0},{28,4},{1,9},{5... | collective-permute-start | bytes 393224 | tf_op jit(solution)/shard_map/ppermute | solution.py:23
  26.6 0.7 %copy-start.7 = (f32[256]{0:T(256)S(1)}, f32[256]{0:T(256)}, u32[]{:S(2)}) copy-start(f32[256]{0:T(256)} %param.10) | copy-start | bytes 3076
  27.3 24.1 %copy-start.1 = (bf16[1,1,32,128,128]{4,3,2,1,0:T(8,128)(2,1)S(1)}, bf16[1,1,32,128,128]{4,3,2,1,0:T(8,128)(2,1)}, u32[]{:S(2)}) copy-start(bf16[1,1,32,128,128]{4,3,2,1,0:T(8,128)(2,1)} %values.3) | copy-start | bytes 3145732
  28.6 14.9 %all-to-all-start = ((bf16[32,16,256]{2,1,0:T(8,128)(2,1)}), bf16[32,16,256]{2,1,0:T(8,128)(2,1)S(1)}, u32[]{:S(2)}, u32[]{:S(2)}) async-start(bf16[32,16,256]{2,1,0:T(8,128)(2,1)} %get-tuple-element.29), calls=%async_computation | async-start | bytes 524288 | tf_op jit(solution)/shard_map/all_to_all | solution.py:219
  33.0 16.7 %collective-permute-start.10 = (bf16[256,256]{1,0:T(8,128)(2,1)S(1)}, bf16[256,256]{1,0:T(8,128)(2,1)S(1)}, u32[]{:S(2)}, u32[]{:S(2)}) collective-permute-start(bf16[256,256]{1,0:T(8,128)(2,1)S(1)} %get-tuple-element.24.local), channel_id=1, source_target_pairs={{0,24},{4,28},{8,0},{12,4},{16,8},{20,12},{24,16},{28,20},{1,25},{... | collective-permute-start | bytes 393224 | tf_op jit(solution)/shard_map/ppermute | solution.py:23
  36.7 13.0 %collective-permute-start.7 = (bf16[256,256]{1,0:T(8,128)(2,1)S(1)}, bf16[256,256]{1,0:T(8,128)(2,1)S(1)}, u32[]{:S(2)}, u32[]{:S(2)}) collective-permute-start(bf16[256,256]{1,0:T(8,128)(2,1)S(1)} %get-tuple-element.24.local), channel_id=1, source_target_pairs={{0,8},{4,12},{8,16},{12,20},{16,24},{20,28},{24,0},{28,4},{1,9},{5... | collective-permute-start | bytes 393224 | tf_op jit(solution)/shard_map/ppermute | solution.py:23
  36.7 14.7 %collective-permute-start.8 = (bf16[256,256]{1,0:T(8,128)(2,1)S(1)}, bf16[256,256]{1,0:T(8,128)(2,1)S(1)}, u32[]{:S(2)}, u32[]{:S(2)}) collective-permute-start(bf16[256,256]{1,0:T(8,128)(2,1)S(1)} %get-tuple-element.24.local), channel_id=1, source_target_pairs={{0,4},{4,8},{8,12},{12,16},{16,20},{20,24},{24,28},{28,0},{1,5},{5... | collective-permute-start | bytes 393224 | tf_op jit(solution)/shard_map/ppermute | solution.py:23
  38.2 13.2 %collective-permute-start.9 = (bf16[256,256]{1,0:T(8,128)(2,1)S(1)}, bf16[256,256]{1,0:T(8,128)(2,1)S(1)}, u32[]{:S(2)}, u32[]{:S(2)}) collective-permute-start(bf16[256,256]{1,0:T(8,128)(2,1)S(1)} %get-tuple-element.24.local), channel_id=1, source_target_pairs={{0,28},{4,0},{8,4},{12,8},{16,12},{20,16},{24,20},{28,24},{1,29},{... | collective-permute-start | bytes 393224 | tf_op jit(solution)/shard_map/ppermute | solution.py:23
  44.2 18.2 %all-to-all-start.1 = ((bf16[32,8,256]{2,1,0:T(8,128)(2,1)}), bf16[32,8,256]{2,1,0:T(8,128)(2,1)S(1)}, u32[]{:S(2)}, u32[]{:S(2)}) async-start(bf16[32,8,256]{2,1,0:T(8,128)(2,1)} %get-tuple-element.30), calls=%async_computation.1 | async-start | bytes 262144 | tf_op jit(solution)/shard_map/all_to_all | solution.py:231
  53.1 1.9 %collective-permute-start.11 = (bf16[256,256]{1,0:T(8,128)(2,1)S(1)}, bf16[256,256]{1,0:T(8,128)(2,1)S(1)}, u32[]{:S(2)}, u32[]{:S(2)}) collective-permute-start(bf16[256,256]{1,0:T(8,128)(2,1)S(1)} %get-tuple-element.26), channel_id=1, source_target_pairs={{0,1},{1,0},{2,3},{3,2},{4,5},{5,4},{6,7},{7,6},{8,9},{9,8},{10,11... | collective-permute-start | bytes 393224 | tf_op jit(solution)/shard_map/ppermute | solution.py:28
  53.2 6.5 %collective-permute-start.12 = (bf16[256,256]{1,0:T(8,128)(2,1)S(1)}, bf16[256,256]{1,0:T(8,128)(2,1)S(1)}, u32[]{:S(2)}, u32[]{:S(2)}) collective-permute-start(bf16[256,256]{1,0:T(8,128)(2,1)S(1)} %get-tuple-element.27), channel_id=1, source_target_pairs={{0,2},{1,3},{2,0},{3,1},{4,6},{5,7},{6,4},{7,5},{8,10},{9,11},{10,... | collective-permute-start | bytes 393224 | tf_op jit(solution)/shard_map/ppermute | solution.py:28
  54.7 6.9 %collective-permute-start.13 = (bf16[256,256]{1,0:T(8,128)(2,1)S(1)}, bf16[256,256]{1,0:T(8,128)(2,1)S(1)}, u32[]{:S(2)}, u32[]{:S(2)}) collective-permute-start(bf16[256,256]{1,0:T(8,128)(2,1)S(1)} %get-tuple-element.28), channel_id=1, source_target_pairs={{0,3},{1,2},{2,1},{3,0},{4,7},{5,6},{6,5},{7,4},{8,11},{9,10},{10,... | collective-permute-start | bytes 393224 | tf_op jit(solution)/shard_map/ppermute | solution.py:28

commit v2 on v1

--- a/solution.py
+++ b/solution.py
@@ -13,7 +13,9 @@
 VB = 2
 SPAN = 2 * HALF + 1
 SLICE = 8
+LANES = 128
 SLOT_GROUP = 8
+LONG = 10**11
 VMEM = pltpu.VMEM
 SMEM = pltpu.SMEM
 
@@ -54,15 +56,34 @@
                 step(slot)
 
 
+def stage_kernel(values, own, bias, values_out, own_out, bias_out, values_sem, own_sem, bias_sem):
+    copies = (
+        pltpu.make_async_copy(values, values_out, values_sem),
+        pltpu.make_async_copy(own, own_out, own_sem),
+        pltpu.make_async_copy(bias, bias_out, bias_sem),
+    )
+    for copy in copies:
+        copy.start()
+    for copy in copies:
+        copy.wait()
+
+
+def table_kernel(own, near, across, head):
+    for relative, part in enumerate((own, near, across)):
+        for block in range(VB):
+            head[relative * VB + block] = part[block * BLK : (block + 1) * BLK, :]
+
+
 def forward_kernel(
-    count, target, source, values, own, near, across, far,
+    count, target, source, values, head, far,
     mine, down2, down1, up1, up2, table, totals,
 ):
     column = lax.axis_index("col")
     live = count[0, 0]
-    for relative, part in enumerate((own, near, across, far)):
-        for block in range(VB):
-            table[relative * VB + block] = part[block * BLK : (block + 1) * BLK, :]
+    known = head.shape[0]
+    table[:known] = head[...]
+    for block in range(VB):
+        table[known + block] = far[block * BLK : (block + 1) * BLK, :]
     totals[...] = jnp.zeros_like(totals)
 
     def step(slot):
@@ -81,7 +102,7 @@
 
 def middle_kernel(
     mine, from_up2, from_up1, from_down1, from_down2, weight, bias, cotangent,
-    output, grad_out, message,
+    output, grad_out, summed, grad, bias_part,
 ):
     total = mine[...]
     for part in (from_up2, from_up1, from_down1, from_down2):
@@ -94,20 +115,33 @@
     gate = 1.0 / (1.0 + jnp.exp(-pre))
     output[...] = (pre * gate).astype(jnp.bfloat16)
     exact = cotangent[...].astype(jnp.float32) * (gate * (1.0 + pre * (1.0 - gate)))
-    grad = exact.astype(jnp.bfloat16)
+    grad[...] = exact.astype(jnp.bfloat16)
     grad_out[...] = lax.dot_general(
-        kernel, grad, (((1,), (1,)), ((), ())), preferred_element_type=jnp.float32
+        kernel, grad[...], (((1,), (1,)), ((), ())), preferred_element_type=jnp.float32
     ).astype(jnp.bfloat16)
+    summed[...] = high
+    bias_part[...] = jnp.sum(exact, axis=0, keepdims=True)
+
+
+def weight_kernel(summed, grad, bias_part, message):
     weight_term = lax.dot_general(
-        high, grad, (((0,), (0,)), ((), ())), preferred_element_type=jnp.float32
-    )
-    bias_term = jnp.sum(exact, axis=0, keepdims=True)
+        summed[...], grad[...], (((0,), (0,)), ((), ())), preferred_element_type=jnp.float32
+    )
+    bias_term = bias_part[...]
     bias_high = bias_term.astype(jnp.bfloat16).astype(jnp.float32)
-    lines = lax.broadcasted_iota(jnp.int32, (SLICE, bias_term.shape[1]), 0)
-    tail = jnp.where(lines == 0, bias_high, jnp.where(lines == 1, bias_term - bias_high, 0.0))
+    lines = lax.broadcasted_iota(jnp.int32, (SLICE, LANES), 0)
+    tail = jnp.zeros((SLICE, LANES), jnp.float32)
+    chunks = bias_term.shape[1] // LANES
+    for half, values in enumerate((bias_high, bias_term - bias_high)):
+        for chunk in range(chunks):
+            row = values[:, chunk * LANES : (chunk + 1) * LANES]
+            tail = jnp.where(lines == half * chunks + chunk, row, tail)
+    tail = tail.astype(jnp.bfloat16)
+    width = weight_term.shape[1]
     for index in range(message.shape[0]):
         rows = weight_term[index * SLICE : (index + 1) * SLICE, :]
-        message[index] = jnp.concatenate([rows, tail], axis=0).astype(jnp.bfloat16)
+        message[index, :, :width] = rows.astype(jnp.bfloat16)
+        message[index, :, width:] = tail
 
 
 def backward_kernel(
@@ -135,10 +169,17 @@
             ].astype(out.dtype)
 
 
-def slice_kernel(scale, received, part, bias_out):
+def slice_kernel(scale, received, after, part, bias_out):
+    del after
     total = jnp.sum(received[...].astype(jnp.float32), axis=0) * scale
-    part[...] = jnp.broadcast_to(total[:SLICE].astype(jnp.bfloat16)[None], part.shape)
-    bias_out[...] = total[SLICE : SLICE + 1] + total[SLICE + 1 : SLICE + 2]
+    width = part.shape[2]
+    part[...] = jnp.broadcast_to(total[:, :width].astype(jnp.bfloat16)[None], part.shape)
+    chunks = width // LANES
+    tail = total[:, width:]
+    for chunk in range(chunks):
+        bias_out[:, chunk * LANES : (chunk + 1) * LANES] = (
+            tail[chunk : chunk + 1] + tail[chunks + chunk : chunks + chunk + 1]
+        )
 
 
 def last_kernel(mine, near, across, far, grad_inputs):
@@ -146,6 +187,11 @@
     for part in (near, across, far):
         total = total + part[...].astype(jnp.float32)
     grad_inputs[...] = total.T.astype(jnp.bfloat16)
+
+
+def join_kernel(parts, grad_weight):
+    for index in range(parts.shape[0]):
+        grad_weight[index * SLICE : (index + 1) * SLICE, :] = parts[index].astype(jnp.float32)
 
 
 def shards(
@@ -159,9 +205,29 @@
     sources = columns * VB
     bf16, f32 = jnp.bfloat16, jnp.float32
 
+    values, own, bias = call(
+        stage_kernel,
+        [
+            jax.ShapeDtypeStruct(block_values.shape, bf16),
+            jax.ShapeDtypeStruct(features.shape, bf16),
+            jax.ShapeDtypeStruct((1, width), f32),
+        ],
+        [pltpu.SemaphoreType.DMA] * 3,
+        LONG,
+        [pltpu.HBM] * 3,
+        "stage",
+    )(block_values, features, bias[None, :])
     near = swapped(features, "col", 1)
     across = swapped(features, "col", 2)
     far = swapped(across, "col", 1)
+    head = call(
+        table_kernel,
+        [jax.ShapeDtypeStruct((sources - VB, BLK, width), bf16)],
+        [],
+        LONG,
+        [VMEM] * 3,
+        "feature_table",
+    )(own, near, across)[0]
     whole = jax.ShapeDtypeStruct((own_rows, width), bf16)
     wide = jax.ShapeDtypeStruct((own_rows, width), f32)
     mine, down2, down1, up1, up2 = call(
@@ -172,9 +238,9 @@
             pltpu.VMEM((SPAN * VB + 1, BLK, width), f32),
         ],
         2 * slots * BLK * BLK * width,
-        [SMEM] * 3 + [VMEM] * 5,
+        [SMEM] * 3 + [VMEM] * 3,
         "aggregate_terms",
-    )(block_count, block_target, block_source, block_values, features, near, across, far)
+    )(block_count, block_target, block_source, values, head, far)
 
     from_up2 = shifted(down2, "row", -2)
     from_down2 = shifted(up2, "row", 2)
@@ -182,19 +248,27 @@
     from_down1 = shifted(up1, "row", 1)
     flipped = jax.ShapeDtypeStruct((width, own_rows), bf16)
     slices = width // SLICE
-    output, grad_out, message = call(
+    output, grad_out, summed, grad, bias_part = call(
         middle_kernel,
-        [whole, flipped, jax.ShapeDtypeStruct((slices, 2 * SLICE, width), bf16)],
+        [whole, flipped, whole, whole, jax.ShapeDtypeStruct((1, width), f32)],
         [],
-        2 * 4 * own_rows * width * width,
+        2 * 3 * own_rows * width * width,
         [VMEM] * 8,
-        "pointwise_and_weight",
-    )(mine, from_up2, from_up1, from_down1, from_down2, weight, bias[None, :], cotangent)
+        "pointwise",
+    )(mine, from_up2, from_up1, from_down1, from_down2, weight, bias, cotangent)
 
     grad_up2 = shifted(grad_out, "row", -2)
     grad_down2 = shifted(grad_out, "row", 2)
     grad_up1 = shifted(grad_out, "row", -1)
     grad_down1 = shifted(grad_out, "row", 1)
+    message = call(
+        weight_kernel,
+        [jax.ShapeDtypeStruct((slices, SLICE, width + LANES), bf16)],
+        [],
+        LONG,
+        [VMEM] * 3,
+        "weight_term",
+    )(summed, grad, bias_part)[0]
     mine, near, across, far = call(
         backward_kernel,
         [jax.ShapeDtypeStruct((width, own_rows), f32)] + [flipped] * 3,
@@ -202,11 +276,11 @@
             pltpu.VMEM((SPAN * VB, width, BLK), bf16),
             pltpu.VMEM((sources + 1, width, BLK), f32),
         ],
-        2 * slots * BLK * BLK * width,
+        LONG,
         [SMEM] * 3 + [VMEM] * 6,
         "source_terms",
     )(
-        block_count, block_target, block_source, block_values,
+        block_count, block_target, block_source, values,
         grad_down2, grad_down1, grad_out, grad_up1, grad_up2,
     )
     near = swapped(near, "col", 1)
@@ -224,22 +298,26 @@
                 jax.ShapeDtypeStruct((1, width), f32),
             ],
             [],
-            slices * SLICE * width,
-            [VMEM],
+            LONG,
+            [VMEM, pl.ANY],
             "weight_slice",
-        )(received)
-        weight_total = lax.all_to_all(part, everyone, 0, 0, tiled=True)
-        weight_total = weight_total.reshape(width, width).astype(f32)
+        )(received, mine)
+        parts = lax.all_to_all(part, everyone, 0, 0, tiled=True)
         bias_total = bias_total[0]
     else:
-        summed = lax.psum(message.astype(f32), everyone) * scale
-        weight_total = summed[:, :SLICE].reshape(width, width)
-        bias_total = summed[0, SLICE] + summed[0, SLICE + 1]
-
-    grad_inputs = call(
-        last_kernel, [whole], [], own_rows * width * 4, [VMEM] * 4, "source_sum"
-    )(mine, near, across, far)[0]
-    return (output, grad_inputs, weight_total, bias_total)
+        total = lax.psum(message.astype(f32), everyone) * scale
+        parts = total[:, :, :width].astype(bf16)
+        chunks = width // LANES
+        tail = total[0, : 2 * chunks, width:].reshape(2, width)
+        bias_total = tail[0] + tail[1]
+
+    grad_inputs = call(last_kernel, [whole], [], LONG, [VMEM] * 4, "source_sum")(
+        mine, near, across, far
+    )[0]
+    grad_weight = call(
+        join_kernel, [jax.ShapeDtypeStruct((width, width), f32)], [], LONG, [VMEM], "weight_join"
+    )(parts)[0]
+    return (output, grad_inputs, grad_weight, bias_total)
 
 
 def solution(mesh):

time: 63.3 us -> 58.5 us (0.924)
  starting transfers between devices: 29.8 us -> 24.3 us
  Pallas kernels: 6.18 us -> 7.23 us
  other arithmetic: 0.72 us -> 0 us
  waiting for transfers between devices: 22.3 us -> 23 us
  local copies, waits for them, and re-layouts: 2.81 us -> 2.15 us
    ppermute x6, waiting for transfers between devices: 11 us -> 1.94 us  [swapped(): return lax.ppermute(block, axis, [(i, i ^ bit) for i in range(size)])]
    all_to_all x1, waiting for transfers between devices: 0.01 us -> 7.4 us  [shards(): parts = lax.all_to_all(part, everyone, 0, 0, tiled=True)]
    all_to_all x1, starting transfers between devices: 5.45 us -> 2.71 us  [shards(): parts = lax.all_to_all(part, everyone, 0, 0, tiled=True)]
    all_to_all x1, waiting for transfers between devices: 2.1 us -> 4.6 us  [shards(): received = lax.all_to_all(message, everyone, 0, 0, tiled=True)]
    pallas_call x2 -> x6, Pallas kernels: 2.12 us -> 3.77 us  [the longest x1 1.05 us: shards(): call(middle_kernel, [whole, flipped, whole, whole, jax.ShapeDtypeStruct((...]
    ppermute x8, starting transfers between devices: 15 us -> 13.6 us  [shifted(): lax.ppermute(block, axis, [(i, (i + distance) % size) for i in range(size)])]
    all_to_all x1, starting transfers between devices: 4.37 us -> 3.05 us  [shards(): received = lax.all_to_all(message, everyone, 0, 0, tiled=True)]
    convert_element_type x1 -> x0, other arithmetic: 0.72 us -> none  [shards(): weight_total = weight_total.reshape(width, width).astype(f32)]
  transfers between devices with their start and end apart: 16 -> 16, of which waited for: 9 -> 8; matrix products, arithmetic and copies ran while one was open for 0% -> 0% of each run, Pallas kernels for 5% -> 7%
where the time goes in v2:
time: 58.5 us; the launch traced here: 58.1 us
  starting transfers between devices  24.3 us (42%)
  waiting for transfers between devices  23 us (39%)
  Pallas kernels  7.23 us (12%)
  local copies, waits for them, and re-layouts  2.15 us (4%)
  between operations  1.42 us (2%)
    ppermute x8, starting transfers between devices, shifted(): lax.ppermute(block, axis, [(i, (i + distance) % size) for i in range(size)])  13.6 us
    ppermute x8, waiting for transfers between devices, shifted(): lax.ppermute(block, axis, [(i, (i + distance) % size) for i in range(size)])  9.04 us
    all_to_all x1, waiting for transfers between devices, shards(): parts = lax.all_to_all(part, everyone, 0, 0, tiled=True)  7.4 us
    ppermute x6, starting transfers between devices, swapped(): return lax.ppermute(block, axis, [(i, i ^ bit) for i in range(size)])  4.96 us
    all_to_all x1, waiting for transfers between devices, shards(): received = lax.all_to_all(message, everyone, 0, 0, tiled=True)  4.6 us
    all_to_all x1, starting transfers between devices, shards(): received = lax.all_to_all(message, everyone, 0, 0, tiled=True)  3.05 us
    all_to_all x1, starting transfers between devices, shards(): parts = lax.all_to_all(part, everyone, 0, 0, tiled=True)  2.71 us
    unnamed x14, local copies, waits for them, and re-layouts  2.15 us
  transfers between devices with their start and end apart: 16, of which 8 were waited for; matrix products, arithmetic and copies ran while one was open for 0% of the time, Pallas kernels for 7%

profile of v2, /device:TPU:0, one launch (start us, length us, event | category | flops | bytes accessed | tf_op | source)
XLA Modules:
  0.0 58.1 jit_solution(16418847743431654642)
XLA Ops:
  0.6 3.0 %collective-permute-start.1 = (bf16[256,256]{1,0:T(8,128)(2,1)}, bf16[256,256]{1,0:T(8,128)(2,1)S(1)}, u32[]{:S(2)}, u32[]{:S(2)}) collective-permute-start(bf16[256,256]{1,0:T(8,128)(2,1)} %own.1), channel_id=1, source_target_pairs={{0,2},{1,3},{2,0},{3,1},{4,6},{5,7},{6,4},{7,5},{8,10},{9,11},{10,... | collective-permute-start | bytes 393224 | tf_op jit(solution)/shard_map/ppermute | solution.py:30
  3.7 1.2 %copy-done.4 = bf16[1,1,32,128,128]{4,3,2,1,0:T(8,128)(2,1)S(1)} copy-done((bf16[1,1,32,128,128]{4,3,2,1,0:T(8,128)(2,1)S(1)}, bf16[1,1,32,128,128]{4,3,2,1,0:T(8,128)(2,1)}, u32[]{:S(2)}) %copy-start.4) | copy-done | bytes 1048600
  4.9 0.9 %copy-done.5 = bf16[256,256]{1,0:T(8,128)(2,1)S(1)} copy-done((bf16[256,256]{1,0:T(8,128)(2,1)S(1)}, bf16[256,256]{1,0:T(8,128)(2,1)}, u32[]{:S(2)}) %copy-start.5) | copy-done | bytes 131096
  5.8 0.3 stage.1
  6.7 0.6 %collective-permute-done.1.across = bf16[256,256]{1,0:T(8,128)(2,1)S(1)} collective-permute-done((bf16[256,256]{1,0:T(8,128)(2,1)}, bf16[256,256]{1,0:T(8,128)(2,1)S(1)}, u32[]{:S(2)}, u32[]{:S(2)}) %collective-permute-start.1) | collective-permute-done | bytes 131104 | tf_op jit(solution)/shard_map/ppermute | solution.py:30
  7.4 0.0 copy-start.3
  7.4 1.3 %collective-permute-done.2.far = bf16[256,256]{1,0:T(8,128)(2,1)S(1)} collective-permute-done((bf16[256,256]{1,0:T(8,128)(2,1)S(1)}, bf16[256,256]{1,0:T(8,128)(2,1)S(1)}, u32[]{:S(2)}, u32[]{:S(2)}) %collective-permute-start.2) | collective-permute-done | bytes 131104 | tf_op jit(solution)/shard_map/ppermute | solution.py:30
  8.7 1.4 %aggregate_terms.1 = (f32[256,256]{1,0:T(8,128)S(1)}, bf16[256,256]{1,0:T(8,128)(2,1)S(1)}, bf16[256,256]{1,0:T(8,128)(2,1)S(1)}, bf16[256,256]{1,0:T(8,128)(2,1)S(1)}, bf16[256,256]{1,0:T(8,128)(2,1)S(1)}) custom-call(s32[1,1]{1,0:T(1,128)S(6)} %copy.12.count, s32[1,1,32]{2,1,0:T(1,128)S(1)} %copy-done.2, s32[1,1,32]{2,1,0:T(1,128)S(1)} %copy-done.3, ...), custom_call_target="tpu_custom_call" | custom-call | flops 268435456 | bytes 1048576 | tf_op jit(solution)/shard_map/aggregate_terms/pallas_call | solution.py:233
  10.1 4.2 %collective-permute-start.3 = (bf16[256,256]{1,0:T(8,128)(2,1)S(1)}, bf16[256,256]{1,0:T(8,128)(2,1)S(1)}, u32[]{:S(2)}, u32[]{:S(2)}) collective-permute-start(bf16[256,256]{1,0:T(8,128)(2,1)S(1)} %get-tuple-element.26), channel_id=1, source_target_pairs={{0,24},{4,28},{8,0},{12,4},{16,8},{20,12},{24,16},{28,20},{1,25},{... | collective-permute-start | bytes 393224 | tf_op jit(solution)/shard_map/ppermute | solution.py:25
  14.3 1.7 %collective-permute-start.4 = (bf16[256,256]{1,0:T(8,128)(2,1)S(1)}, bf16[256,256]{1,0:T(8,128)(2,1)S(1)}, u32[]{:S(2)}, u32[]{:S(2)}) collective-permute-start(bf16[256,256]{1,0:T(8,128)(2,1)S(1)} %get-tuple-element.27), channel_id=1, source_target_pairs={{0,28},{4,0},{8,4},{12,8},{16,12},{20,16},{24,20},{28,24},{1,29},{... | collective-permute-start | bytes 393224 | tf_op jit(solution)/shard_map/ppermute | solution.py:25
  16.0 0.3 collective-permute-start.5
  16.3 0.4 collective-permute-start.6
  16.7 1.6 %collective-permute-done.3.from_up2 = bf16[256,256]{1,0:T(8,128)(2,1)S(1)} collective-permute-done((bf16[256,256]{1,0:T(8,128)(2,1)S(1)}, bf16[256,256]{1,0:T(8,128)(2,1)S(1)}, u32[]{:S(2)}, u32[]{:S(2)}) %collective-permute-start.3) | collective-permute-done | bytes 131104 | tf_op jit(solution)/shard_map/ppermute | solution.py:25
  18.2 2.8 %collective-permute-done.4.from_up1 = bf16[256,256]{1,0:T(8,128)(2,1)S(1)} collective-permute-done((bf16[256,256]{1,0:T(8,128)(2,1)S(1)}, bf16[256,256]{1,0:T(8,128)(2,1)S(1)}, u32[]{:S(2)}, u32[]{:S(2)}) %collective-permute-start.4) | collective-permute-done | bytes 131104 | tf_op jit(solution)/shard_map/ppermute | solution.py:25
  21.1 3.7 %collective-permute-done.5.from_down1 = bf16[256,256]{1,0:T(8,128)(2,1)S(1)} collective-permute-done((bf16[256,256]{1,0:T(8,128)(2,1)S(1)}, bf16[256,256]{1,0:T(8,128)(2,1)S(1)}, u32[]{:S(2)}, u32[]{:S(2)}) %collective-permute-start.5) | collective-permute-done | bytes 131104 | tf_op jit(solution)/shard_map/ppermute | solution.py:25
  24.8 1.1 %pointwise.1 = (bf16[256,256]{1,0:T(8,128)(2,1)}, bf16[256,256]{1,0:T(8,128)(2,1)S(1)}, bf16[256,256]{1,0:T(8,128)(2,1)S(1)}, bf16[256,256]{1,0:T(8,128)(2,1)S(1)}, f32[1,256]{1,0:T(1,128)S(1)}) custom-call(f32[256,256]{1,0:T(8,128)S(1)} %get-tuple-element.25.mine, bf16[256,256]{1,0:T(8,128)(2,1)S(1)} %collective-permute-done.3.from_up2, ...), custom_call_target="tpu_custom_call" | custom-call | flops 100663296 | bytes 1048576 | tf_op jit(solution)/shard_map/pointwise/pallas_call | solution.py:251
  25.9 2.3 %collective-permute-start.10 = (bf16[256,256]{1,0:T(8,128)(2,1)S(1)}, bf16[256,256]{1,0:T(8,128)(2,1)S(1)}, u32[]{:S(2)}, u32[]{:S(2)}) collective-permute-start(bf16[256,256]{1,0:T(8,128)(2,1)S(1)} %get-tuple-element.32.local), channel_id=1, source_target_pairs={{0,24},{4,28},{8,0},{12,4},{16,8},{20,12},{24,16},{28,20},{1,25},{... | collective-permute-start | bytes 393224 | tf_op jit(solution)/shard_map/ppermute | solution.py:25
  28.2 1.7 %collective-permute-start.8 = (bf16[256,256]{1,0:T(8,128)(2,1)S(1)}, bf16[256,256]{1,0:T(8,128)(2,1)S(1)}, u32[]{:S(2)}, u32[]{:S(2)}) collective-permute-start(bf16[256,256]{1,0:T(8,128)(2,1)S(1)} %get-tuple-element.32.local), channel_id=1, source_target_pairs={{0,4},{4,8},{8,12},{12,16},{16,20},{20,24},{24,28},{28,0},{1,5},{5... | collective-permute-start | bytes 393224 | tf_op jit(solution)/shard_map/ppermute | solution.py:25
  29.8 3.0 %collective-permute-start.9 = (bf16[256,256]{1,0:T(8,128)(2,1)S(1)}, bf16[256,256]{1,0:T(8,128)(2,1)S(1)}, u32[]{:S(2)}, u32[]{:S(2)}) collective-permute-start(bf16[256,256]{1,0:T(8,128)(2,1)S(1)} %get-tuple-element.32.local), channel_id=1, source_target_pairs={{0,28},{4,0},{8,4},{12,8},{16,12},{20,16},{24,20},{28,24},{1,29},{... | collective-permute-start | bytes 393224 | tf_op jit(solution)/shard_map/ppermute | solution.py:25
  32.9 0.9 %weight_term.1 = bf16[32,8,384]{2,1,0:T(8,128)(2,1)} custom-call(bf16[256,256]{1,0:T(8,128)(2,1)S(1)} %get-tuple-element.37.summed, bf16[256,256]{1,0:T(8,128)(2,1)S(1)} %get-tuple-element.38.grad, f32[1,256]{1,0:T(1,128)S(1)} %get-tuple-element.39.bias_part), custom_call_target="tpu_custom_call" | custom-call | flops 99999997952 | bytes 1048576 | tf_op jit(solution)/shard_map/weight_term/pallas_call | solution.py:264
  33.8 3.1 %all-to-all-start = ((bf16[32,8,384]{2,1,0:T(8,128)(2,1)}), bf16[32,8,384]{2,1,0:T(8,128)(2,1)S(1)}, u32[]{:S(2)}, u32[]{:S(2)}) async-start(bf16[32,8,384]{2,1,0:T(8,128)(2,1)} %weight_term.1), calls=%async_computation | async-start | bytes 393216 | tf_op jit(solution)/shard_map/all_to_all | solution.py:293
  36.9 0.9 %collective-permute-done.8.from_down1 = bf16[256,256]{1,0:T(8,128)(2,1)S(1)} collective-permute-done((bf16[256,256]{1,0:T(8,128)(2,1)S(1)}, bf16[256,256]{1,0:T(8,128)(2,1)S(1)}, u32[]{:S(2)}, u32[]{:S(2)}) %collective-permute-start.8) | collective-permute-done | bytes 131104 | tf_op jit(solution)/shard_map/ppermute | solution.py:25
  37.8 1.4 %source_terms.1 = (f32[256,256]{1,0:T(8,128)S(1)}, bf16[256,256]{1,0:T(8,128)(2,1)S(1)}, bf16[256,256]{1,0:T(8,128)(2,1)S(1)}, bf16[256,256]{1,0:T(8,128)(2,1)S(1)}) custom-call(s32[1,1]{1,0:T(1,128)S(6)} %copy.12.count, s32[1,1,32]{2,1,0:T(1,128)S(1)} %copy-done.2, s32[1,1,32]{2,1,0:T(1,128)S(1)} %copy-done.3, ...), custom_call_target="tpu_custom_call" | custom-call | flops 99999997952 | bytes 1048576 | tf_op jit(solution)/shard_map/source_terms/pallas_call | solution.py:272
  39.2 0.1 collective-permute-start.11
  39.3 1.8 %collective-permute-start.12 = (bf16[256,256]{1,0:T(8,128)(2,1)S(1)}, bf16[256,256]{1,0:T(8,128)(2,1)S(1)}, u32[]{:S(2)}, u32[]{:S(2)}) collective-permute-start(bf16[256,256]{1,0:T(8,128)(2,1)S(1)} %get-tuple-element.35), channel_id=1, source_target_pairs={{0,2},{1,3},{2,0},{3,1},{4,6},{5,7},{6,4},{7,5},{8,10},{9,11},{10,... | collective-permute-start | bytes 393224 | tf_op jit(solution)/shard_map/ppermute | solution.py:30
  41.1 0.1 collective-permute-start.13
  41.1 4.6 %all-to-all-done.received = bf16[32,8,384]{2,1,0:T(8,128)(2,1)S(1)} async-done(((bf16[32,8,384]{2,1,0:T(8,128)(2,1)}), bf16[32,8,384]{2,1,0:T(8,128)(2,1)S(1)}, u32[]{:S(2)}, u32[]{:S(2)}) %all-to-all-start) | async-done | bytes 196640 | tf_op jit(solution)/shard_map/all_to_all | solution.py:293
  45.7 0.7 %weight_slice.1 = (bf16[32,8,256]{2,1,0:T(8,128)(2,1)}, f32[1,256]{1,0:T(1,128)}) custom-call(bf16[32,8,384]{2,1,0:T(8,128)(2,1)S(1)} %all-to-all-done.received, f32[256,256]{1,0:T(8,128)S(1)} %get-tuple-element.33.mine.after), custom_call_target="tpu_custom_call" | custom-call | flops 99999997952 | bytes 1048576 | tf_op jit(solution)/shard_map/weight_slice/pallas_call | solution.py:294
  46.4 2.7 %all-to-all-start.1 = ((bf16[32,8,256]{2,1,0:T(8,128)(2,1)}), bf16[32,8,256]{2,1,0:T(8,128)(2,1)S(1)}, u32[]{:S(2)}, u32[]{:S(2)}) async-start(bf16[32,8,256]{2,1,0:T(8,128)(2,1)} %get-tuple-element.40), calls=%async_computation.1 | async-start | bytes 262144 | tf_op jit(solution)/shard_map/all_to_all | solution.py:305
  49.2 0.8 %source_sum.1 = bf16[256,256]{1,0:T(8,128)(2,1)} custom-call(f32[256,256]{1,0:T(8,128)S(1)} %get-tuple-element.33.mine.after, bf16[256,256]{1,0:T(8,128)(2,1)S(1)} %collective-permute-done.11.near, bf16[256,256]{1,0:T(8,128)(2,1)S(1)} %collective-permute-done.12.across, bf16[256,256]{1,0:T(8,128)(2,1)S(1)} %collective-permute-done.13.far), custom_call_target="tpu_custom_call" | custom-call | flops 99999997952 | bytes 1048576 | tf_op jit(solution)/shard_map/source_sum/pallas_call | solution.py:314
  50.0 7.4 %all-to-all-done.1.parts = bf16[32,8,256]{2,1,0:T(8,128)(2,1)S(1)} async-done(((bf16[32,8,256]{2,1,0:T(8,128)(2,1)}), bf16[32,8,256]{2,1,0:T(8,128)(2,1)S(1)}, u32[]{:S(2)}, u32[]{:S(2)}) %all-to-all-start.1) | async-done | bytes 131104 | tf_op jit(solution)/shard_map/all_to_all | solution.py:305
  57.4 0.7 %weight_join.1 = f32[256,256]{1,0:T(8,128)} custom-call(bf16[32,8,256]{2,1,0:T(8,128)(2,1)S(1)} %all-to-all-done.1.parts), custom_call_target="tpu_custom_call" | custom-call | flops 99999997952 | bytes 1048576 | tf_op jit(solution)/shard_map/weight_join/pallas_call | solution.py:317
  (23 shorter events, 0.1 us)
Async XLA Ops:
  0.6 3.0 %copy-start.6 = (f32[256]{0:T(256)S(1)}, f32[256]{0:T(256)}, u32[]{:S(2)}) copy-start(f32[256]{0:T(256)} %param.10) | copy-start | bytes 3076
  0.6 6.7 %collective-permute-start.1 = (bf16[256,256]{1,0:T(8,128)(2,1)}, bf16[256,256]{1,0:T(8,128)(2,1)S(1)}, u32[]{:S(2)}, u32[]{:S(2)}) collective-permute-start(bf16[256,256]{1,0:T(8,128)(2,1)} %own.1), channel_id=1, source_target_pairs={{0,2},{1,3},{2,0},{3,1},{4,6},{5,7},{6,4},{7,5},{8,10},{9,11},{10,... | collective-permute-start | bytes 393224 | tf_op jit(solution)/shard_map/ppermute | solution.py:30
  3.6 3.7 %collective-permute-start = (bf16[256,256]{1,0:T(8,128)(2,1)}, bf16[256,256]{1,0:T(8,128)(2,1)S(1)}, u32[]{:S(2)}, u32[]{:S(2)}) collective-permute-start(bf16[256,256]{1,0:T(8,128)(2,1)} %own.1), channel_id=1, source_target_pairs={{0,1},{1,0},{2,3},{3,2},{4,5},{5,4},{6,7},{7,6},{8,9},{9,8},{10,11... | collective-permute-start | bytes 393224 | tf_op jit(solution)/shard_map/ppermute | solution.py:30
  3.7 1.2 %copy-start.4 = (bf16[1,1,32,128,128]{4,3,2,1,0:T(8,128)(2,1)S(1)}, bf16[1,1,32,128,128]{4,3,2,1,0:T(8,128)(2,1)}, u32[]{:S(2)}) copy-start(bf16[1,1,32,128,128]{4,3,2,1,0:T(8,128)(2,1)} %values.1) | copy-start | bytes 3145732
  4.9 0.9 %copy-start.5 = (bf16[256,256]{1,0:T(8,128)(2,1)S(1)}, bf16[256,256]{1,0:T(8,128)(2,1)}, u32[]{:S(2)}) copy-start(bf16[256,256]{1,0:T(8,128)(2,1)} %own.1) | copy-start | bytes 393220
  7.4 1.3 %collective-permute-start.2 = (bf16[256,256]{1,0:T(8,128)(2,1)S(1)}, bf16[256,256]{1,0:T(8,128)(2,1)S(1)}, u32[]{:S(2)}, u32[]{:S(2)}) collective-permute-start(bf16[256,256]{1,0:T(8,128)(2,1)S(1)} %collective-permute-done.1.across), channel_id=1, source_target_pairs={{0,1},{1,0},{2,3},{3,2},{4,5},{5,4},{6,7},{7,6},{8,9},{9,8},{10,11... | collective-permute-start | bytes 393224 | tf_op jit(solution)/shard_map/ppermute | solution.py:30
  7.4 1.3 %copy-start.2 = (s32[1,1,32]{2,1,0:T(1,128)S(1)}, s32[1,1,32]{2,1,0:T(1,128)}, u32[]{:S(2)}) copy-start(s32[1,1,32]{2,1,0:T(1,128)} %target.3) | copy-start | bytes 388
  7.4 1.3 %copy-start.3 = (s32[1,1,32]{2,1,0:T(1,128)S(1)}, s32[1,1,32]{2,1,0:T(1,128)}, u32[]{:S(2)}) copy-start(s32[1,1,32]{2,1,0:T(1,128)} %source.3) | copy-start | bytes 388
  8.7 16.1 %copy-start = (bf16[256,256]{1,0:T(8,128)(2,1)S(1)}, bf16[256,256]{1,0:T(8,128)(2,1)}, u32[]{:S(2)}) copy-start(bf16[256,256]{1,0:T(8,128)(2,1)} %weight.1) | copy-start | bytes 393220
  8.7 16.1 %copy-start.1 = (bf16[256,256]{1,0:T(8,128)(2,1)S(1)}, bf16[256,256]{1,0:T(8,128)(2,1)}, u32[]{:S(2)}) copy-start(bf16[256,256]{1,0:T(8,128)(2,1)} %cotangent.1) | copy-start | bytes 393220
  10.1 8.2 %collective-permute-start.3 = (bf16[256,256]{1,0:T(8,128)(2,1)S(1)}, bf16[256,256]{1,0:T(8,128)(2,1)S(1)}, u32[]{:S(2)}, u32[]{:S(2)}) collective-permute-start(bf16[256,256]{1,0:T(8,128)(2,1)S(1)} %get-tuple-element.26), channel_id=1, source_target_pairs={{0,24},{4,28},{8,0},{12,4},{16,8},{20,12},{24,16},{28,20},{1,25},{... | collective-permute-start | bytes 393224 | tf_op jit(solution)/shard_map/ppermute | solution.py:25
  14.3 6.8 %collective-permute-start.4 = (bf16[256,256]{1,0:T(8,128)(2,1)S(1)}, bf16[256,256]{1,0:T(8,128)(2,1)S(1)}, u32[]{:S(2)}, u32[]{:S(2)}) collective-permute-start(bf16[256,256]{1,0:T(8,128)(2,1)S(1)} %get-tuple-element.27), channel_id=1, source_target_pairs={{0,28},{4,0},{8,4},{12,8},{16,12},{20,16},{24,20},{28,24},{1,29},{... | collective-permute-start | bytes 393224 | tf_op jit(solution)/shard_map/ppermute | solution.py:25
  16.0 8.8 %collective-permute-start.5 = (bf16[256,256]{1,0:T(8,128)(2,1)S(1)}, bf16[256,256]{1,0:T(8,128)(2,1)S(1)}, u32[]{:S(2)}, u32[]{:S(2)}) collective-permute-start(bf16[256,256]{1,0:T(8,128)(2,1)S(1)} %get-tuple-element.28), channel_id=1, source_target_pairs={{0,4},{4,8},{8,12},{12,16},{16,20},{20,24},{24,28},{28,0},{1,5},{5... | collective-permute-start | bytes 393224 | tf_op jit(solution)/shard_map/ppermute | solution.py:25
  16.3 8.5 %collective-permute-start.6 = (bf16[256,256]{1,0:T(8,128)(2,1)S(1)}, bf16[256,256]{1,0:T(8,128)(2,1)S(1)}, u32[]{:S(2)}, u32[]{:S(2)}) collective-permute-start(bf16[256,256]{1,0:T(8,128)(2,1)S(1)} %get-tuple-element.29), channel_id=1, source_target_pairs={{0,8},{4,12},{8,16},{12,20},{16,24},{20,28},{24,0},{28,4},{1,9},{5... | collective-permute-start | bytes 393224 | tf_op jit(solution)/shard_map/ppermute | solution.py:25
  25.9 11.0 %collective-permute-start.10 = (bf16[256,256]{1,0:T(8,128)(2,1)S(1)}, bf16[256,256]{1,0:T(8,128)(2,1)S(1)}, u32[]{:S(2)}, u32[]{:S(2)}) collective-permute-start(bf16[256,256]{1,0:T(8,128)(2,1)S(1)} %get-tuple-element.32.local), channel_id=1, source_target_pairs={{0,24},{4,28},{8,0},{12,4},{16,8},{20,12},{24,16},{28,20},{1,25},{... | collective-permute-start | bytes 393224 | tf_op jit(solution)/shard_map/ppermute | solution.py:25
  28.1 8.7 %collective-permute-start.7 = (bf16[256,256]{1,0:T(8,128)(2,1)S(1)}, bf16[256,256]{1,0:T(8,128)(2,1)S(1)}, u32[]{:S(2)}, u32[]{:S(2)}) collective-permute-start(bf16[256,256]{1,0:T(8,128)(2,1)S(1)} %get-tuple-element.32.local), channel_id=1, source_target_pairs={{0,8},{4,12},{8,16},{12,20},{16,24},{20,28},{24,0},{28,4},{1,9},{5... | collective-permute-start | bytes 393224 | tf_op jit(solution)/shard_map/ppermute | solution.py:25
  28.2 9.6 %collective-permute-start.8 = (bf16[256,256]{1,0:T(8,128)(2,1)S(1)}, bf16[256,256]{1,0:T(8,128)(2,1)S(1)}, u32[]{:S(2)}, u32[]{:S(2)}) collective-permute-start(bf16[256,256]{1,0:T(8,128)(2,1)S(1)} %get-tuple-element.32.local), channel_id=1, source_target_pairs={{0,4},{4,8},{8,12},{12,16},{16,20},{20,24},{24,28},{28,0},{1,5},{5... | collective-permute-start | bytes 393224 | tf_op jit(solution)/shard_map/ppermute | solution.py:25
  29.8 7.9 %collective-permute-start.9 = (bf16[256,256]{1,0:T(8,128)(2,1)S(1)}, bf16[256,256]{1,0:T(8,128)(2,1)S(1)}, u32[]{:S(2)}, u32[]{:S(2)}) collective-permute-start(bf16[256,256]{1,0:T(8,128)(2,1)S(1)} %get-tuple-element.32.local), channel_id=1, source_target_pairs={{0,28},{4,0},{8,4},{12,8},{16,12},{20,16},{24,20},{28,24},{1,29},{... | collective-permute-start | bytes 393224 | tf_op jit(solution)/shard_map/ppermute | solution.py:25
  33.8 11.9 %all-to-all-start = ((bf16[32,8,384]{2,1,0:T(8,128)(2,1)}), bf16[32,8,384]{2,1,0:T(8,128)(2,1)S(1)}, u32[]{:S(2)}, u32[]{:S(2)}) async-start(bf16[32,8,384]{2,1,0:T(8,128)(2,1)} %weight_term.1), calls=%async_computation | async-start | bytes 393216 | tf_op jit(solution)/shard_map/all_to_all | solution.py:293
  39.2 10.0 %collective-permute-start.11 = (bf16[256,256]{1,0:T(8,128)(2,1)S(1)}, bf16[256,256]{1,0:T(8,128)(2,1)S(1)}, u32[]{:S(2)}, u32[]{:S(2)}) collective-permute-start(bf16[256,256]{1,0:T(8,128)(2,1)S(1)} %get-tuple-element.34), channel_id=1, source_target_pairs={{0,1},{1,0},{2,3},{3,2},{4,5},{5,4},{6,7},{7,6},{8,9},{9,8},{10,11... | collective-permute-start | bytes 393224 | tf_op jit(solution)/shard_map/ppermute | solution.py:30
  39.3 9.9 %collective-permute-start.12 = (bf16[256,256]{1,0:T(8,128)(2,1)S(1)}, bf16[256,256]{1,0:T(8,128)(2,1)S(1)}, u32[]{:S(2)}, u32[]{:S(2)}) collective-permute-start(bf16[256,256]{1,0:T(8,128)(2,1)S(1)} %get-tuple-element.35), channel_id=1, source_target_pairs={{0,2},{1,3},{2,0},{3,1},{4,6},{5,7},{6,4},{7,5},{8,10},{9,11},{10,... | collective-permute-start | bytes 393224 | tf_op jit(solution)/shard_map/ppermute | solution.py:30
  41.1 8.1 %collective-permute-start.13 = (bf16[256,256]{1,0:T(8,128)(2,1)S(1)}, bf16[256,256]{1,0:T(8,128)(2,1)S(1)}, u32[]{:S(2)}, u32[]{:S(2)}) collective-permute-start(bf16[256,256]{1,0:T(8,128)(2,1)S(1)} %get-tuple-element.36), channel_id=1, source_target_pairs={{0,3},{1,2},{2,1},{3,0},{4,7},{5,6},{6,5},{7,4},{8,11},{9,10},{10,... | collective-permute-start | bytes 393224 | tf_op jit(solution)/shard_map/ppermute | solution.py:30
  46.4 10.9 %all-to-all-start.1 = ((bf16[32,8,256]{2,1,0:T(8,128)(2,1)}), bf16[32,8,256]{2,1,0:T(8,128)(2,1)S(1)}, u32[]{:S(2)}, u32[]{:S(2)}) async-start(bf16[32,8,256]{2,1,0:T(8,128)(2,1)} %get-tuple-element.40), calls=%async_computation.1 | async-start | bytes 262144 | tf_op jit(solution)/shard_map/all_to_all | solution.py:305

commit v3 on v2

--- a/solution.py
+++ b/solution.py
@@ -12,8 +12,7 @@
 HALF = 2
 VB = 2
 SPAN = 2 * HALF + 1
-SLICE = 8
-LANES = 128
+TAIL = 8
 SLOT_GROUP = 8
 LONG = 10**11
 VMEM = pltpu.VMEM
@@ -123,25 +122,33 @@
     bias_part[...] = jnp.sum(exact, axis=0, keepdims=True)
 
 
-def weight_kernel(summed, grad, bias_part, message):
-    weight_term = lax.dot_general(
+def split_tail(row):
+    high = row.astype(jnp.bfloat16).astype(jnp.float32)
+    lines = lax.broadcasted_iota(jnp.int32, (TAIL, row.shape[1]), 0)
+    return jnp.where(lines == 0, high, jnp.where(lines == 1, row - high, 0.0))
+
+
+def weight_kernel(summed, grad, bias_part, mine, near, across, far, product):
+    column = lax.axis_index("col")
+    product[...] = lax.dot_general(
         summed[...], grad[...], (((0,), (0,)), ((), ())), preferred_element_type=jnp.float32
     )
-    bias_term = bias_part[...]
-    bias_high = bias_term.astype(jnp.bfloat16).astype(jnp.float32)
-    lines = lax.broadcasted_iota(jnp.int32, (SLICE, LANES), 0)
-    tail = jnp.zeros((SLICE, LANES), jnp.float32)
-    chunks = bias_term.shape[1] // LANES
-    for half, values in enumerate((bias_high, bias_term - bias_high)):
-        for chunk in range(chunks):
-            row = values[:, chunk * LANES : (chunk + 1) * LANES]
-            tail = jnp.where(lines == half * chunks + chunk, row, tail)
-    tail = tail.astype(jnp.bfloat16)
-    width = weight_term.shape[1]
-    for index in range(message.shape[0]):
-        rows = weight_term[index * SLICE : (index + 1) * SLICE, :]
-        message[index, :, :width] = rows.astype(jnp.bfloat16)
-        message[index, :, width:] = tail
+    tail = split_tail(bias_part[...])
+    share = mine.shape[0] - TAIL
+    for relative, out in enumerate((mine, near, across, far)):
+        start = pl.multiple_of((column ^ relative) * share, share)
+        rows = product[pl.ds(start, share), :]
+        out[...] = jnp.concatenate([rows, tail], axis=0).astype(out.dtype)
+
+
+def column_sum_kernel(mine, near, across, far, message):
+    total = mine[...]
+    for part in (near, across, far):
+        total = total + part[...].astype(jnp.float32)
+    share = total.shape[0] - TAIL
+    tail = split_tail(total[share : share + 1] + total[share + 1 : share + 2])
+    total = jnp.concatenate([total[:share], tail], axis=0).astype(jnp.bfloat16)
+    message[...] = jnp.broadcast_to(total[None], message.shape)
 
 
 def backward_kernel(
@@ -169,17 +176,12 @@
             ].astype(out.dtype)
 
 
-def slice_kernel(scale, received, after, part, bias_out):
+def row_sum_kernel(scale, received, after, part, bias_out):
     del after
     total = jnp.sum(received[...].astype(jnp.float32), axis=0) * scale
-    width = part.shape[2]
-    part[...] = jnp.broadcast_to(total[:, :width].astype(jnp.bfloat16)[None], part.shape)
-    chunks = width // LANES
-    tail = total[:, width:]
-    for chunk in range(chunks):
-        bias_out[:, chunk * LANES : (chunk + 1) * LANES] = (
-            tail[chunk : chunk + 1] + tail[chunks + chunk : chunks + chunk + 1]
-        )
+    share = part.shape[0]
+    part[...] = total[:share].astype(part.dtype)
+    bias_out[...] = total[share : share + 1] + total[share + 1 : share + 2]
 
 
 def last_kernel(mine, near, across, far, grad_inputs):
@@ -189,9 +191,12 @@
     grad_inputs[...] = total.T.astype(jnp.bfloat16)
 
 
-def join_kernel(parts, grad_weight):
-    for index in range(parts.shape[0]):
-        grad_weight[index * SLICE : (index + 1) * SLICE, :] = parts[index].astype(jnp.float32)
+def join_kernel(own, near, across, far, grad_weight):
+    column = lax.axis_index("col")
+    share = own.shape[0]
+    for relative, part in enumerate((own, near, across, far)):
+        start = pl.multiple_of((column ^ relative) * share, share)
+        grad_weight[pl.ds(start, share), :] = part[...].astype(jnp.float32)
 
 
 def shards(
@@ -247,7 +252,6 @@
     from_up1 = shifted(down1, "row", -1)
     from_down1 = shifted(up1, "row", 1)
     flipped = jax.ShapeDtypeStruct((width, own_rows), bf16)
-    slices = width // SLICE
     output, grad_out, summed, grad, bias_part = call(
         middle_kernel,
         [whole, flipped, whole, whole, jax.ShapeDtypeStruct((1, width), f32)],
@@ -261,14 +265,29 @@
     grad_down2 = shifted(grad_out, "row", 2)
     grad_up1 = shifted(grad_out, "row", -1)
     grad_down1 = shifted(grad_out, "row", 1)
-    message = call(
+    share = width // columns
+    packed = (share + TAIL, width)
+    weight_mine, weight_near, weight_across, weight_far = call(
         weight_kernel,
-        [jax.ShapeDtypeStruct((slices, SLICE, width + LANES), bf16)],
-        [],
+        [jax.ShapeDtypeStruct(packed, f32)] + [jax.ShapeDtypeStruct(packed, bf16)] * 3,
+        [pltpu.VMEM((width, width), f32)],
         LONG,
         [VMEM] * 3,
         "weight_term",
-    )(summed, grad, bias_part)[0]
+    )(summed, grad, bias_part)
+    message = call(
+        column_sum_kernel,
+        [jax.ShapeDtypeStruct((rows,) + packed, bf16)],
+        [],
+        LONG,
+        [VMEM] * 4,
+        "weight_column_sum",
+    )(
+        weight_mine,
+        swapped(weight_near, "col", 1),
+        swapped(weight_across, "col", 2),
+        swapped(weight_far, "col", 3),
+    )[0]
     mine, near, across, far = call(
         backward_kernel,
         [jax.ShapeDtypeStruct((width, own_rows), f32)] + [flipped] * 3,
@@ -288,36 +307,27 @@
     far = swapped(far, "col", 3)
 
     scale = 1.0 / math.sqrt(own_rows * rows * columns)
-    everyone = ("row", "col")
-    if slices == rows * columns:
-        received = lax.all_to_all(message, everyone, 0, 0, tiled=True)
-        part, bias_total = call(
-            functools.partial(slice_kernel, scale),
-            [
-                jax.ShapeDtypeStruct((slices, SLICE, width), bf16),
-                jax.ShapeDtypeStruct((1, width), f32),
-            ],
-            [],
-            LONG,
-            [VMEM, pl.ANY],
-            "weight_slice",
-        )(received, mine)
-        parts = lax.all_to_all(part, everyone, 0, 0, tiled=True)
-        bias_total = bias_total[0]
+    if rows > 8:
+        received = lax.psum(message[:1].astype(f32), "row")
     else:
-        total = lax.psum(message.astype(f32), everyone) * scale
-        parts = total[:, :, :width].astype(bf16)
-        chunks = width // LANES
-        tail = total[0, : 2 * chunks, width:].reshape(2, width)
-        bias_total = tail[0] + tail[1]
+        received = lax.all_to_all(message, "row", 0, 0, tiled=True)
+    part, bias_total = call(
+        functools.partial(row_sum_kernel, scale),
+        [jax.ShapeDtypeStruct((share, width), bf16), jax.ShapeDtypeStruct((1, width), f32)],
+        [],
+        LONG,
+        [VMEM, pl.ANY],
+        "weight_row_sum",
+    )(received, mine)
+    parts = [part] + [swapped(part, "col", bit) for bit in (1, 2, 3)]
 
     grad_inputs = call(last_kernel, [whole], [], LONG, [VMEM] * 4, "source_sum")(
         mine, near, across, far
     )[0]
     grad_weight = call(
-        join_kernel, [jax.ShapeDtypeStruct((width, width), f32)], [], LONG, [VMEM], "weight_join"
-    )(parts)[0]
-    return (output, grad_inputs, grad_weight, bias_total)
+        join_kernel, [jax.ShapeDtypeStruct((width, width), f32)], [], LONG, [VMEM] * 4, "weight_join"
+    )(*parts)[0]
+    return (output, grad_inputs, grad_weight, bias_total[0])
 
 
 def solution(mesh):

time: 58.5 us -> 54.4 us (0.930)
  waiting for transfers between devices: 23 us -> 16.3 us
  starting transfers between devices: 24.3 us -> 26.9 us
    all_to_all x2 -> x1, waiting for transfers between devices: 12 us -> 4.97 us  [shards(): received = lax.all_to_all(message, 'row', 0, 0, tiled=True)]
    ppermute x6 -> x12, starting transfers between devices: 4.96 us -> 8.79 us  [swapped(): return lax.ppermute(block, axis, [(i, i ^ bit) for i in range(size)])]
    ppermute x8, starting transfers between devices: 13.6 us -> 12 us  [shifted(): lax.ppermute(block, axis, [(i, (i + distance) % size) for i in range(size)])]
    ppermute x6 -> x12, waiting for transfers between devices: 1.94 us -> 3.28 us  [swapped(): return lax.ppermute(block, axis, [(i, i ^ bit) for i in range(size)])]
    ppermute x8, waiting for transfers between devices: 9.04 us -> 8.05 us  [shifted(): lax.ppermute(block, axis, [(i, (i + distance) % size) for i in range(size)])]
    all_to_all x2 -> x1, starting transfers between devices: 5.76 us -> 6.07 us  [shards(): received = lax.all_to_all(message, 'row', 0, 0, tiled=True)]
    pallas_call x2 -> x3, Pallas kernels: 1.61 us -> 1.57 us  [the longest x1 0.74 us: shards(): call(column_sum_kernel, [jax.ShapeDtypeStruct((rows,) + packed, bf16)], [...]
    unnamed x14 -> x22, local copies, waits for them, and re-layouts: 2.15 us -> 2.17 us
  transfers between devices with their start and end apart: 16 -> 21, of which waited for: 8 -> 9; matrix products, arithmetic and copies ran while one was open for 0% -> 0% of each run, Pallas kernels for 7% -> 7%
where the time goes in v3:
time: 54.4 us; the launch traced here: 54 us
  starting transfers between devices  26.9 us (49%)
  waiting for transfers between devices  16.3 us (30%)
  Pallas kernels  7.2 us (13%)
  local copies, waits for them, and re-layouts  2.17 us (4%)
  between operations  1.43 us (3%)
    ppermute x8, starting transfers between devices, shifted(): lax.ppermute(block, axis, [(i, (i + distance) % size) for i in range(size)])  12 us
    ppermute x12, starting transfers between devices, swapped(): return lax.ppermute(block, axis, [(i, i ^ bit) for i in range(size)])  8.79 us
    ppermute x8, waiting for transfers between devices, shifted(): lax.ppermute(block, axis, [(i, (i + distance) % size) for i in range(size)])  8.05 us
    all_to_all x1, starting transfers between devices, shards(): received = lax.all_to_all(message, 'row', 0, 0, tiled=True)  6.07 us
    all_to_all x1, waiting for transfers between devices, shards(): received = lax.all_to_all(message, 'row', 0, 0, tiled=True)  4.97 us
    ppermute x12, waiting for transfers between devices, swapped(): return lax.ppermute(block, axis, [(i, i ^ bit) for i in range(size)])  3.28 us
    unnamed x22, local copies, waits for them, and re-layouts  2.17 us
    pallas_call x1, Pallas kernels, shards(): call(backward_kernel, [jax.ShapeDtypeStruct((width, own_rows), f32)] + [f...  1.39 us
  transfers between devices with their start and end apart: 21, of which 9 were waited for; matrix products, arithmetic and copies ran while one was open for 0% of the time, Pallas kernels for 7%

profile of v3, /device:TPU:0, one launch (start us, length us, event | category | flops | bytes accessed | tf_op | source)
XLA Modules:
  0.0 54.0 jit_solution(4279149575826462930)
XLA Ops:
  0.6 3.0 %collective-permute-start.1 = (bf16[256,256]{1,0:T(8,128)(2,1)}, bf16[256,256]{1,0:T(8,128)(2,1)S(1)}, u32[]{:S(2)}, u32[]{:S(2)}) collective-permute-start(bf16[256,256]{1,0:T(8,128)(2,1)} %own.1), channel_id=1, source_target_pairs={{0,2},{1,3},{2,0},{3,1},{4,6},{5,7},{6,4},{7,5},{8,10},{9,11},{10,... | collective-permute-start | bytes 393224 | tf_op jit(solution)/shard_map/ppermute | solution.py:29
  3.7 1.2 %copy-done.8 = bf16[1,1,32,128,128]{4,3,2,1,0:T(8,128)(2,1)S(1)} copy-done((bf16[1,1,32,128,128]{4,3,2,1,0:T(8,128)(2,1)S(1)}, bf16[1,1,32,128,128]{4,3,2,1,0:T(8,128)(2,1)}, u32[]{:S(2)}) %copy-start.8) | copy-done | bytes 1048600
  4.9 0.9 %copy-done.9 = bf16[256,256]{1,0:T(8,128)(2,1)S(1)} copy-done((bf16[256,256]{1,0:T(8,128)(2,1)S(1)}, bf16[256,256]{1,0:T(8,128)(2,1)}, u32[]{:S(2)}) %copy-start.9) | copy-done | bytes 131096
  6.7 0.6 %collective-permute-done.1.across = bf16[256,256]{1,0:T(8,128)(2,1)S(1)} collective-permute-done((bf16[256,256]{1,0:T(8,128)(2,1)}, bf16[256,256]{1,0:T(8,128)(2,1)S(1)}, u32[]{:S(2)}, u32[]{:S(2)}) %collective-permute-start.1) | collective-permute-done | bytes 131104 | tf_op jit(solution)/shard_map/ppermute | solution.py:29
  7.4 1.3 %collective-permute-done.2.far = bf16[256,256]{1,0:T(8,128)(2,1)S(1)} collective-permute-done((bf16[256,256]{1,0:T(8,128)(2,1)S(1)}, bf16[256,256]{1,0:T(8,128)(2,1)S(1)}, u32[]{:S(2)}, u32[]{:S(2)}) %collective-permute-start.2) | collective-permute-done | bytes 131104 | tf_op jit(solution)/shard_map/ppermute | solution.py:29
  8.7 1.4 %aggregate_terms.1 = (f32[256,256]{1,0:T(8,128)S(1)}, bf16[256,256]{1,0:T(8,128)(2,1)S(1)}, bf16[256,256]{1,0:T(8,128)(2,1)S(1)}, bf16[256,256]{1,0:T(8,128)(2,1)S(1)}, bf16[256,256]{1,0:T(8,128)(2,1)S(1)}) custom-call(s32[1,1]{1,0:T(1,128)S(6)} %copy.12.count, s32[1,1,32]{2,1,0:T(1,128)S(1)} %copy-done.4, s32[1,1,32]{2,1,0:T(1,128)S(1)} %copy-done.6, ...), custom_call_target="tpu_custom_call" | custom-call | flops 268435456 | bytes 1048576 | tf_op jit(solution)/shard_map/aggregate_terms/pallas_call | solution.py:238
  10.1 4.5 %collective-permute-start.3 = (bf16[256,256]{1,0:T(8,128)(2,1)S(1)}, bf16[256,256]{1,0:T(8,128)(2,1)S(1)}, u32[]{:S(2)}, u32[]{:S(2)}) collective-permute-start(bf16[256,256]{1,0:T(8,128)(2,1)S(1)} %get-tuple-element.30), channel_id=1, source_target_pairs={{0,24},{4,28},{8,0},{12,4},{16,8},{20,12},{24,16},{28,20},{1,25},{... | collective-permute-start | bytes 393224 | tf_op jit(solution)/shard_map/ppermute | solution.py:24
  14.6 1.1 %collective-permute-start.4 = (bf16[256,256]{1,0:T(8,128)(2,1)S(1)}, bf16[256,256]{1,0:T(8,128)(2,1)S(1)}, u32[]{:S(2)}, u32[]{:S(2)}) collective-permute-start(bf16[256,256]{1,0:T(8,128)(2,1)S(1)} %get-tuple-element.31), channel_id=1, source_target_pairs={{0,28},{4,0},{8,4},{12,8},{16,12},{20,16},{24,20},{28,24},{1,29},{... | collective-permute-start | bytes 393224 | tf_op jit(solution)/shard_map/ppermute | solution.py:24
  15.7 0.9 %collective-permute-start.5 = (bf16[256,256]{1,0:T(8,128)(2,1)S(1)}, bf16[256,256]{1,0:T(8,128)(2,1)S(1)}, u32[]{:S(2)}, u32[]{:S(2)}) collective-permute-start(bf16[256,256]{1,0:T(8,128)(2,1)S(1)} %get-tuple-element.32), channel_id=1, source_target_pairs={{0,4},{4,8},{8,12},{12,16},{16,20},{20,24},{24,28},{28,0},{1,5},{5... | collective-permute-start | bytes 393224 | tf_op jit(solution)/shard_map/ppermute | solution.py:24
  16.7 0.6 %collective-permute-start.6 = (bf16[256,256]{1,0:T(8,128)(2,1)S(1)}, bf16[256,256]{1,0:T(8,128)(2,1)S(1)}, u32[]{:S(2)}, u32[]{:S(2)}) collective-permute-start(bf16[256,256]{1,0:T(8,128)(2,1)S(1)} %get-tuple-element.33), channel_id=1, source_target_pairs={{0,8},{4,12},{8,16},{12,20},{16,24},{20,28},{24,0},{28,4},{1,9},{5... | collective-permute-start | bytes 393224 | tf_op jit(solution)/shard_map/ppermute | solution.py:24
  17.3 1.4 %collective-permute-done.3.from_up2 = bf16[256,256]{1,0:T(8,128)(2,1)S(1)} collective-permute-done((bf16[256,256]{1,0:T(8,128)(2,1)S(1)}, bf16[256,256]{1,0:T(8,128)(2,1)S(1)}, u32[]{:S(2)}, u32[]{:S(2)}) %collective-permute-start.3) | collective-permute-done | bytes 131104 | tf_op jit(solution)/shard_map/ppermute | solution.py:24
  18.7 2.7 %collective-permute-done.4.from_up1 = bf16[256,256]{1,0:T(8,128)(2,1)S(1)} collective-permute-done((bf16[256,256]{1,0:T(8,128)(2,1)S(1)}, bf16[256,256]{1,0:T(8,128)(2,1)S(1)}, u32[]{:S(2)}, u32[]{:S(2)}) %collective-permute-start.4) | collective-permute-done | bytes 131104 | tf_op jit(solution)/shard_map/ppermute | solution.py:24
  21.4 3.3 %collective-permute-done.5.from_down1 = bf16[256,256]{1,0:T(8,128)(2,1)S(1)} collective-permute-done((bf16[256,256]{1,0:T(8,128)(2,1)S(1)}, bf16[256,256]{1,0:T(8,128)(2,1)S(1)}, u32[]{:S(2)}, u32[]{:S(2)}) %collective-permute-start.5) | collective-permute-done | bytes 131104 | tf_op jit(solution)/shard_map/ppermute | solution.py:24
  24.7 1.1 %pointwise.1 = (bf16[256,256]{1,0:T(8,128)(2,1)}, bf16[256,256]{1,0:T(8,128)(2,1)S(1)}, bf16[256,256]{1,0:T(8,128)(2,1)S(1)}, bf16[256,256]{1,0:T(8,128)(2,1)S(1)}, f32[1,256]{1,0:T(1,128)S(1)}) custom-call(f32[256,256]{1,0:T(8,128)S(1)} %get-tuple-element.29.mine, bf16[256,256]{1,0:T(8,128)(2,1)S(1)} %collective-permute-done.3.from_up2, ...), custom_call_target="tpu_custom_call" | custom-call | flops 100663296 | bytes 1048576 | tf_op jit(solution)/shard_map/pointwise/pallas_call | solution.py:255
  26.1 1.3 %collective-permute-start.15 = (bf16[72,256]{1,0:T(8,128)(2,1)S(1)}, bf16[72,256]{1,0:T(8,128)(2,1)S(1)}, u32[]{:S(2)}, u32[]{:S(2)}) collective-permute-start(bf16[72,256]{1,0:T(8,128)(2,1)S(1)} %get-tuple-element.46), channel_id=1, source_target_pairs={{0,2},{1,3},{2,0},{3,1},{4,6},{5,7},{6,4},{7,5},{8,10},{9,11},{10,... | collective-permute-start | bytes 110600 | tf_op jit(solution)/shard_map/ppermute | solution.py:29
  27.4 0.6 %collective-permute-start.16 = (bf16[72,256]{1,0:T(8,128)(2,1)S(1)}, bf16[72,256]{1,0:T(8,128)(2,1)S(1)}, u32[]{:S(2)}, u32[]{:S(2)}) collective-permute-start(bf16[72,256]{1,0:T(8,128)(2,1)S(1)} %get-tuple-element.47), channel_id=1, source_target_pairs={{0,3},{1,2},{2,1},{3,0},{4,7},{5,6},{6,5},{7,4},{8,11},{9,10},{10,... | collective-permute-start | bytes 110600 | tf_op jit(solution)/shard_map/ppermute | solution.py:29
  28.0 2.2 %collective-permute-start.10 = (bf16[256,256]{1,0:T(8,128)(2,1)S(1)}, bf16[256,256]{1,0:T(8,128)(2,1)S(1)}, u32[]{:S(2)}, u32[]{:S(2)}) collective-permute-start(bf16[256,256]{1,0:T(8,128)(2,1)S(1)} %get-tuple-element.36.local), channel_id=1, source_target_pairs={{0,24},{4,28},{8,0},{12,4},{16,8},{20,12},{24,16},{28,20},{1,25},{... | collective-permute-start | bytes 393224 | tf_op jit(solution)/shard_map/ppermute | solution.py:24
  30.1 1.0 %collective-permute-start.9 = (bf16[256,256]{1,0:T(8,128)(2,1)S(1)}, bf16[256,256]{1,0:T(8,128)(2,1)S(1)}, u32[]{:S(2)}, u32[]{:S(2)}) collective-permute-start(bf16[256,256]{1,0:T(8,128)(2,1)S(1)} %get-tuple-element.36.local), channel_id=1, source_target_pairs={{0,28},{4,0},{8,4},{12,8},{16,12},{20,16},{24,20},{28,24},{1,29},{... | collective-permute-start | bytes 393224 | tf_op jit(solution)/shard_map/ppermute | solution.py:24
  31.2 1.0 %collective-permute-start.8 = (bf16[256,256]{1,0:T(8,128)(2,1)S(1)}, bf16[256,256]{1,0:T(8,128)(2,1)S(1)}, u32[]{:S(2)}, u32[]{:S(2)}) collective-permute-start(bf16[256,256]{1,0:T(8,128)(2,1)S(1)} %get-tuple-element.36.local), channel_id=1, source_target_pairs={{0,4},{4,8},{8,12},{12,16},{16,20},{20,24},{24,28},{28,0},{1,5},{5... | collective-permute-start | bytes 393224 | tf_op jit(solution)/shard_map/ppermute | solution.py:24
  32.2 0.6 %collective-permute-start.7 = (bf16[256,256]{1,0:T(8,128)(2,1)S(1)}, bf16[256,256]{1,0:T(8,128)(2,1)S(1)}, u32[]{:S(2)}, u32[]{:S(2)}) collective-permute-start(bf16[256,256]{1,0:T(8,128)(2,1)S(1)} %get-tuple-element.36.local), channel_id=1, source_target_pairs={{0,8},{4,12},{8,16},{12,20},{16,24},{20,28},{24,0},{28,4},{1,9},{5... | collective-permute-start | bytes 393224 | tf_op jit(solution)/shard_map/ppermute | solution.py:24
  32.8 0.7 %weight_column_sum.1 = bf16[8,72,256]{2,1,0:T(8,128)(2,1)} custom-call(f32[72,256]{1,0:T(8,128)S(1)} %get-tuple-element.44.mine, bf16[72,256]{1,0:T(8,128)(2,1)S(1)} %collective-permute-done.14.near, bf16[72,256]{1,0:T(8,128)(2,1)S(1)} %collective-permute-done.15.across, bf16[72,256]{1,0:T(8,128)(2,1)S(1)} %collective-permute-done.16.far), custom_call_target="tpu_custom_call" | custom-call | flops 99999997952 | bytes 1048576 | tf_op jit(solution)/shard_map/weight_column_sum/pallas_call | solution.py:278
  33.5 6.1 %all-to-all-start = ((bf16[8,72,256]{2,1,0:T(8,128)(2,1)}), bf16[8,72,256]{2,1,0:T(8,128)(2,1)S(1)}, u32[]{:S(2)}, u32[]{:S(2)}) async-start(bf16[8,72,256]{2,1,0:T(8,128)(2,1)} %weight_column_sum.1), calls=%async_computation | async-start | bytes 589824 | tf_op jit(solution)/shard_map/all_to_all | solution.py:313
  39.6 0.6 %collective-permute-done.8.from_down1 = bf16[256,256]{1,0:T(8,128)(2,1)S(1)} collective-permute-done((bf16[256,256]{1,0:T(8,128)(2,1)S(1)}, bf16[256,256]{1,0:T(8,128)(2,1)S(1)}, u32[]{:S(2)}, u32[]{:S(2)}) %collective-permute-start.8) | collective-permute-done | bytes 131104 | tf_op jit(solution)/shard_map/ppermute | solution.py:24
  40.3 1.4 %source_terms.1 = (f32[256,256]{1,0:T(8,128)S(1)}, bf16[256,256]{1,0:T(8,128)(2,1)S(1)}, bf16[256,256]{1,0:T(8,128)(2,1)S(1)}, bf16[256,256]{1,0:T(8,128)(2,1)S(1)}) custom-call(s32[1,1]{1,0:T(1,128)S(6)} %copy.12.count, s32[1,1,32]{2,1,0:T(1,128)S(1)} %copy-done.5, s32[1,1,32]{2,1,0:T(1,128)S(1)} %copy-done.7, bf16[1,1,32,128,128]{4,3,2,1,0:T(8,128)(2,1)S(1)} %copy-done.1, ...), custom_call_target="tpu_custom_call" | custom-call | flops 99999997952 | bytes 1048576 | tf_op jit(solution)/shard_map/source_terms/pallas_call | solution.py:291
  41.8 1.8 %collective-permute-start.12 = (bf16[256,256]{1,0:T(8,128)(2,1)S(1)}, bf16[256,256]{1,0:T(8,128)(2,1)S(1)}, u32[]{:S(2)}, u32[]{:S(2)}) collective-permute-start(bf16[256,256]{1,0:T(8,128)(2,1)S(1)} %get-tuple-element.39), channel_id=1, source_target_pairs={{0,2},{1,3},{2,0},{3,1},{4,6},{5,7},{6,4},{7,5},{8,10},{9,11},{10,... | collective-permute-start | bytes 393224 | tf_op jit(solution)/shard_map/ppermute | solution.py:29
  43.6 5.0 %all-to-all-done.received = bf16[8,72,256]{2,1,0:T(8,128)(2,1)S(1)} async-done(((bf16[8,72,256]{2,1,0:T(8,128)(2,1)}), bf16[8,72,256]{2,1,0:T(8,128)(2,1)S(1)}, u32[]{:S(2)}, u32[]{:S(2)}) %all-to-all-start) | async-done | bytes 294944 | tf_op jit(solution)/shard_map/all_to_all | solution.py:313
  48.6 0.6 %weight_row_sum.1 = (bf16[64,256]{1,0:T(8,128)(2,1)S(1)}, f32[1,256]{1,0:T(1,128)}) custom-call(bf16[8,72,256]{2,1,0:T(8,128)(2,1)S(1)} %all-to-all-done.received, f32[256,256]{1,0:T(8,128)S(1)} %get-tuple-element.37.mine.after), custom_call_target="tpu_custom_call" | custom-call | flops 99999997952 | bytes 1048576 | tf_op jit(solution)/shard_map/weight_row_sum/pallas_call | solution.py:314
  49.2 1.8 %collective-permute-start.18 = (bf16[64,256]{1,0:T(8,128)(2,1)S(1)}, bf16[64,256]{1,0:T(8,128)(2,1)S(1)}, u32[]{:S(2)}, u32[]{:S(2)}) collective-permute-start(bf16[64,256]{1,0:T(8,128)(2,1)S(1)} %get-tuple-element.48.own), channel_id=1, source_target_pairs={{0,2},{1,3},{2,0},{3,1},{4,6},{5,7},{6,4},{7,5},{8,10},{9,11},{10,... | collective-permute-start | bytes 98312 | tf_op jit(solution)/shard_map/ppermute | solution.py:29
  51.1 0.8 %source_sum.1 = bf16[256,256]{1,0:T(8,128)(2,1)} custom-call(f32[256,256]{1,0:T(8,128)S(1)} %get-tuple-element.37.mine.after, bf16[256,256]{1,0:T(8,128)(2,1)S(1)} %collective-permute-done.11.near, bf16[256,256]{1,0:T(8,128)(2,1)S(1)} %collective-permute-done.12.across, bf16[256,256]{1,0:T(8,128)(2,1)S(1)} %collective-permute-done.13.far), custom_call_target="tpu_custom_call" | custom-call | flops 99999997952 | bytes 1048576 | tf_op jit(solution)/shard_map/source_sum/pallas_call | solution.py:324
  51.9 0.7 %collective-permute-done.19.far = bf16[64,256]{1,0:T(8,128)(2,1)S(1)} collective-permute-done((bf16[64,256]{1,0:T(8,128)(2,1)S(1)}, bf16[64,256]{1,0:T(8,128)(2,1)S(1)}, u32[]{:S(2)}, u32[]{:S(2)}) %collective-permute-start.19) | collective-permute-done | bytes 32800 | tf_op jit(solution)/shard_map/ppermute | solution.py:29
  52.6 0.6 %collective-permute-done.18.across = bf16[64,256]{1,0:T(8,128)(2,1)S(1)} collective-permute-done((bf16[64,256]{1,0:T(8,128)(2,1)S(1)}, bf16[64,256]{1,0:T(8,128)(2,1)S(1)}, u32[]{:S(2)}, u32[]{:S(2)}) %collective-permute-start.18) | collective-permute-done | bytes 32800 | tf_op jit(solution)/shard_map/ppermute | solution.py:29
  53.2 0.7 %weight_join.1 = f32[256,256]{1,0:T(8,128)} custom-call(bf16[64,256]{1,0:T(8,128)(2,1)S(1)} %get-tuple-element.48.own, bf16[64,256]{1,0:T(8,128)(2,1)S(1)} %collective-permute-done.17.near, bf16[64,256]{1,0:T(8,128)(2,1)S(1)} %collective-permute-done.18.across, bf16[64,256]{1,0:T(8,128)(2,1)S(1)} %collective-permute-done.19.far), custom_call_target="tpu_custom_call" | custom-call | flops 99999997952 | bytes 1048576 | tf_op jit(solution)/shard_map/weight_join/pallas_call | solution.py:327
  (42 shorter events, 1.0 us)
Async XLA Ops:
  0.6 3.0 %copy-start.10 = (f32[256]{0:T(256)S(1)}, f32[256]{0:T(256)}, u32[]{:S(2)}) copy-start(f32[256]{0:T(256)} %param.10) | copy-start | bytes 3076
  0.6 6.7 %collective-permute-start.1 = (bf16[256,256]{1,0:T(8,128)(2,1)}, bf16[256,256]{1,0:T(8,128)(2,1)S(1)}, u32[]{:S(2)}, u32[]{:S(2)}) collective-permute-start(bf16[256,256]{1,0:T(8,128)(2,1)} %own.1), channel_id=1, source_target_pairs={{0,2},{1,3},{2,0},{3,1},{4,6},{5,7},{6,4},{7,5},{8,10},{9,11},{10,... | collective-permute-start | bytes 393224 | tf_op jit(solution)/shard_map/ppermute | solution.py:29
  3.6 3.7 %collective-permute-start = (bf16[256,256]{1,0:T(8,128)(2,1)}, bf16[256,256]{1,0:T(8,128)(2,1)S(1)}, u32[]{:S(2)}, u32[]{:S(2)}) collective-permute-start(bf16[256,256]{1,0:T(8,128)(2,1)} %own.1), channel_id=1, source_target_pairs={{0,1},{1,0},{2,3},{3,2},{4,5},{5,4},{6,7},{7,6},{8,9},{9,8},{10,11... | collective-permute-start | bytes 393224 | tf_op jit(solution)/shard_map/ppermute | solution.py:29
  3.7 1.2 %copy-start.8 = (bf16[1,1,32,128,128]{4,3,2,1,0:T(8,128)(2,1)S(1)}, bf16[1,1,32,128,128]{4,3,2,1,0:T(8,128)(2,1)}, u32[]{:S(2)}) copy-start(bf16[1,1,32,128,128]{4,3,2,1,0:T(8,128)(2,1)} %values.1) | copy-start | bytes 3145732
  4.9 0.9 %copy-start.9 = (bf16[256,256]{1,0:T(8,128)(2,1)S(1)}, bf16[256,256]{1,0:T(8,128)(2,1)}, u32[]{:S(2)}) copy-start(bf16[256,256]{1,0:T(8,128)(2,1)} %own.1) | copy-start | bytes 393220
  6.1 2.6 %copy-start = (bf16[1,1,32,128,128]{4,3,2,1,0:T(8,128)(2,1)}, bf16[1,1,32,128,128]{4,3,2,1,0:T(8,128)(2,1)S(1)}, u32[]{:S(2)}) copy-start(bf16[1,1,32,128,128]{4,3,2,1,0:T(8,128)(2,1)S(1)} %get-tuple-element.27.values) | copy-start | bytes 3145732
  7.4 1.3 %collective-permute-start.2 = (bf16[256,256]{1,0:T(8,128)(2,1)S(1)}, bf16[256,256]{1,0:T(8,128)(2,1)S(1)}, u32[]{:S(2)}, u32[]{:S(2)}) collective-permute-start(bf16[256,256]{1,0:T(8,128)(2,1)S(1)} %collective-permute-done.1.across), channel_id=1, source_target_pairs={{0,1},{1,0},{2,3},{3,2},{4,5},{5,4},{6,7},{7,6},{8,9},{9,8},{10,11... | collective-permute-start | bytes 393224 | tf_op jit(solution)/shard_map/ppermute | solution.py:29
  7.4 1.3 %copy-start.4 = (s32[1,1,32]{2,1,0:T(1,128)S(1)}, s32[1,1,32]{2,1,0:T(1,128)}, u32[]{:S(2)}) copy-start(s32[1,1,32]{2,1,0:T(1,128)} %target.3) | copy-start | bytes 388
  7.4 1.3 %copy-start.6 = (s32[1,1,32]{2,1,0:T(1,128)S(1)}, s32[1,1,32]{2,1,0:T(1,128)}, u32[]{:S(2)}) copy-start(s32[1,1,32]{2,1,0:T(1,128)} %source.3) | copy-start | bytes 388
  8.7 16.0 %copy-start.2 = (bf16[256,256]{1,0:T(8,128)(2,1)S(1)}, bf16[256,256]{1,0:T(8,128)(2,1)}, u32[]{:S(2)}) copy-start(bf16[256,256]{1,0:T(8,128)(2,1)} %weight.1) | copy-start | bytes 393220
  8.7 16.0 %copy-start.3 = (bf16[256,256]{1,0:T(8,128)(2,1)S(1)}, bf16[256,256]{1,0:T(8,128)(2,1)}, u32[]{:S(2)}) copy-start(bf16[256,256]{1,0:T(8,128)(2,1)} %cotangent.1) | copy-start | bytes 393220
  10.1 8.6 %collective-permute-start.3 = (bf16[256,256]{1,0:T(8,128)(2,1)S(1)}, bf16[256,256]{1,0:T(8,128)(2,1)S(1)}, u32[]{:S(2)}, u32[]{:S(2)}) collective-permute-start(bf16[256,256]{1,0:T(8,128)(2,1)S(1)} %get-tuple-element.30), channel_id=1, source_target_pairs={{0,24},{4,28},{8,0},{12,4},{16,8},{20,12},{24,16},{28,20},{1,25},{... | collective-permute-start | bytes 393224 | tf_op jit(solution)/shard_map/ppermute | solution.py:24
  14.6 6.7 %collective-permute-start.4 = (bf16[256,256]{1,0:T(8,128)(2,1)S(1)}, bf16[256,256]{1,0:T(8,128)(2,1)S(1)}, u32[]{:S(2)}, u32[]{:S(2)}) collective-permute-start(bf16[256,256]{1,0:T(8,128)(2,1)S(1)} %get-tuple-element.31), channel_id=1, source_target_pairs={{0,28},{4,0},{8,4},{12,8},{16,12},{20,16},{24,20},{28,24},{1,29},{... | collective-permute-start | bytes 393224 | tf_op jit(solution)/shard_map/ppermute | solution.py:24
  15.7 9.0 %collective-permute-start.5 = (bf16[256,256]{1,0:T(8,128)(2,1)S(1)}, bf16[256,256]{1,0:T(8,128)(2,1)S(1)}, u32[]{:S(2)}, u32[]{:S(2)}) collective-permute-start(bf16[256,256]{1,0:T(8,128)(2,1)S(1)} %get-tuple-element.32), channel_id=1, source_target_pairs={{0,4},{4,8},{8,12},{12,16},{16,20},{20,24},{24,28},{28,0},{1,5},{5... | collective-permute-start | bytes 393224 | tf_op jit(solution)/shard_map/ppermute | solution.py:24
  16.7 8.0 %collective-permute-start.6 = (bf16[256,256]{1,0:T(8,128)(2,1)S(1)}, bf16[256,256]{1,0:T(8,128)(2,1)S(1)}, u32[]{:S(2)}, u32[]{:S(2)}) collective-permute-start(bf16[256,256]{1,0:T(8,128)(2,1)S(1)} %get-tuple-element.33), channel_id=1, source_target_pairs={{0,8},{4,12},{8,16},{12,20},{16,24},{20,28},{24,0},{28,4},{1,9},{5... | collective-permute-start | bytes 393224 | tf_op jit(solution)/shard_map/ppermute | solution.py:24
  26.0 5.1 %collective-permute-start.14 = (bf16[72,256]{1,0:T(8,128)(2,1)S(1)}, bf16[72,256]{1,0:T(8,128)(2,1)S(1)}, u32[]{:S(2)}, u32[]{:S(2)}) collective-permute-start(bf16[72,256]{1,0:T(8,128)(2,1)S(1)} %get-tuple-element.45), channel_id=1, source_target_pairs={{0,1},{1,0},{2,3},{3,2},{4,5},{5,4},{6,7},{7,6},{8,9},{9,8},{10,11... | collective-permute-start | bytes 110600 | tf_op jit(solution)/shard_map/ppermute | solution.py:29
  26.1 6.1 %collective-permute-start.15 = (bf16[72,256]{1,0:T(8,128)(2,1)S(1)}, bf16[72,256]{1,0:T(8,128)(2,1)S(1)}, u32[]{:S(2)}, u32[]{:S(2)}) collective-permute-start(bf16[72,256]{1,0:T(8,128)(2,1)S(1)} %get-tuple-element.46), channel_id=1, source_target_pairs={{0,2},{1,3},{2,0},{3,1},{4,6},{5,7},{6,4},{7,5},{8,10},{9,11},{10,... | collective-permute-start | bytes 110600 | tf_op jit(solution)/shard_map/ppermute | solution.py:29
  27.4 5.4 %collective-permute-start.16 = (bf16[72,256]{1,0:T(8,128)(2,1)S(1)}, bf16[72,256]{1,0:T(8,128)(2,1)S(1)}, u32[]{:S(2)}, u32[]{:S(2)}) collective-permute-start(bf16[72,256]{1,0:T(8,128)(2,1)S(1)} %get-tuple-element.47), channel_id=1, source_target_pairs={{0,3},{1,2},{2,1},{3,0},{4,7},{5,6},{6,5},{7,4},{8,11},{9,10},{10,... | collective-permute-start | bytes 110600 | tf_op jit(solution)/shard_map/ppermute | solution.py:29
  28.0 11.6 %collective-permute-start.10 = (bf16[256,256]{1,0:T(8,128)(2,1)S(1)}, bf16[256,256]{1,0:T(8,128)(2,1)S(1)}, u32[]{:S(2)}, u32[]{:S(2)}) collective-permute-start(bf16[256,256]{1,0:T(8,128)(2,1)S(1)} %get-tuple-element.36.local), channel_id=1, source_target_pairs={{0,24},{4,28},{8,0},{12,4},{16,8},{20,12},{24,16},{28,20},{1,25},{... | collective-permute-start | bytes 393224 | tf_op jit(solution)/shard_map/ppermute | solution.py:24
  30.1 9.5 %collective-permute-start.9 = (bf16[256,256]{1,0:T(8,128)(2,1)S(1)}, bf16[256,256]{1,0:T(8,128)(2,1)S(1)}, u32[]{:S(2)}, u32[]{:S(2)}) collective-permute-start(bf16[256,256]{1,0:T(8,128)(2,1)S(1)} %get-tuple-element.36.local), channel_id=1, source_target_pairs={{0,28},{4,0},{8,4},{12,8},{16,12},{20,16},{24,20},{28,24},{1,29},{... | collective-permute-start | bytes 393224 | tf_op jit(solution)/shard_map/ppermute | solution.py:24
  31.2 9.1 %collective-permute-start.8 = (bf16[256,256]{1,0:T(8,128)(2,1)S(1)}, bf16[256,256]{1,0:T(8,128)(2,1)S(1)}, u32[]{:S(2)}, u32[]{:S(2)}) collective-permute-start(bf16[256,256]{1,0:T(8,128)(2,1)S(1)} %get-tuple-element.36.local), channel_id=1, source_target_pairs={{0,4},{4,8},{8,12},{12,16},{16,20},{20,24},{24,28},{28,0},{1,5},{5... | collective-permute-start | bytes 393224 | tf_op jit(solution)/shard_map/ppermute | solution.py:24
  32.2 8.1 %collective-permute-start.7 = (bf16[256,256]{1,0:T(8,128)(2,1)S(1)}, bf16[256,256]{1,0:T(8,128)(2,1)S(1)}, u32[]{:S(2)}, u32[]{:S(2)}) collective-permute-start(bf16[256,256]{1,0:T(8,128)(2,1)S(1)} %get-tuple-element.36.local), channel_id=1, source_target_pairs={{0,8},{4,12},{8,16},{12,20},{16,24},{20,28},{24,0},{28,4},{1,9},{5... | collective-permute-start | bytes 393224 | tf_op jit(solution)/shard_map/ppermute | solution.py:24
  32.8 7.5 %copy-start.1 = (bf16[1,1,32,128,128]{4,3,2,1,0:T(8,128)(2,1)S(1)}, bf16[1,1,32,128,128]{4,3,2,1,0:T(8,128)(2,1)}, u32[]{:S(2)}) copy-start(bf16[1,1,32,128,128]{4,3,2,1,0:T(8,128)(2,1)} %copy-done) | copy-start | bytes 3145732
  33.5 6.7 %copy-start.5 = (s32[1,1,32]{2,1,0:T(1,128)S(1)}, s32[1,1,32]{2,1,0:T(1,128)}, u32[]{:S(2)}) copy-start(s32[1,1,32]{2,1,0:T(1,128)} %target.3) | copy-start | bytes 388
  33.5 6.7 %copy-start.7 = (s32[1,1,32]{2,1,0:T(1,128)S(1)}, s32[1,1,32]{2,1,0:T(1,128)}, u32[]{:S(2)}) copy-start(s32[1,1,32]{2,1,0:T(1,128)} %source.3) | copy-start | bytes 388
  33.5 15.1 %all-to-all-start = ((bf16[8,72,256]{2,1,0:T(8,128)(2,1)}), bf16[8,72,256]{2,1,0:T(8,128)(2,1)S(1)}, u32[]{:S(2)}, u32[]{:S(2)}) async-start(bf16[8,72,256]{2,1,0:T(8,128)(2,1)} %weight_column_sum.1), calls=%async_computation | async-start | bytes 589824 | tf_op jit(solution)/shard_map/all_to_all | solution.py:313
  41.7 9.3 %collective-permute-start.11 = (bf16[256,256]{1,0:T(8,128)(2,1)S(1)}, bf16[256,256]{1,0:T(8,128)(2,1)S(1)}, u32[]{:S(2)}, u32[]{:S(2)}) collective-permute-start(bf16[256,256]{1,0:T(8,128)(2,1)S(1)} %get-tuple-element.38), channel_id=1, source_target_pairs={{0,1},{1,0},{2,3},{3,2},{4,5},{5,4},{6,7},{7,6},{8,9},{9,8},{10,11... | collective-permute-start | bytes 393224 | tf_op jit(solution)/shard_map/ppermute | solution.py:29
  41.8 9.3 %collective-permute-start.12 = (bf16[256,256]{1,0:T(8,128)(2,1)S(1)}, bf16[256,256]{1,0:T(8,128)(2,1)S(1)}, u32[]{:S(2)}, u32[]{:S(2)}) collective-permute-start(bf16[256,256]{1,0:T(8,128)(2,1)S(1)} %get-tuple-element.39), channel_id=1, source_target_pairs={{0,2},{1,3},{2,0},{3,1},{4,6},{5,7},{6,4},{7,5},{8,10},{9,11},{10,... | collective-permute-start | bytes 393224 | tf_op jit(solution)/shard_map/ppermute | solution.py:29
  43.6 7.5 %collective-permute-start.13 = (bf16[256,256]{1,0:T(8,128)(2,1)S(1)}, bf16[256,256]{1,0:T(8,128)(2,1)S(1)}, u32[]{:S(2)}, u32[]{:S(2)}) collective-permute-start(bf16[256,256]{1,0:T(8,128)(2,1)S(1)} %get-tuple-element.40), channel_id=1, source_target_pairs={{0,3},{1,2},{2,1},{3,0},{4,7},{5,6},{6,5},{7,4},{8,11},{9,10},{10,... | collective-permute-start | bytes 393224 | tf_op jit(solution)/shard_map/ppermute | solution.py:29
  49.2 3.4 %collective-permute-start.19 = (bf16[64,256]{1,0:T(8,128)(2,1)S(1)}, bf16[64,256]{1,0:T(8,128)(2,1)S(1)}, u32[]{:S(2)}, u32[]{:S(2)}) collective-permute-start(bf16[64,256]{1,0:T(8,128)(2,1)S(1)} %get-tuple-element.48.own), channel_id=1, source_target_pairs={{0,3},{1,2},{2,1},{3,0},{4,7},{5,6},{6,5},{7,4},{8,11},{9,10},{10,... | collective-permute-start | bytes 98312 | tf_op jit(solution)/shard_map/ppermute | solution.py:29
  49.2 4.0 %collective-permute-start.18 = (bf16[64,256]{1,0:T(8,128)(2,1)S(1)}, bf16[64,256]{1,0:T(8,128)(2,1)S(1)}, u32[]{:S(2)}, u32[]{:S(2)}) collective-permute-start(bf16[64,256]{1,0:T(8,128)(2,1)S(1)} %get-tuple-element.48.own), channel_id=1, source_target_pairs={{0,2},{1,3},{2,0},{3,1},{4,6},{5,7},{6,4},{7,5},{8,10},{9,11},{10,... | collective-permute-start | bytes 98312 | tf_op jit(solution)/shard_map/ppermute | solution.py:29
  51.0 2.3 %collective-permute-start.17 = (bf16[64,256]{1,0:T(8,128)(2,1)S(1)}, bf16[64,256]{1,0:T(8,128)(2,1)S(1)}, u32[]{:S(2)}, u32[]{:S(2)}) collective-permute-start(bf16[64,256]{1,0:T(8,128)(2,1)S(1)} %get-tuple-element.48.own), channel_id=1, source_target_pairs={{0,1},{1,0},{2,3},{3,2},{4,5},{5,4},{6,7},{7,6},{8,9},{9,8},{10,11... | collective-permute-start | bytes 98312 | tf_op jit(solution)/shard_map/ppermute | solution.py:29

commit v4 on v3

--- a/solution.py
+++ b/solution.py
@@ -13,15 +13,32 @@
 VB = 2
 SPAN = 2 * HALF + 1
 TAIL = 8
-SLOT_GROUP = 8
+FORWARD = ((2, None), (1, None), (-2, None), (-1, None))
+BACKWARD = ((2, None), (1, None), (-2, None), (-1, None))
+SLOT_GROUP = 32
 LONG = 10**11
 VMEM = pltpu.VMEM
 SMEM = pltpu.SMEM
 
 
-def shifted(block, axis, distance):
-    size = lax.axis_size(axis)
-    return lax.ppermute(block, axis, [(i, (i + distance) % size) for i in range(size)])
+def offset_at(route, row):
+    reach, phase = route
+    if phase is None:
+        return reach, -reach
+    toward = reach * (1 - 2 * lax.rem(row // reach + phase, 2))
+    return toward, toward
+
+
+def routed(block, route):
+    size = lax.axis_size("row")
+    reach, phase = route
+    pairs = []
+    for i in range(size):
+        if phase is None:
+            pairs.append((i, (i + reach) % size))
+        else:
+            pairs.append((i, (i + reach * (1 - 2 * ((i // reach + phase) % 2))) % size))
+    return lax.ppermute(block, "row", pairs)
 
 
 def swapped(block, axis, bit):
@@ -75,7 +92,7 @@
 
 def forward_kernel(
     count, target, source, values, head, far,
-    mine, down2, down1, up1, up2, table, totals,
+    mine, first, second, third, fourth, table, totals,
 ):
     column = lax.axis_index("col")
     live = count[0, 0]
@@ -94,17 +111,21 @@
         )
 
     for_slots(values.shape[2], live, step)
-    for offset, out in enumerate((down2, down1, mine, up1, up2)):
+    row = lax.axis_index("row")
+    offsets = [0] + [offset_at(route, row)[0] for route in FORWARD]
+    for offset, out in zip(offsets, (mine, first, second, third, fourth)):
         for block in range(VB):
-            out[block * BLK : (block + 1) * BLK, :] = totals[offset * VB + block].astype(out.dtype)
+            out[block * BLK : (block + 1) * BLK, :] = totals[
+                (HALF + offset) * VB + block
+            ].astype(out.dtype)
 
 
 def middle_kernel(
-    mine, from_up2, from_up1, from_down1, from_down2, weight, bias, cotangent,
+    mine, first, second, third, fourth, weight, bias, cotangent,
     output, grad_out, summed, grad, bias_part,
 ):
     total = mine[...]
-    for part in (from_up2, from_up1, from_down1, from_down2):
+    for part in (first, second, third, fourth):
         total = total + part[...].astype(jnp.float32)
     high = total.astype(jnp.bfloat16)
     low = (total - high.astype(jnp.float32)).astype(jnp.bfloat16)
@@ -152,14 +173,16 @@
 
 
 def backward_kernel(
-    count, target, source, values, from_down2, from_down1, local, from_up1, from_up2,
+    count, target, source, values, local, first, second, third, fourth,
     mine, near, across, far, table, totals,
 ):
     column = lax.axis_index("col")
     live = count[0, 0]
-    for offset, part in enumerate((from_down2, from_down1, local, from_up1, from_up2)):
+    row = lax.axis_index("row")
+    offsets = [0] + [offset_at(route, row)[1] for route in BACKWARD]
+    for offset, part in zip(offsets, (local, first, second, third, fourth)):
         for block in range(VB):
-            table[offset * VB + block] = part[:, block * BLK : (block + 1) * BLK]
+            table[(HALF + offset) * VB + block] = part[:, block * BLK : (block + 1) * BLK]
     totals[...] = jnp.zeros_like(totals)
 
     def step(slot):
@@ -191,12 +214,17 @@
     grad_inputs[...] = total.T.astype(jnp.bfloat16)
 
 
-def join_kernel(own, near, across, far, grad_weight):
+def join_kernel(
+    own, near, across, far, bias_in, output_in, source_in, grad_weight, bias_out, output, grad_inputs
+):
     column = lax.axis_index("col")
     share = own.shape[0]
     for relative, part in enumerate((own, near, across, far)):
         start = pl.multiple_of((column ^ relative) * share, share)
         grad_weight[pl.ds(start, share), :] = part[...].astype(jnp.float32)
+    bias_out[...] = bias_in[...]
+    output[...] = output_in[...]
+    grad_inputs[...] = source_in[...]
 
 
 def shards(
@@ -235,7 +263,7 @@
     )(own, near, across)[0]
     whole = jax.ShapeDtypeStruct((own_rows, width), bf16)
     wide = jax.ShapeDtypeStruct((own_rows, width), f32)
-    mine, down2, down1, up1, up2 = call(
+    mine, *leaving = call(
         forward_kernel,
         [wide] + [whole] * 4,
         [
@@ -247,10 +275,7 @@
         "aggregate_terms",
     )(block_count, block_target, block_source, values, head, far)
 
-    from_up2 = shifted(down2, "row", -2)
-    from_down2 = shifted(up2, "row", 2)
-    from_up1 = shifted(down1, "row", -1)
-    from_down1 = shifted(up1, "row", 1)
+    arrived = [routed(block, route) for block, route in zip(leaving, FORWARD)]
     flipped = jax.ShapeDtypeStruct((width, own_rows), bf16)
     output, grad_out, summed, grad, bias_part = call(
         middle_kernel,
@@ -259,12 +284,9 @@
         2 * 3 * own_rows * width * width,
         [VMEM] * 8,
         "pointwise",
-    )(mine, from_up2, from_up1, from_down1, from_down2, weight, bias, cotangent)
-
-    grad_up2 = shifted(grad_out, "row", -2)
-    grad_down2 = shifted(grad_out, "row", 2)
-    grad_up1 = shifted(grad_out, "row", -1)
-    grad_down1 = shifted(grad_out, "row", 1)
+    )(mine, *arrived, weight, bias, cotangent)
+
+    arrived = [routed(grad_out, route) for route in BACKWARD]
     share = width // columns
     packed = (share + TAIL, width)
     weight_mine, weight_near, weight_across, weight_far = call(
@@ -300,7 +322,7 @@
         "source_terms",
     )(
         block_count, block_target, block_source, values,
-        grad_down2, grad_down1, grad_out, grad_up1, grad_up2,
+        grad_out, *arrived,
     )
     near = swapped(near, "col", 1)
     across = swapped(across, "col", 2)
@@ -324,9 +346,19 @@
     grad_inputs = call(last_kernel, [whole], [], LONG, [VMEM] * 4, "source_sum")(
         mine, near, across, far
     )[0]
-    grad_weight = call(
-        join_kernel, [jax.ShapeDtypeStruct((width, width), f32)], [], LONG, [VMEM] * 4, "weight_join"
-    )(*parts)[0]
+    grad_weight, bias_total, output, grad_inputs = call(
+        join_kernel,
+        [
+            jax.ShapeDtypeStruct((width, width), f32),
+            jax.ShapeDtypeStruct((1, width), f32),
+            whole,
+            whole,
+        ],
+        [],
+        LONG,
+        [VMEM] * 7,
+        "results",
+    )(*parts, bias_total, output, grad_inputs)
     return (output, grad_inputs, grad_weight, bias_total[0])
 
 

time: 54.4 us -> 52.7 us (0.969)
  Pallas kernels: 7.2 us -> 5.88 us
  starting transfers between devices: 26.9 us -> 26 us
  waiting for transfers between devices: 16.3 us -> 16.9 us
    all_to_all x1, starting transfers between devices: 6.07 us -> 3.55 us  [shards(): received = lax.all_to_all(message, 'row', 0, 0, tiled=True)]
    ppermute x8, starting transfers between devices: 12 us -> 13.6 us  [routed(): return lax.ppermute(block, 'row', pairs)]
    ppermute x12, waiting for transfers between devices: 3.28 us -> 4.84 us  [swapped(): return lax.ppermute(block, axis, [(i, i ^ bit) for i in range(size)])]
    all_to_all x1, waiting for transfers between devices: 4.97 us -> 3.58 us  [shards(): received = lax.all_to_all(message, 'row', 0, 0, tiled=True)]
    pallas_call x1, Pallas kernels: 0.79 us -> 0.13 us  [shards(): call(last_kernel, [whole], [], LONG, [VMEM] * 4, 'source_sum')]
  transfers between devices with their start and end apart: 21 -> 21, of which waited for: 9 -> 11; matrix products, arithmetic and copies ran while one was open for 0% -> 0% of each run, Pallas kernels for 7% -> 5%
where the time goes in v4:
time: 52.7 us; the launch traced here: 52.4 us
  starting transfers between devices  26 us (49%)
  waiting for transfers between devices  16.9 us (32%)
  Pallas kernels  5.88 us (11%)
  local copies, waits for them, and re-layouts  2.17 us (4%)
  between operations  1.45 us (3%)
    ppermute x8, starting transfers between devices, routed(): return lax.ppermute(block, 'row', pairs)  13.6 us
    ppermute x12, starting transfers between devices, swapped(): return lax.ppermute(block, axis, [(i, i ^ bit) for i in range(size)])  8.81 us
    ppermute x8, waiting for transfers between devices, routed(): return lax.ppermute(block, 'row', pairs)  8.48 us
    ppermute x12, waiting for transfers between devices, swapped(): return lax.ppermute(block, axis, [(i, i ^ bit) for i in range(size)])  4.84 us
    all_to_all x1, waiting for transfers between devices, shards(): received = lax.all_to_all(message, 'row', 0, 0, tiled=True)  3.58 us
    all_to_all x1, starting transfers between devices, shards(): received = lax.all_to_all(message, 'row', 0, 0, tiled=True)  3.55 us
    unnamed x22, local copies, waits for them, and re-layouts  2.17 us
    pallas_call x1, Pallas kernels, shards(): call(forward_kernel, [wide] + [whole] * 4, [pltpu.VMEM((sources, BLK, wid...  1.51 us
  transfers between devices with their start and end apart: 21, of which 11 were waited for; matrix products, arithmetic and copies ran while one was open for 0% of the time, Pallas kernels for 5%

profile of v4, /device:TPU:0, one launch (start us, length us, event | category | flops | bytes accessed | tf_op | source)
XLA Modules:
  0.0 52.4 jit_solution(385928741797896295)
XLA Ops:
  0.6 3.0 %collective-permute-start.1 = (bf16[256,256]{1,0:T(8,128)(2,1)}, bf16[256,256]{1,0:T(8,128)(2,1)S(1)}, u32[]{:S(2)}, u32[]{:S(2)}) collective-permute-start(bf16[256,256]{1,0:T(8,128)(2,1)} %own.1), channel_id=1, source_target_pairs={{0,2},{1,3},{2,0},{3,1},{4,6},{5,7},{6,4},{7,5},{8,10},{9,11},{10,... | collective-permute-start | bytes 393224 | tf_op jit(solution)/shard_map/ppermute | solution.py:46
  3.7 1.2 %copy-done.8 = bf16[1,1,32,128,128]{4,3,2,1,0:T(8,128)(2,1)S(1)} copy-done((bf16[1,1,32,128,128]{4,3,2,1,0:T(8,128)(2,1)S(1)}, bf16[1,1,32,128,128]{4,3,2,1,0:T(8,128)(2,1)}, u32[]{:S(2)}) %copy-start.8) | copy-done | bytes 1048600
  4.9 0.9 %copy-done.9 = bf16[256,256]{1,0:T(8,128)(2,1)S(1)} copy-done((bf16[256,256]{1,0:T(8,128)(2,1)S(1)}, bf16[256,256]{1,0:T(8,128)(2,1)}, u32[]{:S(2)}) %copy-start.9) | copy-done | bytes 131096
  6.7 0.6 %collective-permute-done.1.across = bf16[256,256]{1,0:T(8,128)(2,1)S(1)} collective-permute-done((bf16[256,256]{1,0:T(8,128)(2,1)}, bf16[256,256]{1,0:T(8,128)(2,1)S(1)}, u32[]{:S(2)}, u32[]{:S(2)}) %collective-permute-start.1) | collective-permute-done | bytes 131104 | tf_op jit(solution)/shard_map/ppermute | solution.py:46
  7.4 1.3 %collective-permute-done.2.far = bf16[256,256]{1,0:T(8,128)(2,1)S(1)} collective-permute-done((bf16[256,256]{1,0:T(8,128)(2,1)S(1)}, bf16[256,256]{1,0:T(8,128)(2,1)S(1)}, u32[]{:S(2)}, u32[]{:S(2)}) %collective-permute-start.2) | collective-permute-done | bytes 131104 | tf_op jit(solution)/shard_map/ppermute | solution.py:46
  8.7 1.5 %aggregate_terms.1 = (f32[256,256]{1,0:T(8,128)S(1)}, bf16[256,256]{1,0:T(8,128)(2,1)S(1)}, bf16[256,256]{1,0:T(8,128)(2,1)S(1)}, bf16[256,256]{1,0:T(8,128)(2,1)S(1)}, bf16[256,256]{1,0:T(8,128)(2,1)S(1)}) custom-call(s32[1,1]{1,0:T(1,128)S(6)} %copy.12.count, s32[1,1,32]{2,1,0:T(1,128)S(1)} %copy-done.4, s32[1,1,32]{2,1,0:T(1,128)S(1)} %copy-done.6, ...), custom_call_target="tpu_custom_call" | custom-call | flops 268435456 | bytes 1048576 | tf_op jit(solution)/shard_map/aggregate_terms/pallas_call | solution.py:266
  10.3 1.9 %collective-permute-start.3 = (bf16[256,256]{1,0:T(8,128)(2,1)S(1)}, bf16[256,256]{1,0:T(8,128)(2,1)S(1)}, u32[]{:S(2)}, u32[]{:S(2)}) collective-permute-start(bf16[256,256]{1,0:T(8,128)(2,1)S(1)} %get-tuple-element.34), channel_id=1, source_target_pairs={{0,8},{4,12},{8,16},{12,20},{16,24},{20,28},{24,0},{28,4},{1,9},{5... | collective-permute-start | bytes 393224 | tf_op jit(solution)/shard_map/ppermute | solution.py:41
  12.1 1.5 %collective-permute-start.4 = (bf16[256,256]{1,0:T(8,128)(2,1)S(1)}, bf16[256,256]{1,0:T(8,128)(2,1)S(1)}, u32[]{:S(2)}, u32[]{:S(2)}) collective-permute-start(bf16[256,256]{1,0:T(8,128)(2,1)S(1)} %get-tuple-element.35), channel_id=1, source_target_pairs={{0,4},{4,8},{8,12},{12,16},{16,20},{20,24},{24,28},{28,0},{1,5},{5... | collective-permute-start | bytes 393224 | tf_op jit(solution)/shard_map/ppermute | solution.py:41
  13.7 2.2 %collective-permute-start.5 = (bf16[256,256]{1,0:T(8,128)(2,1)S(1)}, bf16[256,256]{1,0:T(8,128)(2,1)S(1)}, u32[]{:S(2)}, u32[]{:S(2)}) collective-permute-start(bf16[256,256]{1,0:T(8,128)(2,1)S(1)} %get-tuple-element.36), channel_id=1, source_target_pairs={{0,24},{4,28},{8,0},{12,4},{16,8},{20,12},{24,16},{28,20},{1,25},{... | collective-permute-start | bytes 393224 | tf_op jit(solution)/shard_map/ppermute | solution.py:41
  15.9 1.2 %collective-permute-start.6 = (bf16[256,256]{1,0:T(8,128)(2,1)S(1)}, bf16[256,256]{1,0:T(8,128)(2,1)S(1)}, u32[]{:S(2)}, u32[]{:S(2)}) collective-permute-start(bf16[256,256]{1,0:T(8,128)(2,1)S(1)} %get-tuple-element.37), channel_id=1, source_target_pairs={{0,28},{4,0},{8,4},{12,8},{16,12},{20,16},{24,20},{28,24},{1,29},{... | collective-permute-start | bytes 393224 | tf_op jit(solution)/shard_map/ppermute | solution.py:41
  17.2 1.0 %collective-permute-done.3.first = bf16[256,256]{1,0:T(8,128)(2,1)S(1)} collective-permute-done((bf16[256,256]{1,0:T(8,128)(2,1)S(1)}, bf16[256,256]{1,0:T(8,128)(2,1)S(1)}, u32[]{:S(2)}, u32[]{:S(2)}) %collective-permute-start.3) | collective-permute-done | bytes 131104 | tf_op jit(solution)/shard_map/ppermute | solution.py:41
  18.1 4.4 %collective-permute-done.4.second = bf16[256,256]{1,0:T(8,128)(2,1)S(1)} collective-permute-done((bf16[256,256]{1,0:T(8,128)(2,1)S(1)}, bf16[256,256]{1,0:T(8,128)(2,1)S(1)}, u32[]{:S(2)}, u32[]{:S(2)}) %collective-permute-start.4) | collective-permute-done | bytes 131104 | tf_op jit(solution)/shard_map/ppermute | solution.py:41
  22.5 1.0 %collective-permute-done.6.fourth = bf16[256,256]{1,0:T(8,128)(2,1)S(1)} collective-permute-done((bf16[256,256]{1,0:T(8,128)(2,1)S(1)}, bf16[256,256]{1,0:T(8,128)(2,1)S(1)}, u32[]{:S(2)}, u32[]{:S(2)}) %collective-permute-start.6) | collective-permute-done | bytes 131104 | tf_op jit(solution)/shard_map/ppermute | solution.py:41
  23.5 0.6 %pointwise.1 = (bf16[256,256]{1,0:T(8,128)(2,1)S(1)}, bf16[256,256]{1,0:T(8,128)(2,1)S(1)}, bf16[256,256]{1,0:T(8,128)(2,1)S(1)}, bf16[256,256]{1,0:T(8,128)(2,1)S(1)}, f32[1,256]{1,0:T(1,128)S(1)}) custom-call(f32[256,256]{1,0:T(8,128)S(1)} %get-tuple-element.33.mine, bf16[256,256]{1,0:T(8,128)(2,1)S(1)} %collective-permute-done.3.first, ...), custom_call_target="tpu_custom_call" | custom-call | flops 100663296 | bytes 1048576 | tf_op jit(solution)/shard_map/pointwise/pallas_call | solution.py:280
  24.5 1.6 %collective-permute-start.8 = (bf16[72,256]{1,0:T(8,128)(2,1)S(1)}, bf16[72,256]{1,0:T(8,128)(2,1)S(1)}, u32[]{:S(2)}, u32[]{:S(2)}) collective-permute-start(bf16[72,256]{1,0:T(8,128)(2,1)S(1)} %get-tuple-element.44), channel_id=1, source_target_pairs={{0,2},{1,3},{2,0},{3,1},{4,6},{5,7},{6,4},{7,5},{8,10},{9,11},{10,... | collective-permute-start | bytes 110600 | tf_op jit(solution)/shard_map/ppermute | solution.py:46
  26.0 0.3 collective-permute-start.9
  26.3 2.1 %collective-permute-start.11 = (bf16[256,256]{1,0:T(8,128)(2,1)S(1)}, bf16[256,256]{1,0:T(8,128)(2,1)S(1)}, u32[]{:S(2)}, u32[]{:S(2)}) collective-permute-start(bf16[256,256]{1,0:T(8,128)(2,1)S(1)} %get-tuple-element.46.local), channel_id=1, source_target_pairs={{0,4},{4,8},{8,12},{12,16},{16,20},{20,24},{24,28},{28,0},{1,5},{5... | collective-permute-start | bytes 393224 | tf_op jit(solution)/shard_map/ppermute | solution.py:41
  28.5 3.3 %collective-permute-start.12 = (bf16[256,256]{1,0:T(8,128)(2,1)S(1)}, bf16[256,256]{1,0:T(8,128)(2,1)S(1)}, u32[]{:S(2)}, u32[]{:S(2)}) collective-permute-start(bf16[256,256]{1,0:T(8,128)(2,1)S(1)} %get-tuple-element.46.local), channel_id=1, source_target_pairs={{0,24},{4,28},{8,0},{12,4},{16,8},{20,12},{24,16},{28,20},{1,25},{... | collective-permute-start | bytes 393224 | tf_op jit(solution)/shard_map/ppermute | solution.py:41
  31.7 1.4 %collective-permute-start.13 = (bf16[256,256]{1,0:T(8,128)(2,1)S(1)}, bf16[256,256]{1,0:T(8,128)(2,1)S(1)}, u32[]{:S(2)}, u32[]{:S(2)}) collective-permute-start(bf16[256,256]{1,0:T(8,128)(2,1)S(1)} %get-tuple-element.46.local), channel_id=1, source_target_pairs={{0,28},{4,0},{8,4},{12,8},{16,12},{20,16},{24,20},{28,24},{1,29},{... | collective-permute-start | bytes 393224 | tf_op jit(solution)/shard_map/ppermute | solution.py:41
  33.1 0.7 %weight_column_sum.1 = bf16[8,72,256]{2,1,0:T(8,128)(2,1)} custom-call(f32[72,256]{1,0:T(8,128)S(1)} %get-tuple-element.42.mine, bf16[72,256]{1,0:T(8,128)(2,1)S(1)} %collective-permute-done.7.near, bf16[72,256]{1,0:T(8,128)(2,1)S(1)} %collective-permute-done.8.across, bf16[72,256]{1,0:T(8,128)(2,1)S(1)} %collective-permute-done.9.far), custom_call_target="tpu_custom_call" | custom-call | flops 99999997952 | bytes 1048576 | tf_op jit(solution)/shard_map/weight_column_sum/pallas_call | solution.py:300
  33.8 3.6 %all-to-all-start = ((bf16[8,72,256]{2,1,0:T(8,128)(2,1)}), bf16[8,72,256]{2,1,0:T(8,128)(2,1)S(1)}, u32[]{:S(2)}, u32[]{:S(2)}) async-start(bf16[8,72,256]{2,1,0:T(8,128)(2,1)} %weight_column_sum.1), calls=%async_computation | async-start | bytes 589824 | tf_op jit(solution)/shard_map/all_to_all | solution.py:335
  37.4 0.9 %collective-permute-done.11.second = bf16[256,256]{1,0:T(8,128)(2,1)S(1)} collective-permute-done((bf16[256,256]{1,0:T(8,128)(2,1)S(1)}, bf16[256,256]{1,0:T(8,128)(2,1)S(1)}, u32[]{:S(2)}, u32[]{:S(2)}) %collective-permute-start.11) | collective-permute-done | bytes 131104 | tf_op jit(solution)/shard_map/ppermute | solution.py:41
  38.3 1.2 %collective-permute-done.13.fourth = bf16[256,256]{1,0:T(8,128)(2,1)S(1)} collective-permute-done((bf16[256,256]{1,0:T(8,128)(2,1)S(1)}, bf16[256,256]{1,0:T(8,128)(2,1)S(1)}, u32[]{:S(2)}, u32[]{:S(2)}) %collective-permute-start.13) | collective-permute-done | bytes 131104 | tf_op jit(solution)/shard_map/ppermute | solution.py:41
  39.5 1.5 %source_terms.1 = (f32[256,256]{1,0:T(8,128)S(1)}, bf16[256,256]{1,0:T(8,128)(2,1)S(1)}, bf16[256,256]{1,0:T(8,128)(2,1)S(1)}, bf16[256,256]{1,0:T(8,128)(2,1)S(1)}) custom-call(s32[1,1]{1,0:T(1,128)S(6)} %copy.12.count, s32[1,1,32]{2,1,0:T(1,128)S(1)} %copy-done.5, s32[1,1,32]{2,1,0:T(1,128)S(1)} %copy-done.7, bf16[1,1,32,128,128]{4,3,2,1,0:T(8,128)(2,1)S(1)} %copy-done.1, ...), custom_call_target="tpu_custom_call" | custom-call | flops 99999997952 | bytes 1048576 | tf_op jit(solution)/shard_map/source_terms/pallas_call | solution.py:313
  41.1 1.6 %collective-permute-start.18 = (bf16[256,256]{1,0:T(8,128)(2,1)S(1)}, bf16[256,256]{1,0:T(8,128)(2,1)S(1)}, u32[]{:S(2)}, u32[]{:S(2)}) collective-permute-start(bf16[256,256]{1,0:T(8,128)(2,1)S(1)} %get-tuple-element.52), channel_id=1, source_target_pairs={{0,2},{1,3},{2,0},{3,1},{4,6},{5,7},{6,4},{7,5},{8,10},{9,11},{10,... | collective-permute-start | bytes 393224 | tf_op jit(solution)/shard_map/ppermute | solution.py:46
  43.0 3.6 %all-to-all-done.received = bf16[8,72,256]{2,1,0:T(8,128)(2,1)S(1)} async-done(((bf16[8,72,256]{2,1,0:T(8,128)(2,1)}), bf16[8,72,256]{2,1,0:T(8,128)(2,1)S(1)}, u32[]{:S(2)}, u32[]{:S(2)}) %all-to-all-start) | async-done | bytes 294944 | tf_op jit(solution)/shard_map/all_to_all | solution.py:335
  46.7 1.6 %collective-permute-start.15 = (bf16[64,256]{1,0:T(8,128)(2,1)S(1)}, bf16[64,256]{1,0:T(8,128)(2,1)S(1)}, u32[]{:S(2)}, u32[]{:S(2)}) collective-permute-start(bf16[64,256]{1,0:T(8,128)(2,1)S(1)} %get-tuple-element.48.own), channel_id=1, source_target_pairs={{0,2},{1,3},{2,0},{3,1},{4,6},{5,7},{6,4},{7,5},{8,10},{9,11},{10,... | collective-permute-start | bytes 98312 | tf_op jit(solution)/shard_map/ppermute | solution.py:46
  48.2 0.3 collective-permute-start.16
  48.6 0.8 %collective-permute-done.19.far = bf16[256,256]{1,0:T(8,128)(2,1)S(1)} collective-permute-done((bf16[256,256]{1,0:T(8,128)(2,1)S(1)}, bf16[256,256]{1,0:T(8,128)(2,1)S(1)}, u32[]{:S(2)}, u32[]{:S(2)}) %collective-permute-start.19) | collective-permute-done | bytes 131104 | tf_op jit(solution)/shard_map/ppermute | solution.py:46
  49.5 1.1 %collective-permute-done.15.across = bf16[64,256]{1,0:T(8,128)(2,1)S(1)} collective-permute-done((bf16[64,256]{1,0:T(8,128)(2,1)S(1)}, bf16[64,256]{1,0:T(8,128)(2,1)S(1)}, u32[]{:S(2)}, u32[]{:S(2)}) %collective-permute-start.15) | collective-permute-done | bytes 32800 | tf_op jit(solution)/shard_map/ppermute | solution.py:46
  50.7 0.9 %collective-permute-done.16.far = bf16[64,256]{1,0:T(8,128)(2,1)S(1)} collective-permute-done((bf16[64,256]{1,0:T(8,128)(2,1)S(1)}, bf16[64,256]{1,0:T(8,128)(2,1)S(1)}, u32[]{:S(2)}, u32[]{:S(2)}) %collective-permute-start.16) | collective-permute-done | bytes 32800 | tf_op jit(solution)/shard_map/ppermute | solution.py:46
  51.6 0.8 %results.1 = (f32[256,256]{1,0:T(8,128)}, f32[1,256]{1,0:T(1,128)}, bf16[256,256]{1,0:T(8,128)(2,1)}, bf16[256,256]{1,0:T(8,128)(2,1)}) custom-call(bf16[64,256]{1,0:T(8,128)(2,1)S(1)} %get-tuple-element.48.own, bf16[64,256]{1,0:T(8,128)(2,1)S(1)} %collective-permute-done.14.near, bf16[64,256]{1,0:T(8,128)(2,1)S(1)} %collective-permute-done.15.across, ...), custom_call_target="tpu_custom_call" | custom-call | flops 99999997952 | bytes 1048576 | tf_op jit(solution)/shard_map/results/pallas_call | solution.py:349
  (42 shorter events, 1.3 us)
Async XLA Ops:
  0.6 3.0 %copy-start.10 = (f32[256]{0:T(256)S(1)}, f32[256]{0:T(256)}, u32[]{:S(2)}) copy-start(f32[256]{0:T(256)} %param.10) | copy-start | bytes 3076
  0.6 6.7 %collective-permute-start.1 = (bf16[256,256]{1,0:T(8,128)(2,1)}, bf16[256,256]{1,0:T(8,128)(2,1)S(1)}, u32[]{:S(2)}, u32[]{:S(2)}) collective-permute-start(bf16[256,256]{1,0:T(8,128)(2,1)} %own.1), channel_id=1, source_target_pairs={{0,2},{1,3},{2,0},{3,1},{4,6},{5,7},{6,4},{7,5},{8,10},{9,11},{10,... | collective-permute-start | bytes 393224 | tf_op jit(solution)/shard_map/ppermute | solution.py:46
  3.6 3.7 %collective-permute-start = (bf16[256,256]{1,0:T(8,128)(2,1)}, bf16[256,256]{1,0:T(8,128)(2,1)S(1)}, u32[]{:S(2)}, u32[]{:S(2)}) collective-permute-start(bf16[256,256]{1,0:T(8,128)(2,1)} %own.1), channel_id=1, source_target_pairs={{0,1},{1,0},{2,3},{3,2},{4,5},{5,4},{6,7},{7,6},{8,9},{9,8},{10,11... | collective-permute-start | bytes 393224 | tf_op jit(solution)/shard_map/ppermute | solution.py:46
  3.7 1.2 %copy-start.8 = (bf16[1,1,32,128,128]{4,3,2,1,0:T(8,128)(2,1)S(1)}, bf16[1,1,32,128,128]{4,3,2,1,0:T(8,128)(2,1)}, u32[]{:S(2)}) copy-start(bf16[1,1,32,128,128]{4,3,2,1,0:T(8,128)(2,1)} %values.1) | copy-start | bytes 3145732
  4.9 0.9 %copy-start.9 = (bf16[256,256]{1,0:T(8,128)(2,1)S(1)}, bf16[256,256]{1,0:T(8,128)(2,1)}, u32[]{:S(2)}) copy-start(bf16[256,256]{1,0:T(8,128)(2,1)} %own.1) | copy-start | bytes 393220
  6.1 2.6 %copy-start = (bf16[1,1,32,128,128]{4,3,2,1,0:T(8,128)(2,1)}, bf16[1,1,32,128,128]{4,3,2,1,0:T(8,128)(2,1)S(1)}, u32[]{:S(2)}) copy-start(bf16[1,1,32,128,128]{4,3,2,1,0:T(8,128)(2,1)S(1)} %get-tuple-element.31.values) | copy-start | bytes 3145732
  7.4 1.3 %collective-permute-start.2 = (bf16[256,256]{1,0:T(8,128)(2,1)S(1)}, bf16[256,256]{1,0:T(8,128)(2,1)S(1)}, u32[]{:S(2)}, u32[]{:S(2)}) collective-permute-start(bf16[256,256]{1,0:T(8,128)(2,1)S(1)} %collective-permute-done.1.across), channel_id=1, source_target_pairs={{0,1},{1,0},{2,3},{3,2},{4,5},{5,4},{6,7},{7,6},{8,9},{9,8},{10,11... | collective-permute-start | bytes 393224 | tf_op jit(solution)/shard_map/ppermute | solution.py:46
  7.4 1.3 %copy-start.4 = (s32[1,1,32]{2,1,0:T(1,128)S(1)}, s32[1,1,32]{2,1,0:T(1,128)}, u32[]{:S(2)}) copy-start(s32[1,1,32]{2,1,0:T(1,128)} %target.3) | copy-start | bytes 388
  7.4 1.3 %copy-start.6 = (s32[1,1,32]{2,1,0:T(1,128)S(1)}, s32[1,1,32]{2,1,0:T(1,128)}, u32[]{:S(2)}) copy-start(s32[1,1,32]{2,1,0:T(1,128)} %source.3) | copy-start | bytes 388
  8.7 14.8 %copy-start.2 = (bf16[256,256]{1,0:T(8,128)(2,1)S(1)}, bf16[256,256]{1,0:T(8,128)(2,1)}, u32[]{:S(2)}) copy-start(bf16[256,256]{1,0:T(8,128)(2,1)} %weight.1) | copy-start | bytes 393220
  8.7 14.8 %copy-start.3 = (bf16[256,256]{1,0:T(8,128)(2,1)S(1)}, bf16[256,256]{1,0:T(8,128)(2,1)}, u32[]{:S(2)}) copy-start(bf16[256,256]{1,0:T(8,128)(2,1)} %cotangent.1) | copy-start | bytes 393220
  10.3 7.9 %collective-permute-start.3 = (bf16[256,256]{1,0:T(8,128)(2,1)S(1)}, bf16[256,256]{1,0:T(8,128)(2,1)S(1)}, u32[]{:S(2)}, u32[]{:S(2)}) collective-permute-start(bf16[256,256]{1,0:T(8,128)(2,1)S(1)} %get-tuple-element.34), channel_id=1, source_target_pairs={{0,8},{4,12},{8,16},{12,20},{16,24},{20,28},{24,0},{28,4},{1,9},{5... | collective-permute-start | bytes 393224 | tf_op jit(solution)/shard_map/ppermute | solution.py:41
  12.1 10.4 %collective-permute-start.4 = (bf16[256,256]{1,0:T(8,128)(2,1)S(1)}, bf16[256,256]{1,0:T(8,128)(2,1)S(1)}, u32[]{:S(2)}, u32[]{:S(2)}) collective-permute-start(bf16[256,256]{1,0:T(8,128)(2,1)S(1)} %get-tuple-element.35), channel_id=1, source_target_pairs={{0,4},{4,8},{8,12},{12,16},{16,20},{20,24},{24,28},{28,0},{1,5},{5... | collective-permute-start | bytes 393224 | tf_op jit(solution)/shard_map/ppermute | solution.py:41
  13.7 8.8 %collective-permute-start.5 = (bf16[256,256]{1,0:T(8,128)(2,1)S(1)}, bf16[256,256]{1,0:T(8,128)(2,1)S(1)}, u32[]{:S(2)}, u32[]{:S(2)}) collective-permute-start(bf16[256,256]{1,0:T(8,128)(2,1)S(1)} %get-tuple-element.36), channel_id=1, source_target_pairs={{0,24},{4,28},{8,0},{12,4},{16,8},{20,12},{24,16},{28,20},{1,25},{... | collective-permute-start | bytes 393224 | tf_op jit(solution)/shard_map/ppermute | solution.py:41
  15.9 7.6 %collective-permute-start.6 = (bf16[256,256]{1,0:T(8,128)(2,1)S(1)}, bf16[256,256]{1,0:T(8,128)(2,1)S(1)}, u32[]{:S(2)}, u32[]{:S(2)}) collective-permute-start(bf16[256,256]{1,0:T(8,128)(2,1)S(1)} %get-tuple-element.37), channel_id=1, source_target_pairs={{0,28},{4,0},{8,4},{12,8},{16,12},{20,16},{24,20},{28,24},{1,29},{... | collective-permute-start | bytes 393224 | tf_op jit(solution)/shard_map/ppermute | solution.py:41
  24.4 4.1 %collective-permute-start.7 = (bf16[72,256]{1,0:T(8,128)(2,1)S(1)}, bf16[72,256]{1,0:T(8,128)(2,1)S(1)}, u32[]{:S(2)}, u32[]{:S(2)}) collective-permute-start(bf16[72,256]{1,0:T(8,128)(2,1)S(1)} %get-tuple-element.43), channel_id=1, source_target_pairs={{0,1},{1,0},{2,3},{3,2},{4,5},{5,4},{6,7},{7,6},{8,9},{9,8},{10,11... | collective-permute-start | bytes 110600 | tf_op jit(solution)/shard_map/ppermute | solution.py:46
  24.5 7.3 %collective-permute-start.8 = (bf16[72,256]{1,0:T(8,128)(2,1)S(1)}, bf16[72,256]{1,0:T(8,128)(2,1)S(1)}, u32[]{:S(2)}, u32[]{:S(2)}) collective-permute-start(bf16[72,256]{1,0:T(8,128)(2,1)S(1)} %get-tuple-element.44), channel_id=1, source_target_pairs={{0,2},{1,3},{2,0},{3,1},{4,6},{5,7},{6,4},{7,5},{8,10},{9,11},{10,... | collective-permute-start | bytes 110600 | tf_op jit(solution)/shard_map/ppermute | solution.py:46
  26.0 7.1 %collective-permute-start.9 = (bf16[72,256]{1,0:T(8,128)(2,1)S(1)}, bf16[72,256]{1,0:T(8,128)(2,1)S(1)}, u32[]{:S(2)}, u32[]{:S(2)}) collective-permute-start(bf16[72,256]{1,0:T(8,128)(2,1)S(1)} %get-tuple-element.45), channel_id=1, source_target_pairs={{0,3},{1,2},{2,1},{3,0},{4,7},{5,6},{6,5},{7,4},{8,11},{9,10},{10,... | collective-permute-start | bytes 110600 | tf_op jit(solution)/shard_map/ppermute | solution.py:46
  26.3 11.1 %collective-permute-start.10 = (bf16[256,256]{1,0:T(8,128)(2,1)S(1)}, bf16[256,256]{1,0:T(8,128)(2,1)S(1)}, u32[]{:S(2)}, u32[]{:S(2)}) collective-permute-start(bf16[256,256]{1,0:T(8,128)(2,1)S(1)} %get-tuple-element.46.local), channel_id=1, source_target_pairs={{0,8},{4,12},{8,16},{12,20},{16,24},{20,28},{24,0},{28,4},{1,9},{5... | collective-permute-start | bytes 393224 | tf_op jit(solution)/shard_map/ppermute | solution.py:41
  26.3 12.0 %collective-permute-start.11 = (bf16[256,256]{1,0:T(8,128)(2,1)S(1)}, bf16[256,256]{1,0:T(8,128)(2,1)S(1)}, u32[]{:S(2)}, u32[]{:S(2)}) collective-permute-start(bf16[256,256]{1,0:T(8,128)(2,1)S(1)} %get-tuple-element.46.local), channel_id=1, source_target_pairs={{0,4},{4,8},{8,12},{12,16},{16,20},{20,24},{24,28},{28,0},{1,5},{5... | collective-permute-start | bytes 393224 | tf_op jit(solution)/shard_map/ppermute | solution.py:41
  28.5 9.8 %collective-permute-start.12 = (bf16[256,256]{1,0:T(8,128)(2,1)S(1)}, bf16[256,256]{1,0:T(8,128)(2,1)S(1)}, u32[]{:S(2)}, u32[]{:S(2)}) collective-permute-start(bf16[256,256]{1,0:T(8,128)(2,1)S(1)} %get-tuple-element.46.local), channel_id=1, source_target_pairs={{0,24},{4,28},{8,0},{12,4},{16,8},{20,12},{24,16},{28,20},{1,25},{... | collective-permute-start | bytes 393224 | tf_op jit(solution)/shard_map/ppermute | solution.py:41
  31.7 7.8 %collective-permute-start.13 = (bf16[256,256]{1,0:T(8,128)(2,1)S(1)}, bf16[256,256]{1,0:T(8,128)(2,1)S(1)}, u32[]{:S(2)}, u32[]{:S(2)}) collective-permute-start(bf16[256,256]{1,0:T(8,128)(2,1)S(1)} %get-tuple-element.46.local), channel_id=1, source_target_pairs={{0,28},{4,0},{8,4},{12,8},{16,12},{20,16},{24,20},{28,24},{1,29},{... | collective-permute-start | bytes 393224 | tf_op jit(solution)/shard_map/ppermute | solution.py:41
  33.1 6.4 %copy-start.1 = (bf16[1,1,32,128,128]{4,3,2,1,0:T(8,128)(2,1)S(1)}, bf16[1,1,32,128,128]{4,3,2,1,0:T(8,128)(2,1)}, u32[]{:S(2)}) copy-start(bf16[1,1,32,128,128]{4,3,2,1,0:T(8,128)(2,1)} %copy-done) | copy-start | bytes 3145732
  33.8 5.7 %copy-start.5 = (s32[1,1,32]{2,1,0:T(1,128)S(1)}, s32[1,1,32]{2,1,0:T(1,128)}, u32[]{:S(2)}) copy-start(s32[1,1,32]{2,1,0:T(1,128)} %target.3) | copy-start | bytes 388
  33.8 5.7 %copy-start.7 = (s32[1,1,32]{2,1,0:T(1,128)S(1)}, s32[1,1,32]{2,1,0:T(1,128)}, u32[]{:S(2)}) copy-start(s32[1,1,32]{2,1,0:T(1,128)} %source.3) | copy-start | bytes 388
  33.8 12.7 %all-to-all-start = ((bf16[8,72,256]{2,1,0:T(8,128)(2,1)}), bf16[8,72,256]{2,1,0:T(8,128)(2,1)S(1)}, u32[]{:S(2)}, u32[]{:S(2)}) async-start(bf16[8,72,256]{2,1,0:T(8,128)(2,1)} %weight_column_sum.1), calls=%async_computation | async-start | bytes 589824 | tf_op jit(solution)/shard_map/all_to_all | solution.py:335
  41.0 7.2 %collective-permute-start.17 = (bf16[256,256]{1,0:T(8,128)(2,1)S(1)}, bf16[256,256]{1,0:T(8,128)(2,1)S(1)}, u32[]{:S(2)}, u32[]{:S(2)}) collective-permute-start(bf16[256,256]{1,0:T(8,128)(2,1)S(1)} %get-tuple-element.51), channel_id=1, source_target_pairs={{0,1},{1,0},{2,3},{3,2},{4,5},{5,4},{6,7},{7,6},{8,9},{9,8},{10,11... | collective-permute-start | bytes 393224 | tf_op jit(solution)/shard_map/ppermute | solution.py:46
  41.1 7.4 %collective-permute-start.18 = (bf16[256,256]{1,0:T(8,128)(2,1)S(1)}, bf16[256,256]{1,0:T(8,128)(2,1)S(1)}, u32[]{:S(2)}, u32[]{:S(2)}) collective-permute-start(bf16[256,256]{1,0:T(8,128)(2,1)S(1)} %get-tuple-element.52), channel_id=1, source_target_pairs={{0,2},{1,3},{2,0},{3,1},{4,6},{5,7},{6,4},{7,5},{8,10},{9,11},{10,... | collective-permute-start | bytes 393224 | tf_op jit(solution)/shard_map/ppermute | solution.py:46
  42.7 6.7 %collective-permute-start.19 = (bf16[256,256]{1,0:T(8,128)(2,1)S(1)}, bf16[256,256]{1,0:T(8,128)(2,1)S(1)}, u32[]{:S(2)}, u32[]{:S(2)}) collective-permute-start(bf16[256,256]{1,0:T(8,128)(2,1)S(1)} %get-tuple-element.53), channel_id=1, source_target_pairs={{0,3},{1,2},{2,1},{3,0},{4,7},{5,6},{6,5},{7,4},{8,11},{9,10},{10,... | collective-permute-start | bytes 393224 | tf_op jit(solution)/shard_map/ppermute | solution.py:46
  46.6 2.9 %collective-permute-start.14 = (bf16[64,256]{1,0:T(8,128)(2,1)S(1)}, bf16[64,256]{1,0:T(8,128)(2,1)S(1)}, u32[]{:S(2)}, u32[]{:S(2)}) collective-permute-start(bf16[64,256]{1,0:T(8,128)(2,1)S(1)} %get-tuple-element.48.own), channel_id=1, source_target_pairs={{0,1},{1,0},{2,3},{3,2},{4,5},{5,4},{6,7},{7,6},{8,9},{9,8},{10,11... | collective-permute-start | bytes 98312 | tf_op jit(solution)/shard_map/ppermute | solution.py:46
  46.7 4.0 %collective-permute-start.15 = (bf16[64,256]{1,0:T(8,128)(2,1)S(1)}, bf16[64,256]{1,0:T(8,128)(2,1)S(1)}, u32[]{:S(2)}, u32[]{:S(2)}) collective-permute-start(bf16[64,256]{1,0:T(8,128)(2,1)S(1)} %get-tuple-element.48.own), channel_id=1, source_target_pairs={{0,2},{1,3},{2,0},{3,1},{4,6},{5,7},{6,4},{7,5},{8,10},{9,11},{10,... | collective-permute-start | bytes 98312 | tf_op jit(solution)/shard_map/ppermute | solution.py:46
  48.2 3.3 %collective-permute-start.16 = (bf16[64,256]{1,0:T(8,128)(2,1)S(1)}, bf16[64,256]{1,0:T(8,128)(2,1)S(1)}, u32[]{:S(2)}, u32[]{:S(2)}) collective-permute-start(bf16[64,256]{1,0:T(8,128)(2,1)S(1)} %get-tuple-element.48.own), channel_id=1, source_target_pairs={{0,3},{1,2},{2,1},{3,0},{4,7},{5,6},{6,5},{7,4},{8,11},{9,10},{10,... | collective-permute-start | bytes 98312 | tf_op jit(solution)/shard_map/ppermute | solution.py:46

commit v5 on v4

--- a/solution.py
+++ b/solution.py
@@ -14,7 +14,7 @@
 SPAN = 2 * HALF + 1
 TAIL = 8
 FORWARD = ((2, None), (1, None), (-2, None), (-1, None))
-BACKWARD = ((2, None), (1, None), (-2, None), (-1, None))
+BACKWARD = ((-2, None), (-1, None), (1, None), (2, None))
 SLOT_GROUP = 32
 LONG = 10**11
 VMEM = pltpu.VMEM
@@ -174,7 +174,7 @@
 
 def backward_kernel(
     count, target, source, values, local, first, second, third, fourth,
-    mine, near, across, far, table, totals,
+    mine, across, leaving, table, totals,
 ):
     column = lax.axis_index("col")
     live = count[0, 0]
@@ -192,11 +192,17 @@
         )
 
     for_slots(values.shape[2], live, step)
-    for relative, out in enumerate((mine, near, across, far)):
+    outs = (mine, leaving.at[0], across, leaving.at[1])
+    for relative, out in enumerate(outs):
         for block in range(VB):
             out[:, block * BLK : (block + 1) * BLK] = totals[
                 (column ^ relative) * VB + block
             ].astype(out.dtype)
+
+
+def source_pair_kernel(mine, across, arrived, kept, leaving):
+    kept[...] = mine[...] + arrived[0].astype(jnp.float32)
+    leaving[...] = (across[...] + arrived[1].astype(jnp.float32)).astype(leaving.dtype)
 
 
 def row_sum_kernel(scale, received, after, part, bias_out):
@@ -207,24 +213,19 @@
     bias_out[...] = total[share : share + 1] + total[share + 1 : share + 2]
 
 
-def last_kernel(mine, near, across, far, grad_inputs):
-    total = mine[...]
-    for part in (near, across, far):
-        total = total + part[...].astype(jnp.float32)
+def last_kernel(mine, arrived, output_in, bias_in, grad_inputs, output, bias_out):
+    total = mine[...] + arrived[...].astype(jnp.float32)
     grad_inputs[...] = total.T.astype(jnp.bfloat16)
-
-
-def join_kernel(
-    own, near, across, far, bias_in, output_in, source_in, grad_weight, bias_out, output, grad_inputs
-):
+    output[...] = output_in[...]
+    bias_out[...] = bias_in[...]
+
+
+def join_kernel(own, near, across, far, grad_weight):
     column = lax.axis_index("col")
     share = own.shape[0]
     for relative, part in enumerate((own, near, across, far)):
         start = pl.multiple_of((column ^ relative) * share, share)
         grad_weight[pl.ds(start, share), :] = part[...].astype(jnp.float32)
-    bias_out[...] = bias_in[...]
-    output[...] = output_in[...]
-    grad_inputs[...] = source_in[...]
 
 
 def shards(
@@ -310,9 +311,10 @@
         swapped(weight_across, "col", 2),
         swapped(weight_far, "col", 3),
     )[0]
-    mine, near, across, far = call(
+    tall = jax.ShapeDtypeStruct((width, own_rows), f32)
+    mine, across, leaving = call(
         backward_kernel,
-        [jax.ShapeDtypeStruct((width, own_rows), f32)] + [flipped] * 3,
+        [tall, tall, jax.ShapeDtypeStruct((2, width, own_rows), bf16)],
         [
             pltpu.VMEM((SPAN * VB, width, BLK), bf16),
             pltpu.VMEM((sources + 1, width, BLK), f32),
@@ -324,9 +326,10 @@
         block_count, block_target, block_source, values,
         grad_out, *arrived,
     )
-    near = swapped(near, "col", 1)
-    across = swapped(across, "col", 2)
-    far = swapped(far, "col", 3)
+    kept, leaving = call(
+        source_pair_kernel, [tall, flipped], [], 0, [VMEM] * 3, "source_pair_sum"
+    )(mine, across, swapped(leaving, "col", 1))
+    across = swapped(leaving, "col", 2)
 
     scale = 1.0 / math.sqrt(own_rows * rows * columns)
     if rows > 8:
@@ -343,22 +346,17 @@
     )(received, mine)
     parts = [part] + [swapped(part, "col", bit) for bit in (1, 2, 3)]
 
-    grad_inputs = call(last_kernel, [whole], [], LONG, [VMEM] * 4, "source_sum")(
-        mine, near, across, far
-    )[0]
-    grad_weight, bias_total, output, grad_inputs = call(
-        join_kernel,
-        [
-            jax.ShapeDtypeStruct((width, width), f32),
-            jax.ShapeDtypeStruct((1, width), f32),
-            whole,
-            whole,
-        ],
-        [],
-        LONG,
-        [VMEM] * 7,
-        "results",
-    )(*parts, bias_total, output, grad_inputs)
+    grad_inputs, output, bias_total = call(
+        last_kernel,
+        [whole, whole, jax.ShapeDtypeStruct((1, width), f32)],
+        [],
+        LONG,
+        [VMEM] * 4,
+        "source_sum",
+    )(kept, across, output, bias_total)
+    grad_weight = call(
+        join_kernel, [jax.ShapeDtypeStruct((width, width), f32)], [], LONG, [VMEM] * 4, "weight_join"
+    )(*parts)[0]
     return (output, grad_inputs, grad_weight, bias_total[0])
 
 

time: 52.7 us -> 51.7 us (0.981)
  waiting for transfers between devices: 16.9 us -> 15.7 us
  Pallas kernels: 5.88 us -> 6.46 us
    all_to_all x1, waiting for transfers between devices: 3.58 us -> 2.24 us  [shards(): received = lax.all_to_all(message, 'row', 0, 0, tiled=True)]
    pallas_call x3 -> x4, Pallas kernels: 2.46 us -> 3.04 us  [the longest x1 1.51 us: shards(): call(backward_kernel, [tall, tall, jax.ShapeDtypeStruct((2, width, own_ro...]
    ppermute x12 -> x11, starting transfers between devices: 8.81 us -> 8.49 us  [swapped(): return lax.ppermute(block, axis, [(i, i ^ bit) for i in range(size)])]
    ppermute x12 -> x11, waiting for transfers between devices: 4.84 us -> 4.87 us  [swapped(): return lax.ppermute(block, axis, [(i, i ^ bit) for i in range(size)])]
  transfers between devices with their start and end apart: 21 -> 20, of which waited for: 11 -> 11; matrix products, arithmetic and copies ran while one was open for 0% -> 0% of each run, Pallas kernels for 5% -> 7%
where the time goes in v5:
time: 51.7 us; the launch traced here: 51.4 us
  starting transfers between devices  25.7 us (50%)
  waiting for transfers between devices  15.7 us (30%)
  Pallas kernels  6.46 us (12%)
  local copies, waits for them, and re-layouts  2.17 us (4%)
  between operations  1.45 us (3%)
    ppermute x8, starting transfers between devices, routed(): return lax.ppermute(block, 'row', pairs)  13.6 us
    ppermute x8, waiting for transfers between devices, routed(): return lax.ppermute(block, 'row', pairs)  8.56 us
    ppermute x11, starting transfers between devices, swapped(): return lax.ppermute(block, axis, [(i, i ^ bit) for i in range(size)])  8.49 us
    ppermute x11, waiting for transfers between devices, swapped(): return lax.ppermute(block, axis, [(i, i ^ bit) for i in range(size)])  4.87 us
    all_to_all x1, starting transfers between devices, shards(): received = lax.all_to_all(message, 'row', 0, 0, tiled=True)  3.55 us
    all_to_all x1, waiting for transfers between devices, shards(): received = lax.all_to_all(message, 'row', 0, 0, tiled=True)  2.24 us
    unnamed x22, local copies, waits for them, and re-layouts  2.17 us
    pallas_call x1, Pallas kernels, shards(): call(forward_kernel, [wide] + [whole] * 4, [pltpu.VMEM((sources, BLK, wid...  1.51 us
  transfers between devices with their start and end apart: 20, of which 11 were waited for; matrix products, arithmetic and copies ran while one was open for 0% of the time, Pallas kernels for 7%

profile of v5, /device:TPU:0, one launch (start us, length us, event | category | flops | bytes accessed | tf_op | source)
XLA Modules:
  0.0 51.4 jit_solution(2573074863861436844)
XLA Ops:
  0.6 3.0 %collective-permute-start.1 = (bf16[256,256]{1,0:T(8,128)(2,1)}, bf16[256,256]{1,0:T(8,128)(2,1)S(1)}, u32[]{:S(2)}, u32[]{:S(2)}) collective-permute-start(bf16[256,256]{1,0:T(8,128)(2,1)} %own.1), channel_id=1, source_target_pairs={{0,2},{1,3},{2,0},{3,1},{4,6},{5,7},{6,4},{7,5},{8,10},{9,11},{10,... | collective-permute-start | bytes 393224 | tf_op jit(solution)/shard_map/ppermute | solution.py:46
  3.7 1.2 %copy-done.8 = bf16[1,1,32,128,128]{4,3,2,1,0:T(8,128)(2,1)S(1)} copy-done((bf16[1,1,32,128,128]{4,3,2,1,0:T(8,128)(2,1)S(1)}, bf16[1,1,32,128,128]{4,3,2,1,0:T(8,128)(2,1)}, u32[]{:S(2)}) %copy-start.8) | copy-done | bytes 1048600
  4.9 0.9 %copy-done.9 = bf16[256,256]{1,0:T(8,128)(2,1)S(1)} copy-done((bf16[256,256]{1,0:T(8,128)(2,1)S(1)}, bf16[256,256]{1,0:T(8,128)(2,1)}, u32[]{:S(2)}) %copy-start.9) | copy-done | bytes 131096
  6.7 0.6 %collective-permute-done.1.across = bf16[256,256]{1,0:T(8,128)(2,1)S(1)} collective-permute-done((bf16[256,256]{1,0:T(8,128)(2,1)}, bf16[256,256]{1,0:T(8,128)(2,1)S(1)}, u32[]{:S(2)}, u32[]{:S(2)}) %collective-permute-start.1) | collective-permute-done | bytes 131104 | tf_op jit(solution)/shard_map/ppermute | solution.py:46
  7.4 1.3 %collective-permute-done.2.far = bf16[256,256]{1,0:T(8,128)(2,1)S(1)} collective-permute-done((bf16[256,256]{1,0:T(8,128)(2,1)S(1)}, bf16[256,256]{1,0:T(8,128)(2,1)S(1)}, u32[]{:S(2)}, u32[]{:S(2)}) %collective-permute-start.2) | collective-permute-done | bytes 131104 | tf_op jit(solution)/shard_map/ppermute | solution.py:46
  8.7 1.5 %aggregate_terms.1 = (f32[256,256]{1,0:T(8,128)S(1)}, bf16[256,256]{1,0:T(8,128)(2,1)S(1)}, bf16[256,256]{1,0:T(8,128)(2,1)S(1)}, bf16[256,256]{1,0:T(8,128)(2,1)S(1)}, bf16[256,256]{1,0:T(8,128)(2,1)S(1)}) custom-call(s32[1,1]{1,0:T(1,128)S(6)} %copy.12.count, s32[1,1,32]{2,1,0:T(1,128)S(1)} %copy-done.4, s32[1,1,32]{2,1,0:T(1,128)S(1)} %copy-done.6, ...), custom_call_target="tpu_custom_call" | custom-call | flops 268435456 | bytes 1048576 | tf_op jit(solution)/shard_map/aggregate_terms/pallas_call | solution.py:267
  10.3 1.9 %collective-permute-start.3 = (bf16[256,256]{1,0:T(8,128)(2,1)S(1)}, bf16[256,256]{1,0:T(8,128)(2,1)S(1)}, u32[]{:S(2)}, u32[]{:S(2)}) collective-permute-start(bf16[256,256]{1,0:T(8,128)(2,1)S(1)} %get-tuple-element.34), channel_id=1, source_target_pairs={{0,8},{4,12},{8,16},{12,20},{16,24},{20,28},{24,0},{28,4},{1,9},{5... | collective-permute-start | bytes 393224 | tf_op jit(solution)/shard_map/ppermute | solution.py:41
  12.1 1.5 %collective-permute-start.4 = (bf16[256,256]{1,0:T(8,128)(2,1)S(1)}, bf16[256,256]{1,0:T(8,128)(2,1)S(1)}, u32[]{:S(2)}, u32[]{:S(2)}) collective-permute-start(bf16[256,256]{1,0:T(8,128)(2,1)S(1)} %get-tuple-element.35), channel_id=1, source_target_pairs={{0,4},{4,8},{8,12},{12,16},{16,20},{20,24},{24,28},{28,0},{1,5},{5... | collective-permute-start | bytes 393224 | tf_op jit(solution)/shard_map/ppermute | solution.py:41
  13.7 2.2 %collective-permute-start.5 = (bf16[256,256]{1,0:T(8,128)(2,1)S(1)}, bf16[256,256]{1,0:T(8,128)(2,1)S(1)}, u32[]{:S(2)}, u32[]{:S(2)}) collective-permute-start(bf16[256,256]{1,0:T(8,128)(2,1)S(1)} %get-tuple-element.36), channel_id=1, source_target_pairs={{0,24},{4,28},{8,0},{12,4},{16,8},{20,12},{24,16},{28,20},{1,25},{... | collective-permute-start | bytes 393224 | tf_op jit(solution)/shard_map/ppermute | solution.py:41
  15.9 1.2 %collective-permute-start.6 = (bf16[256,256]{1,0:T(8,128)(2,1)S(1)}, bf16[256,256]{1,0:T(8,128)(2,1)S(1)}, u32[]{:S(2)}, u32[]{:S(2)}) collective-permute-start(bf16[256,256]{1,0:T(8,128)(2,1)S(1)} %get-tuple-element.37), channel_id=1, source_target_pairs={{0,28},{4,0},{8,4},{12,8},{16,12},{20,16},{24,20},{28,24},{1,29},{... | collective-permute-start | bytes 393224 | tf_op jit(solution)/shard_map/ppermute | solution.py:41
  17.2 1.0 %collective-permute-done.3.first = bf16[256,256]{1,0:T(8,128)(2,1)S(1)} collective-permute-done((bf16[256,256]{1,0:T(8,128)(2,1)S(1)}, bf16[256,256]{1,0:T(8,128)(2,1)S(1)}, u32[]{:S(2)}, u32[]{:S(2)}) %collective-permute-start.3) | collective-permute-done | bytes 131104 | tf_op jit(solution)/shard_map/ppermute | solution.py:41
  18.1 4.4 %collective-permute-done.4.second = bf16[256,256]{1,0:T(8,128)(2,1)S(1)} collective-permute-done((bf16[256,256]{1,0:T(8,128)(2,1)S(1)}, bf16[256,256]{1,0:T(8,128)(2,1)S(1)}, u32[]{:S(2)}, u32[]{:S(2)}) %collective-permute-start.4) | collective-permute-done | bytes 131104 | tf_op jit(solution)/shard_map/ppermute | solution.py:41
  22.5 1.0 %collective-permute-done.6.fourth = bf16[256,256]{1,0:T(8,128)(2,1)S(1)} collective-permute-done((bf16[256,256]{1,0:T(8,128)(2,1)S(1)}, bf16[256,256]{1,0:T(8,128)(2,1)S(1)}, u32[]{:S(2)}, u32[]{:S(2)}) %collective-permute-start.6) | collective-permute-done | bytes 131104 | tf_op jit(solution)/shard_map/ppermute | solution.py:41
  23.5 0.6 %pointwise.1 = (bf16[256,256]{1,0:T(8,128)(2,1)S(1)}, bf16[256,256]{1,0:T(8,128)(2,1)S(1)}, bf16[256,256]{1,0:T(8,128)(2,1)S(1)}, bf16[256,256]{1,0:T(8,128)(2,1)S(1)}, f32[1,256]{1,0:T(1,128)S(1)}) custom-call(f32[256,256]{1,0:T(8,128)S(1)} %get-tuple-element.33.mine, bf16[256,256]{1,0:T(8,128)(2,1)S(1)} %collective-permute-done.3.first, ...), custom_call_target="tpu_custom_call" | custom-call | flops 100663296 | bytes 1048576 | tf_op jit(solution)/shard_map/pointwise/pallas_call | solution.py:281
  24.5 1.6 %collective-permute-start.14 = (bf16[72,256]{1,0:T(8,128)(2,1)S(1)}, bf16[72,256]{1,0:T(8,128)(2,1)S(1)}, u32[]{:S(2)}, u32[]{:S(2)}) collective-permute-start(bf16[72,256]{1,0:T(8,128)(2,1)S(1)} %get-tuple-element.51), channel_id=1, source_target_pairs={{0,2},{1,3},{2,0},{3,1},{4,6},{5,7},{6,4},{7,5},{8,10},{9,11},{10,... | collective-permute-start | bytes 110600 | tf_op jit(solution)/shard_map/ppermute | solution.py:46
  26.0 0.3 collective-permute-start.15
  26.3 2.1 %collective-permute-start.9 = (bf16[256,256]{1,0:T(8,128)(2,1)S(1)}, bf16[256,256]{1,0:T(8,128)(2,1)S(1)}, u32[]{:S(2)}, u32[]{:S(2)}) collective-permute-start(bf16[256,256]{1,0:T(8,128)(2,1)S(1)} %get-tuple-element.39.local), channel_id=1, source_target_pairs={{0,4},{4,8},{8,12},{12,16},{16,20},{20,24},{24,28},{28,0},{1,5},{5... | collective-permute-start | bytes 393224 | tf_op jit(solution)/shard_map/ppermute | solution.py:41
  28.5 2.7 %collective-permute-start.8 = (bf16[256,256]{1,0:T(8,128)(2,1)S(1)}, bf16[256,256]{1,0:T(8,128)(2,1)S(1)}, u32[]{:S(2)}, u32[]{:S(2)}) collective-permute-start(bf16[256,256]{1,0:T(8,128)(2,1)S(1)} %get-tuple-element.39.local), channel_id=1, source_target_pairs={{0,28},{4,0},{8,4},{12,8},{16,12},{20,16},{24,20},{28,24},{1,29},{... | collective-permute-start | bytes 393224 | tf_op jit(solution)/shard_map/ppermute | solution.py:41
  31.2 1.9 %collective-permute-start.7 = (bf16[256,256]{1,0:T(8,128)(2,1)S(1)}, bf16[256,256]{1,0:T(8,128)(2,1)S(1)}, u32[]{:S(2)}, u32[]{:S(2)}) collective-permute-start(bf16[256,256]{1,0:T(8,128)(2,1)S(1)} %get-tuple-element.39.local), channel_id=1, source_target_pairs={{0,24},{4,28},{8,0},{12,4},{16,8},{20,12},{24,16},{28,20},{1,25},{... | collective-permute-start | bytes 393224 | tf_op jit(solution)/shard_map/ppermute | solution.py:41
  33.1 0.7 %weight_column_sum.1 = bf16[8,72,256]{2,1,0:T(8,128)(2,1)} custom-call(f32[72,256]{1,0:T(8,128)S(1)} %get-tuple-element.49.mine, bf16[72,256]{1,0:T(8,128)(2,1)S(1)} %collective-permute-done.13.near, bf16[72,256]{1,0:T(8,128)(2,1)S(1)} %collective-permute-done.14.across, bf16[72,256]{1,0:T(8,128)(2,1)S(1)} %collective-permute-done.15.far), custom_call_target="tpu_custom_call" | custom-call | flops 99999997952 | bytes 1048576 | tf_op jit(solution)/shard_map/weight_column_sum/pallas_call | solution.py:301
  33.8 3.6 %all-to-all-start = ((bf16[8,72,256]{2,1,0:T(8,128)(2,1)}), bf16[8,72,256]{2,1,0:T(8,128)(2,1)S(1)}, u32[]{:S(2)}, u32[]{:S(2)}) async-start(bf16[8,72,256]{2,1,0:T(8,128)(2,1)} %weight_column_sum.1), calls=%async_computation | async-start | bytes 589824 | tf_op jit(solution)/shard_map/all_to_all | solution.py:338
  37.4 0.9 %collective-permute-done.9.third = bf16[256,256]{1,0:T(8,128)(2,1)S(1)} collective-permute-done((bf16[256,256]{1,0:T(8,128)(2,1)S(1)}, bf16[256,256]{1,0:T(8,128)(2,1)S(1)}, u32[]{:S(2)}, u32[]{:S(2)}) %collective-permute-start.9) | collective-permute-done | bytes 131104 | tf_op jit(solution)/shard_map/ppermute | solution.py:41
  38.3 1.2 %collective-permute-done.7.first = bf16[256,256]{1,0:T(8,128)(2,1)S(1)} collective-permute-done((bf16[256,256]{1,0:T(8,128)(2,1)S(1)}, bf16[256,256]{1,0:T(8,128)(2,1)S(1)}, u32[]{:S(2)}, u32[]{:S(2)}) %collective-permute-start.7) | collective-permute-done | bytes 131104 | tf_op jit(solution)/shard_map/ppermute | solution.py:41
  39.6 1.5 %source_terms.1 = (f32[256,256]{1,0:T(8,128)S(1)}, f32[256,256]{1,0:T(8,128)S(1)}, bf16[2,256,256]{2,1,0:T(8,128)(2,1)S(1)}) custom-call(s32[1,1]{1,0:T(1,128)S(6)} %copy.12.count, s32[1,1,32]{2,1,0:T(1,128)S(1)} %copy-done.5, s32[1,1,32]{2,1,0:T(1,128)S(1)} %copy-done.7, bf16[1,1,32,128,128]{4,3,2,1,0:T(8,128)(2,1)S(1)} %copy-done.1, ...), custom_call_target="tpu_custom_call" | custom-call | flops 99999997952 | bytes 1048576 | tf_op jit(solution)/shard_map/source_terms/pallas_call | solution.py:315
  41.2 1.5 %collective-permute-done.11.arrived = bf16[2,256,256]{2,1,0:T(8,128)(2,1)S(1)} collective-permute-done((bf16[2,256,256]{2,1,0:T(8,128)(2,1)S(1)}, bf16[2,256,256]{2,1,0:T(8,128)(2,1)S(1)}, u32[]{:S(2)}, u32[]{:S(2)}) %collective-permute-start.11) | collective-permute-done | bytes 262176 | tf_op jit(solution)/shard_map/ppermute | solution.py:46
  42.8 1.6 %collective-permute-start.12 = (bf16[256,256]{1,0:T(8,128)(2,1)S(1)}, bf16[256,256]{1,0:T(8,128)(2,1)S(1)}, u32[]{:S(2)}, u32[]{:S(2)}) collective-permute-start(bf16[256,256]{1,0:T(8,128)(2,1)S(1)} %get-tuple-element.44), channel_id=1, source_target_pairs={{0,2},{1,3},{2,0},{3,1},{4,6},{5,7},{6,4},{7,5},{8,10},{9,11},{10,... | collective-permute-start | bytes 393224 | tf_op jit(solution)/shard_map/ppermute | solution.py:46
  44.3 2.2 %all-to-all-done.received = bf16[8,72,256]{2,1,0:T(8,128)(2,1)S(1)} async-done(((bf16[8,72,256]{2,1,0:T(8,128)(2,1)}), bf16[8,72,256]{2,1,0:T(8,128)(2,1)S(1)}, u32[]{:S(2)}, u32[]{:S(2)}) %all-to-all-start) | async-done | bytes 294944 | tf_op jit(solution)/shard_map/all_to_all | solution.py:338
  46.7 1.6 %collective-permute-start.17 = (bf16[64,256]{1,0:T(8,128)(2,1)S(1)}, bf16[64,256]{1,0:T(8,128)(2,1)S(1)}, u32[]{:S(2)}, u32[]{:S(2)}) collective-permute-start(bf16[64,256]{1,0:T(8,128)(2,1)S(1)} %get-tuple-element.56.own), channel_id=1, source_target_pairs={{0,2},{1,3},{2,0},{3,1},{4,6},{5,7},{6,4},{7,5},{8,10},{9,11},{10,... | collective-permute-start | bytes 98312 | tf_op jit(solution)/shard_map/ppermute | solution.py:46
  48.5 0.8 %source_sum.1 = (bf16[256,256]{1,0:T(8,128)(2,1)}, bf16[256,256]{1,0:T(8,128)(2,1)}, f32[1,256]{1,0:T(1,128)}) custom-call(f32[256,256]{1,0:T(8,128)S(1)} %get-tuple-element.43.mine, bf16[256,256]{1,0:T(8,128)(2,1)S(1)} %collective-permute-done.12.arrived, bf16[256,256]{1,0:T(8,128)(2,1)S(1)} %get-tuple-element.45.output_in, ...), custom_call_target="tpu_custom_call" | custom-call | flops 99999997952 | bytes 1048576 | tf_op jit(solution)/shard_map/source_sum/pallas_call | solution.py:349
  49.3 1.0 %collective-permute-done.18.far = bf16[64,256]{1,0:T(8,128)(2,1)S(1)} collective-permute-done((bf16[64,256]{1,0:T(8,128)(2,1)S(1)}, bf16[64,256]{1,0:T(8,128)(2,1)S(1)}, u32[]{:S(2)}, u32[]{:S(2)}) %collective-permute-start.18) | collective-permute-done | bytes 32800 | tf_op jit(solution)/shard_map/ppermute | solution.py:46
  50.3 0.4 collective-permute-done.17.across
  50.7 0.7 %weight_join.1 = f32[256,256]{1,0:T(8,128)} custom-call(bf16[64,256]{1,0:T(8,128)(2,1)S(1)} %get-tuple-element.56.own, bf16[64,256]{1,0:T(8,128)(2,1)S(1)} %collective-permute-done.16.near, bf16[64,256]{1,0:T(8,128)(2,1)S(1)} %collective-permute-done.17.across, bf16[64,256]{1,0:T(8,128)(2,1)S(1)} %collective-permute-done.18.far), custom_call_target="tpu_custom_call" | custom-call | flops 99999997952 | bytes 1048576 | tf_op jit(solution)/shard_map/weight_join/pallas_call | solution.py:357
  (41 shorter events, 1.2 us)
Async XLA Ops:
  0.6 3.0 %copy-start.10 = (f32[256]{0:T(256)S(1)}, f32[256]{0:T(256)}, u32[]{:S(2)}) copy-start(f32[256]{0:T(256)} %param.10) | copy-start | bytes 3076
  0.6 6.7 %collective-permute-start.1 = (bf16[256,256]{1,0:T(8,128)(2,1)}, bf16[256,256]{1,0:T(8,128)(2,1)S(1)}, u32[]{:S(2)}, u32[]{:S(2)}) collective-permute-start(bf16[256,256]{1,0:T(8,128)(2,1)} %own.1), channel_id=1, source_target_pairs={{0,2},{1,3},{2,0},{3,1},{4,6},{5,7},{6,4},{7,5},{8,10},{9,11},{10,... | collective-permute-start | bytes 393224 | tf_op jit(solution)/shard_map/ppermute | solution.py:46
  3.6 3.7 %collective-permute-start = (bf16[256,256]{1,0:T(8,128)(2,1)}, bf16[256,256]{1,0:T(8,128)(2,1)S(1)}, u32[]{:S(2)}, u32[]{:S(2)}) collective-permute-start(bf16[256,256]{1,0:T(8,128)(2,1)} %own.1), channel_id=1, source_target_pairs={{0,1},{1,0},{2,3},{3,2},{4,5},{5,4},{6,7},{7,6},{8,9},{9,8},{10,11... | collective-permute-start | bytes 393224 | tf_op jit(solution)/shard_map/ppermute | solution.py:46
  3.7 1.2 %copy-start.8 = (bf16[1,1,32,128,128]{4,3,2,1,0:T(8,128)(2,1)S(1)}, bf16[1,1,32,128,128]{4,3,2,1,0:T(8,128)(2,1)}, u32[]{:S(2)}) copy-start(bf16[1,1,32,128,128]{4,3,2,1,0:T(8,128)(2,1)} %values.1) | copy-start | bytes 3145732
  4.9 0.9 %copy-start.9 = (bf16[256,256]{1,0:T(8,128)(2,1)S(1)}, bf16[256,256]{1,0:T(8,128)(2,1)}, u32[]{:S(2)}) copy-start(bf16[256,256]{1,0:T(8,128)(2,1)} %own.1) | copy-start | bytes 393220
  6.1 2.6 %copy-start = (bf16[1,1,32,128,128]{4,3,2,1,0:T(8,128)(2,1)}, bf16[1,1,32,128,128]{4,3,2,1,0:T(8,128)(2,1)S(1)}, u32[]{:S(2)}) copy-start(bf16[1,1,32,128,128]{4,3,2,1,0:T(8,128)(2,1)S(1)} %get-tuple-element.31.values) | copy-start | bytes 3145732
  7.4 1.3 %collective-permute-start.2 = (bf16[256,256]{1,0:T(8,128)(2,1)S(1)}, bf16[256,256]{1,0:T(8,128)(2,1)S(1)}, u32[]{:S(2)}, u32[]{:S(2)}) collective-permute-start(bf16[256,256]{1,0:T(8,128)(2,1)S(1)} %collective-permute-done.1.across), channel_id=1, source_target_pairs={{0,1},{1,0},{2,3},{3,2},{4,5},{5,4},{6,7},{7,6},{8,9},{9,8},{10,11... | collective-permute-start | bytes 393224 | tf_op jit(solution)/shard_map/ppermute | solution.py:46
  7.4 1.3 %copy-start.4 = (s32[1,1,32]{2,1,0:T(1,128)S(1)}, s32[1,1,32]{2,1,0:T(1,128)}, u32[]{:S(2)}) copy-start(s32[1,1,32]{2,1,0:T(1,128)} %target.3) | copy-start | bytes 388
  7.4 1.3 %copy-start.6 = (s32[1,1,32]{2,1,0:T(1,128)S(1)}, s32[1,1,32]{2,1,0:T(1,128)}, u32[]{:S(2)}) copy-start(s32[1,1,32]{2,1,0:T(1,128)} %source.3) | copy-start | bytes 388
  8.7 14.8 %copy-start.2 = (bf16[256,256]{1,0:T(8,128)(2,1)S(1)}, bf16[256,256]{1,0:T(8,128)(2,1)}, u32[]{:S(2)}) copy-start(bf16[256,256]{1,0:T(8,128)(2,1)} %weight.1) | copy-start | bytes 393220
  8.7 14.8 %copy-start.3 = (bf16[256,256]{1,0:T(8,128)(2,1)S(1)}, bf16[256,256]{1,0:T(8,128)(2,1)}, u32[]{:S(2)}) copy-start(bf16[256,256]{1,0:T(8,128)(2,1)} %cotangent.1) | copy-start | bytes 393220
  10.3 7.9 %collective-permute-start.3 = (bf16[256,256]{1,0:T(8,128)(2,1)S(1)}, bf16[256,256]{1,0:T(8,128)(2,1)S(1)}, u32[]{:S(2)}, u32[]{:S(2)}) collective-permute-start(bf16[256,256]{1,0:T(8,128)(2,1)S(1)} %get-tuple-element.34), channel_id=1, source_target_pairs={{0,8},{4,12},{8,16},{12,20},{16,24},{20,28},{24,0},{28,4},{1,9},{5... | collective-permute-start | bytes 393224 | tf_op jit(solution)/shard_map/ppermute | solution.py:41
  12.1 10.4 %collective-permute-start.4 = (bf16[256,256]{1,0:T(8,128)(2,1)S(1)}, bf16[256,256]{1,0:T(8,128)(2,1)S(1)}, u32[]{:S(2)}, u32[]{:S(2)}) collective-permute-start(bf16[256,256]{1,0:T(8,128)(2,1)S(1)} %get-tuple-element.35), channel_id=1, source_target_pairs={{0,4},{4,8},{8,12},{12,16},{16,20},{20,24},{24,28},{28,0},{1,5},{5... | collective-permute-start | bytes 393224 | tf_op jit(solution)/shard_map/ppermute | solution.py:41
  13.7 8.8 %collective-permute-start.5 = (bf16[256,256]{1,0:T(8,128)(2,1)S(1)}, bf16[256,256]{1,0:T(8,128)(2,1)S(1)}, u32[]{:S(2)}, u32[]{:S(2)}) collective-permute-start(bf16[256,256]{1,0:T(8,128)(2,1)S(1)} %get-tuple-element.36), channel_id=1, source_target_pairs={{0,24},{4,28},{8,0},{12,4},{16,8},{20,12},{24,16},{28,20},{1,25},{... | collective-permute-start | bytes 393224 | tf_op jit(solution)/shard_map/ppermute | solution.py:41
  15.9 7.6 %collective-permute-start.6 = (bf16[256,256]{1,0:T(8,128)(2,1)S(1)}, bf16[256,256]{1,0:T(8,128)(2,1)S(1)}, u32[]{:S(2)}, u32[]{:S(2)}) collective-permute-start(bf16[256,256]{1,0:T(8,128)(2,1)S(1)} %get-tuple-element.37), channel_id=1, source_target_pairs={{0,28},{4,0},{8,4},{12,8},{16,12},{20,16},{24,20},{28,24},{1,29},{... | collective-permute-start | bytes 393224 | tf_op jit(solution)/shard_map/ppermute | solution.py:41
  24.4 4.1 %collective-permute-start.13 = (bf16[72,256]{1,0:T(8,128)(2,1)S(1)}, bf16[72,256]{1,0:T(8,128)(2,1)S(1)}, u32[]{:S(2)}, u32[]{:S(2)}) collective-permute-start(bf16[72,256]{1,0:T(8,128)(2,1)S(1)} %get-tuple-element.50), channel_id=1, source_target_pairs={{0,1},{1,0},{2,3},{3,2},{4,5},{5,4},{6,7},{7,6},{8,9},{9,8},{10,11... | collective-permute-start | bytes 110600 | tf_op jit(solution)/shard_map/ppermute | solution.py:46
  24.5 6.7 %collective-permute-start.14 = (bf16[72,256]{1,0:T(8,128)(2,1)S(1)}, bf16[72,256]{1,0:T(8,128)(2,1)S(1)}, u32[]{:S(2)}, u32[]{:S(2)}) collective-permute-start(bf16[72,256]{1,0:T(8,128)(2,1)S(1)} %get-tuple-element.51), channel_id=1, source_target_pairs={{0,2},{1,3},{2,0},{3,1},{4,6},{5,7},{6,4},{7,5},{8,10},{9,11},{10,... | collective-permute-start | bytes 110600 | tf_op jit(solution)/shard_map/ppermute | solution.py:46
  26.0 7.1 %collective-permute-start.15 = (bf16[72,256]{1,0:T(8,128)(2,1)S(1)}, bf16[72,256]{1,0:T(8,128)(2,1)S(1)}, u32[]{:S(2)}, u32[]{:S(2)}) collective-permute-start(bf16[72,256]{1,0:T(8,128)(2,1)S(1)} %get-tuple-element.52), channel_id=1, source_target_pairs={{0,3},{1,2},{2,1},{3,0},{4,7},{5,6},{6,5},{7,4},{8,11},{9,10},{10,... | collective-permute-start | bytes 110600 | tf_op jit(solution)/shard_map/ppermute | solution.py:46
  26.3 11.1 %collective-permute-start.10 = (bf16[256,256]{1,0:T(8,128)(2,1)S(1)}, bf16[256,256]{1,0:T(8,128)(2,1)S(1)}, u32[]{:S(2)}, u32[]{:S(2)}) collective-permute-start(bf16[256,256]{1,0:T(8,128)(2,1)S(1)} %get-tuple-element.39.local), channel_id=1, source_target_pairs={{0,8},{4,12},{8,16},{12,20},{16,24},{20,28},{24,0},{28,4},{1,9},{5... | collective-permute-start | bytes 393224 | tf_op jit(solution)/shard_map/ppermute | solution.py:41
  26.3 12.0 %collective-permute-start.9 = (bf16[256,256]{1,0:T(8,128)(2,1)S(1)}, bf16[256,256]{1,0:T(8,128)(2,1)S(1)}, u32[]{:S(2)}, u32[]{:S(2)}) collective-permute-start(bf16[256,256]{1,0:T(8,128)(2,1)S(1)} %get-tuple-element.39.local), channel_id=1, source_target_pairs={{0,4},{4,8},{8,12},{12,16},{16,20},{20,24},{24,28},{28,0},{1,5},{5... | collective-permute-start | bytes 393224 | tf_op jit(solution)/shard_map/ppermute | solution.py:41
  28.5 9.9 %collective-permute-start.8 = (bf16[256,256]{1,0:T(8,128)(2,1)S(1)}, bf16[256,256]{1,0:T(8,128)(2,1)S(1)}, u32[]{:S(2)}, u32[]{:S(2)}) collective-permute-start(bf16[256,256]{1,0:T(8,128)(2,1)S(1)} %get-tuple-element.39.local), channel_id=1, source_target_pairs={{0,28},{4,0},{8,4},{12,8},{16,12},{20,16},{24,20},{28,24},{1,29},{... | collective-permute-start | bytes 393224 | tf_op jit(solution)/shard_map/ppermute | solution.py:41
  31.2 8.4 %collective-permute-start.7 = (bf16[256,256]{1,0:T(8,128)(2,1)S(1)}, bf16[256,256]{1,0:T(8,128)(2,1)S(1)}, u32[]{:S(2)}, u32[]{:S(2)}) collective-permute-start(bf16[256,256]{1,0:T(8,128)(2,1)S(1)} %get-tuple-element.39.local), channel_id=1, source_target_pairs={{0,24},{4,28},{8,0},{12,4},{16,8},{20,12},{24,16},{28,20},{1,25},{... | collective-permute-start | bytes 393224 | tf_op jit(solution)/shard_map/ppermute | solution.py:41
  33.1 6.5 %copy-start.1 = (bf16[1,1,32,128,128]{4,3,2,1,0:T(8,128)(2,1)S(1)}, bf16[1,1,32,128,128]{4,3,2,1,0:T(8,128)(2,1)}, u32[]{:S(2)}) copy-start(bf16[1,1,32,128,128]{4,3,2,1,0:T(8,128)(2,1)} %copy-done) | copy-start | bytes 3145732
  33.8 5.8 %copy-start.5 = (s32[1,1,32]{2,1,0:T(1,128)S(1)}, s32[1,1,32]{2,1,0:T(1,128)}, u32[]{:S(2)}) copy-start(s32[1,1,32]{2,1,0:T(1,128)} %target.3) | copy-start | bytes 388
  33.8 5.8 %copy-start.7 = (s32[1,1,32]{2,1,0:T(1,128)S(1)}, s32[1,1,32]{2,1,0:T(1,128)}, u32[]{:S(2)}) copy-start(s32[1,1,32]{2,1,0:T(1,128)} %source.3) | copy-start | bytes 388
  33.8 12.7 %all-to-all-start = ((bf16[8,72,256]{2,1,0:T(8,128)(2,1)}), bf16[8,72,256]{2,1,0:T(8,128)(2,1)S(1)}, u32[]{:S(2)}, u32[]{:S(2)}) async-start(bf16[8,72,256]{2,1,0:T(8,128)(2,1)} %weight_column_sum.1), calls=%async_computation | async-start | bytes 589824 | tf_op jit(solution)/shard_map/all_to_all | solution.py:338
  41.1 1.6 %collective-permute-start.11 = (bf16[2,256,256]{2,1,0:T(8,128)(2,1)S(1)}, bf16[2,256,256]{2,1,0:T(8,128)(2,1)S(1)}, u32[]{:S(2)}, u32[]{:S(2)}) collective-permute-start(bf16[2,256,256]{2,1,0:T(8,128)(2,1)S(1)} %get-tuple-element.42), channel_id=1, source_target_pairs={{0,1},{1,0},{2,3},{3,2},{4,5},{5,4},{6,7},{7,6},{8,9},{9,8},{10,11... | collective-permute-start | bytes 786440 | tf_op jit(solution)/shard_map/ppermute | solution.py:46
  42.8 5.8 %collective-permute-start.12 = (bf16[256,256]{1,0:T(8,128)(2,1)S(1)}, bf16[256,256]{1,0:T(8,128)(2,1)S(1)}, u32[]{:S(2)}, u32[]{:S(2)}) collective-permute-start(bf16[256,256]{1,0:T(8,128)(2,1)S(1)} %get-tuple-element.44), channel_id=1, source_target_pairs={{0,2},{1,3},{2,0},{3,1},{4,6},{5,7},{6,4},{7,5},{8,10},{9,11},{10,... | collective-permute-start | bytes 393224 | tf_op jit(solution)/shard_map/ppermute | solution.py:46
  46.6 3.7 %collective-permute-start.18 = (bf16[64,256]{1,0:T(8,128)(2,1)S(1)}, bf16[64,256]{1,0:T(8,128)(2,1)S(1)}, u32[]{:S(2)}, u32[]{:S(2)}) collective-permute-start(bf16[64,256]{1,0:T(8,128)(2,1)S(1)} %get-tuple-element.56.own), channel_id=1, source_target_pairs={{0,3},{1,2},{2,1},{3,0},{4,7},{5,6},{6,5},{7,4},{8,11},{9,10},{10,... | collective-permute-start | bytes 98312 | tf_op jit(solution)/shard_map/ppermute | solution.py:46
  46.7 4.0 %collective-permute-start.17 = (bf16[64,256]{1,0:T(8,128)(2,1)S(1)}, bf16[64,256]{1,0:T(8,128)(2,1)S(1)}, u32[]{:S(2)}, u32[]{:S(2)}) collective-permute-start(bf16[64,256]{1,0:T(8,128)(2,1)S(1)} %get-tuple-element.56.own), channel_id=1, source_target_pairs={{0,2},{1,3},{2,0},{3,1},{4,6},{5,7},{6,4},{7,5},{8,10},{9,11},{10,... | collective-permute-start | bytes 98312 | tf_op jit(solution)/shard_map/ppermute | solution.py:46
  48.2 2.5 %collective-permute-start.16 = (bf16[64,256]{1,0:T(8,128)(2,1)S(1)}, bf16[64,256]{1,0:T(8,128)(2,1)S(1)}, u32[]{:S(2)}, u32[]{:S(2)}) collective-permute-start(bf16[64,256]{1,0:T(8,128)(2,1)S(1)} %get-tuple-element.56.own), channel_id=1, source_target_pairs={{0,1},{1,0},{2,3},{3,2},{4,5},{5,4},{6,7},{7,6},{8,9},{9,8},{10,11... | collective-permute-start | bytes 98312 | tf_op jit(solution)/shard_map/ppermute | solution.py:46

commit v6 on v5

--- a/solution.py
+++ b/solution.py
@@ -13,8 +13,8 @@
 VB = 2
 SPAN = 2 * HALF + 1
 TAIL = 8
-FORWARD = ((2, None), (1, None), (-2, None), (-1, None))
-BACKWARD = ((-2, None), (-1, None), (1, None), (2, None))
+FORWARD = ((1, None), (2, None), (-2, None), (-1, None))
+BACKWARD = ((-1, None), (-2, None), (1, None), (2, None))
 SLOT_GROUP = 32
 LONG = 10**11
 VMEM = pltpu.VMEM

time: 51.7 us -> 51.3 us (level)
  waiting for transfers between devices: 15.7 us -> 14.6 us
  starting transfers between devices: 25.7 us -> 26.4 us
    all_to_all x1, waiting for transfers between devices: 2.24 us -> 0.97 us  [shards(): received = lax.all_to_all(message, 'row', 0, 0, tiled=True)]
    ppermute x8, starting transfers between devices: 13.6 us -> 14.3 us  [routed(): return lax.ppermute(block, 'row', pairs)]
where the time goes in v6:
time: 51.3 us; the launch traced here: 51 us
  starting transfers between devices  26.4 us (51%)
  waiting for transfers between devices  14.6 us (28%)
  Pallas kernels  6.46 us (13%)
  local copies, waits for them, and re-layouts  2.17 us (4%)
  between operations  1.46 us (3%)
    ppermute x8, starting transfers between devices, routed(): return lax.ppermute(block, 'row', pairs)  14.3 us
    ppermute x8, waiting for transfers between devices, routed(): return lax.ppermute(block, 'row', pairs)  8.73 us
    ppermute x11, starting transfers between devices, swapped(): return lax.ppermute(block, axis, [(i, i ^ bit) for i in range(size)])  8.49 us
    ppermute x11, waiting for transfers between devices, swapped(): return lax.ppermute(block, axis, [(i, i ^ bit) for i in range(size)])  4.87 us
    all_to_all x1, starting transfers between devices, shards(): received = lax.all_to_all(message, 'row', 0, 0, tiled=True)  3.55 us
    unnamed x22, local copies, waits for them, and re-layouts  2.17 us
    pallas_call x1, Pallas kernels, shards(): call(forward_kernel, [wide] + [whole] * 4, [pltpu.VMEM((sources, BLK, wid...  1.51 us
    pallas_call x1, Pallas kernels, shards(): call(backward_kernel, [tall, tall, jax.ShapeDtypeStruct((2, width, own_ro...  1.51 us
  transfers between devices with their start and end apart: 20, of which 11 were waited for; matrix products, arithmetic and copies ran while one was open for 0% of the time, Pallas kernels for 7%

profile of v6, /device:TPU:0, one launch (start us, length us, event | category | flops | bytes accessed | tf_op | source)
XLA Modules:
  0.0 51.0 jit_solution(10765625617652234730)
XLA Ops:
  0.6 3.0 %collective-permute-start.1 = (bf16[256,256]{1,0:T(8,128)(2,1)}, bf16[256,256]{1,0:T(8,128)(2,1)S(1)}, u32[]{:S(2)}, u32[]{:S(2)}) collective-permute-start(bf16[256,256]{1,0:T(8,128)(2,1)} %own.1), channel_id=1, source_target_pairs={{0,2},{1,3},{2,0},{3,1},{4,6},{5,7},{6,4},{7,5},{8,10},{9,11},{10,... | collective-permute-start | bytes 393224 | tf_op jit(solution)/shard_map/ppermute | solution.py:46
  3.7 1.2 %copy-done.8 = bf16[1,1,32,128,128]{4,3,2,1,0:T(8,128)(2,1)S(1)} copy-done((bf16[1,1,32,128,128]{4,3,2,1,0:T(8,128)(2,1)S(1)}, bf16[1,1,32,128,128]{4,3,2,1,0:T(8,128)(2,1)}, u32[]{:S(2)}) %copy-start.8) | copy-done | bytes 1048600
  4.9 0.9 %copy-done.9 = bf16[256,256]{1,0:T(8,128)(2,1)S(1)} copy-done((bf16[256,256]{1,0:T(8,128)(2,1)S(1)}, bf16[256,256]{1,0:T(8,128)(2,1)}, u32[]{:S(2)}) %copy-start.9) | copy-done | bytes 131096
  6.7 0.6 %collective-permute-done.1.across = bf16[256,256]{1,0:T(8,128)(2,1)S(1)} collective-permute-done((bf16[256,256]{1,0:T(8,128)(2,1)}, bf16[256,256]{1,0:T(8,128)(2,1)S(1)}, u32[]{:S(2)}, u32[]{:S(2)}) %collective-permute-start.1) | collective-permute-done | bytes 131104 | tf_op jit(solution)/shard_map/ppermute | solution.py:46
  7.4 1.3 %collective-permute-done.2.far = bf16[256,256]{1,0:T(8,128)(2,1)S(1)} collective-permute-done((bf16[256,256]{1,0:T(8,128)(2,1)S(1)}, bf16[256,256]{1,0:T(8,128)(2,1)S(1)}, u32[]{:S(2)}, u32[]{:S(2)}) %collective-permute-start.2) | collective-permute-done | bytes 131104 | tf_op jit(solution)/shard_map/ppermute | solution.py:46
  8.7 1.5 %aggregate_terms.1 = (f32[256,256]{1,0:T(8,128)S(1)}, bf16[256,256]{1,0:T(8,128)(2,1)S(1)}, bf16[256,256]{1,0:T(8,128)(2,1)S(1)}, bf16[256,256]{1,0:T(8,128)(2,1)S(1)}, bf16[256,256]{1,0:T(8,128)(2,1)S(1)}) custom-call(s32[1,1]{1,0:T(1,128)S(6)} %copy.12.count, s32[1,1,32]{2,1,0:T(1,128)S(1)} %copy-done.4, s32[1,1,32]{2,1,0:T(1,128)S(1)} %copy-done.6, ...), custom_call_target="tpu_custom_call" | custom-call | flops 268435456 | bytes 1048576 | tf_op jit(solution)/shard_map/aggregate_terms/pallas_call | solution.py:267
  10.3 1.8 %collective-permute-start.3 = (bf16[256,256]{1,0:T(8,128)(2,1)S(1)}, bf16[256,256]{1,0:T(8,128)(2,1)S(1)}, u32[]{:S(2)}, u32[]{:S(2)}) collective-permute-start(bf16[256,256]{1,0:T(8,128)(2,1)S(1)} %get-tuple-element.34), channel_id=1, source_target_pairs={{0,4},{4,8},{8,12},{12,16},{16,20},{20,24},{24,28},{28,0},{1,5},{5... | collective-permute-start | bytes 393224 | tf_op jit(solution)/shard_map/ppermute | solution.py:41
  12.1 1.6 %collective-permute-start.4 = (bf16[256,256]{1,0:T(8,128)(2,1)S(1)}, bf16[256,256]{1,0:T(8,128)(2,1)S(1)}, u32[]{:S(2)}, u32[]{:S(2)}) collective-permute-start(bf16[256,256]{1,0:T(8,128)(2,1)S(1)} %get-tuple-element.35), channel_id=1, source_target_pairs={{0,8},{4,12},{8,16},{12,20},{16,24},{20,28},{24,0},{28,4},{1,9},{5... | collective-permute-start | bytes 393224 | tf_op jit(solution)/shard_map/ppermute | solution.py:41
  13.7 2.2 %collective-permute-start.5 = (bf16[256,256]{1,0:T(8,128)(2,1)S(1)}, bf16[256,256]{1,0:T(8,128)(2,1)S(1)}, u32[]{:S(2)}, u32[]{:S(2)}) collective-permute-start(bf16[256,256]{1,0:T(8,128)(2,1)S(1)} %get-tuple-element.36), channel_id=1, source_target_pairs={{0,24},{4,28},{8,0},{12,4},{16,8},{20,12},{24,16},{28,20},{1,25},{... | collective-permute-start | bytes 393224 | tf_op jit(solution)/shard_map/ppermute | solution.py:41
  15.9 1.3 %collective-permute-start.6 = (bf16[256,256]{1,0:T(8,128)(2,1)S(1)}, bf16[256,256]{1,0:T(8,128)(2,1)S(1)}, u32[]{:S(2)}, u32[]{:S(2)}) collective-permute-start(bf16[256,256]{1,0:T(8,128)(2,1)S(1)} %get-tuple-element.37), channel_id=1, source_target_pairs={{0,28},{4,0},{8,4},{12,8},{16,12},{20,16},{24,20},{28,24},{1,29},{... | collective-permute-start | bytes 393224 | tf_op jit(solution)/shard_map/ppermute | solution.py:41
  17.2 2.3 %collective-permute-done.3.first = bf16[256,256]{1,0:T(8,128)(2,1)S(1)} collective-permute-done((bf16[256,256]{1,0:T(8,128)(2,1)S(1)}, bf16[256,256]{1,0:T(8,128)(2,1)S(1)}, u32[]{:S(2)}, u32[]{:S(2)}) %collective-permute-start.3) | collective-permute-done | bytes 131104 | tf_op jit(solution)/shard_map/ppermute | solution.py:41
  19.6 0.7 %collective-permute-done.4.second = bf16[256,256]{1,0:T(8,128)(2,1)S(1)} collective-permute-done((bf16[256,256]{1,0:T(8,128)(2,1)S(1)}, bf16[256,256]{1,0:T(8,128)(2,1)S(1)}, u32[]{:S(2)}, u32[]{:S(2)}) %collective-permute-start.4) | collective-permute-done | bytes 131104 | tf_op jit(solution)/shard_map/ppermute | solution.py:41
  20.3 1.9 %collective-permute-done.5.third = bf16[256,256]{1,0:T(8,128)(2,1)S(1)} collective-permute-done((bf16[256,256]{1,0:T(8,128)(2,1)S(1)}, bf16[256,256]{1,0:T(8,128)(2,1)S(1)}, u32[]{:S(2)}, u32[]{:S(2)}) %collective-permute-start.5) | collective-permute-done | bytes 131104 | tf_op jit(solution)/shard_map/ppermute | solution.py:41
  22.2 0.6 %pointwise.1 = (bf16[256,256]{1,0:T(8,128)(2,1)S(1)}, bf16[256,256]{1,0:T(8,128)(2,1)S(1)}, bf16[256,256]{1,0:T(8,128)(2,1)S(1)}, bf16[256,256]{1,0:T(8,128)(2,1)S(1)}, f32[1,256]{1,0:T(1,128)S(1)}) custom-call(f32[256,256]{1,0:T(8,128)S(1)} %get-tuple-element.33.mine, bf16[256,256]{1,0:T(8,128)(2,1)S(1)} %collective-permute-done.3.first, ...), custom_call_target="tpu_custom_call" | custom-call | flops 100663296 | bytes 1048576 | tf_op jit(solution)/shard_map/pointwise/pallas_call | solution.py:281
  23.1 1.6 %collective-permute-start.14 = (bf16[72,256]{1,0:T(8,128)(2,1)S(1)}, bf16[72,256]{1,0:T(8,128)(2,1)S(1)}, u32[]{:S(2)}, u32[]{:S(2)}) collective-permute-start(bf16[72,256]{1,0:T(8,128)(2,1)S(1)} %get-tuple-element.51), channel_id=1, source_target_pairs={{0,2},{1,3},{2,0},{3,1},{4,6},{5,7},{6,4},{7,5},{8,10},{9,11},{10,... | collective-permute-start | bytes 110600 | tf_op jit(solution)/shard_map/ppermute | solution.py:46
  25.0 1.6 %collective-permute-start.10 = (bf16[256,256]{1,0:T(8,128)(2,1)S(1)}, bf16[256,256]{1,0:T(8,128)(2,1)S(1)}, u32[]{:S(2)}, u32[]{:S(2)}) collective-permute-start(bf16[256,256]{1,0:T(8,128)(2,1)S(1)} %get-tuple-element.39.local), channel_id=1, source_target_pairs={{0,8},{4,12},{8,16},{12,20},{16,24},{20,28},{24,0},{28,4},{1,9},{5... | collective-permute-start | bytes 393224 | tf_op jit(solution)/shard_map/ppermute | solution.py:41
  26.6 3.0 %collective-permute-start.9 = (bf16[256,256]{1,0:T(8,128)(2,1)S(1)}, bf16[256,256]{1,0:T(8,128)(2,1)S(1)}, u32[]{:S(2)}, u32[]{:S(2)}) collective-permute-start(bf16[256,256]{1,0:T(8,128)(2,1)S(1)} %get-tuple-element.39.local), channel_id=1, source_target_pairs={{0,4},{4,8},{8,12},{12,16},{16,20},{20,24},{24,28},{28,0},{1,5},{5... | collective-permute-start | bytes 393224 | tf_op jit(solution)/shard_map/ppermute | solution.py:41
  29.6 2.7 %collective-permute-start.8 = (bf16[256,256]{1,0:T(8,128)(2,1)S(1)}, bf16[256,256]{1,0:T(8,128)(2,1)S(1)}, u32[]{:S(2)}, u32[]{:S(2)}) collective-permute-start(bf16[256,256]{1,0:T(8,128)(2,1)S(1)} %get-tuple-element.39.local), channel_id=1, source_target_pairs={{0,24},{4,28},{8,0},{12,4},{16,8},{20,12},{24,16},{28,20},{1,25},{... | collective-permute-start | bytes 393224 | tf_op jit(solution)/shard_map/ppermute | solution.py:41
  32.4 0.7 %weight_column_sum.1 = bf16[8,72,256]{2,1,0:T(8,128)(2,1)} custom-call(f32[72,256]{1,0:T(8,128)S(1)} %get-tuple-element.49.mine, bf16[72,256]{1,0:T(8,128)(2,1)S(1)} %collective-permute-done.13.near, bf16[72,256]{1,0:T(8,128)(2,1)S(1)} %collective-permute-done.14.across, bf16[72,256]{1,0:T(8,128)(2,1)S(1)} %collective-permute-done.15.far), custom_call_target="tpu_custom_call" | custom-call | flops 99999997952 | bytes 1048576 | tf_op jit(solution)/shard_map/weight_column_sum/pallas_call | solution.py:301
  33.1 3.6 %all-to-all-start = ((bf16[8,72,256]{2,1,0:T(8,128)(2,1)}), bf16[8,72,256]{2,1,0:T(8,128)(2,1)S(1)}, u32[]{:S(2)}, u32[]{:S(2)}) async-start(bf16[8,72,256]{2,1,0:T(8,128)(2,1)} %weight_column_sum.1), calls=%async_computation | async-start | bytes 589824 | tf_op jit(solution)/shard_map/all_to_all | solution.py:338
  36.7 2.2 %collective-permute-done.9.third = bf16[256,256]{1,0:T(8,128)(2,1)S(1)} collective-permute-done((bf16[256,256]{1,0:T(8,128)(2,1)S(1)}, bf16[256,256]{1,0:T(8,128)(2,1)S(1)}, u32[]{:S(2)}, u32[]{:S(2)}) %collective-permute-start.9) | collective-permute-done | bytes 131104 | tf_op jit(solution)/shard_map/ppermute | solution.py:41
  38.9 1.5 %collective-permute-done.7.first = bf16[256,256]{1,0:T(8,128)(2,1)S(1)} collective-permute-done((bf16[256,256]{1,0:T(8,128)(2,1)S(1)}, bf16[256,256]{1,0:T(8,128)(2,1)S(1)}, u32[]{:S(2)}, u32[]{:S(2)}) %collective-permute-start.7) | collective-permute-done | bytes 131104 | tf_op jit(solution)/shard_map/ppermute | solution.py:41
  40.5 1.5 %source_terms.1 = (f32[256,256]{1,0:T(8,128)S(1)}, f32[256,256]{1,0:T(8,128)S(1)}, bf16[2,256,256]{2,1,0:T(8,128)(2,1)S(1)}) custom-call(s32[1,1]{1,0:T(1,128)S(6)} %copy.12.count, s32[1,1,32]{2,1,0:T(1,128)S(1)} %copy-done.5, s32[1,1,32]{2,1,0:T(1,128)S(1)} %copy-done.7, bf16[1,1,32,128,128]{4,3,2,1,0:T(8,128)(2,1)S(1)} %copy-done.1, ...), custom_call_target="tpu_custom_call" | custom-call | flops 99999997952 | bytes 1048576 | tf_op jit(solution)/shard_map/source_terms/pallas_call | solution.py:315
  42.1 1.5 %collective-permute-done.11.arrived = bf16[2,256,256]{2,1,0:T(8,128)(2,1)S(1)} collective-permute-done((bf16[2,256,256]{2,1,0:T(8,128)(2,1)S(1)}, bf16[2,256,256]{2,1,0:T(8,128)(2,1)S(1)}, u32[]{:S(2)}, u32[]{:S(2)}) %collective-permute-start.11) | collective-permute-done | bytes 262176 | tf_op jit(solution)/shard_map/ppermute | solution.py:46
  43.6 1.6 %collective-permute-start.12 = (bf16[256,256]{1,0:T(8,128)(2,1)S(1)}, bf16[256,256]{1,0:T(8,128)(2,1)S(1)}, u32[]{:S(2)}, u32[]{:S(2)}) collective-permute-start(bf16[256,256]{1,0:T(8,128)(2,1)S(1)} %get-tuple-element.44), channel_id=1, source_target_pairs={{0,2},{1,3},{2,0},{3,1},{4,6},{5,7},{6,4},{7,5},{8,10},{9,11},{10,... | collective-permute-start | bytes 393224 | tf_op jit(solution)/shard_map/ppermute | solution.py:46
  45.2 1.0 %all-to-all-done.received = bf16[8,72,256]{2,1,0:T(8,128)(2,1)S(1)} async-done(((bf16[8,72,256]{2,1,0:T(8,128)(2,1)}), bf16[8,72,256]{2,1,0:T(8,128)(2,1)S(1)}, u32[]{:S(2)}, u32[]{:S(2)}) %all-to-all-start) | async-done | bytes 294944 | tf_op jit(solution)/shard_map/all_to_all | solution.py:338
  46.3 1.5 %collective-permute-start.17 = (bf16[64,256]{1,0:T(8,128)(2,1)S(1)}, bf16[64,256]{1,0:T(8,128)(2,1)S(1)}, u32[]{:S(2)}, u32[]{:S(2)}) collective-permute-start(bf16[64,256]{1,0:T(8,128)(2,1)S(1)} %get-tuple-element.56.own), channel_id=1, source_target_pairs={{0,2},{1,3},{2,0},{3,1},{4,6},{5,7},{6,4},{7,5},{8,10},{9,11},{10,... | collective-permute-start | bytes 98312 | tf_op jit(solution)/shard_map/ppermute | solution.py:46
  47.8 0.3 collective-permute-start.16
  48.1 1.1 %collective-permute-done.12.arrived = bf16[256,256]{1,0:T(8,128)(2,1)S(1)} collective-permute-done((bf16[256,256]{1,0:T(8,128)(2,1)S(1)}, bf16[256,256]{1,0:T(8,128)(2,1)S(1)}, u32[]{:S(2)}, u32[]{:S(2)}) %collective-permute-start.12) | collective-permute-done | bytes 131104 | tf_op jit(solution)/shard_map/ppermute | solution.py:46
  49.2 0.8 %source_sum.1 = (bf16[256,256]{1,0:T(8,128)(2,1)}, bf16[256,256]{1,0:T(8,128)(2,1)}, f32[1,256]{1,0:T(1,128)}) custom-call(f32[256,256]{1,0:T(8,128)S(1)} %get-tuple-element.43.mine, bf16[256,256]{1,0:T(8,128)(2,1)S(1)} %collective-permute-done.12.arrived, bf16[256,256]{1,0:T(8,128)(2,1)S(1)} %get-tuple-element.45.output_in, ...), custom_call_target="tpu_custom_call" | custom-call | flops 99999997952 | bytes 1048576 | tf_op jit(solution)/shard_map/source_sum/pallas_call | solution.py:349
  50.0 0.3 collective-permute-done.17.across
  50.3 0.7 %weight_join.1 = f32[256,256]{1,0:T(8,128)} custom-call(bf16[64,256]{1,0:T(8,128)(2,1)S(1)} %get-tuple-element.56.own, bf16[64,256]{1,0:T(8,128)(2,1)S(1)} %collective-permute-done.16.near, bf16[64,256]{1,0:T(8,128)(2,1)S(1)} %collective-permute-done.17.across, bf16[64,256]{1,0:T(8,128)(2,1)S(1)} %collective-permute-done.18.far), custom_call_target="tpu_custom_call" | custom-call | flops 99999997952 | bytes 1048576 | tf_op jit(solution)/shard_map/weight_join/pallas_call | solution.py:357
  (41 shorter events, 1.2 us)
Async XLA Ops:
  0.6 3.0 %copy-start.10 = (f32[256]{0:T(256)S(1)}, f32[256]{0:T(256)}, u32[]{:S(2)}) copy-start(f32[256]{0:T(256)} %param.10) | copy-start | bytes 3076
  0.6 6.7 %collective-permute-start.1 = (bf16[256,256]{1,0:T(8,128)(2,1)}, bf16[256,256]{1,0:T(8,128)(2,1)S(1)}, u32[]{:S(2)}, u32[]{:S(2)}) collective-permute-start(bf16[256,256]{1,0:T(8,128)(2,1)} %own.1), channel_id=1, source_target_pairs={{0,2},{1,3},{2,0},{3,1},{4,6},{5,7},{6,4},{7,5},{8,10},{9,11},{10,... | collective-permute-start | bytes 393224 | tf_op jit(solution)/shard_map/ppermute | solution.py:46
  3.6 3.7 %collective-permute-start = (bf16[256,256]{1,0:T(8,128)(2,1)}, bf16[256,256]{1,0:T(8,128)(2,1)S(1)}, u32[]{:S(2)}, u32[]{:S(2)}) collective-permute-start(bf16[256,256]{1,0:T(8,128)(2,1)} %own.1), channel_id=1, source_target_pairs={{0,1},{1,0},{2,3},{3,2},{4,5},{5,4},{6,7},{7,6},{8,9},{9,8},{10,11... | collective-permute-start | bytes 393224 | tf_op jit(solution)/shard_map/ppermute | solution.py:46
  3.7 1.2 %copy-start.8 = (bf16[1,1,32,128,128]{4,3,2,1,0:T(8,128)(2,1)S(1)}, bf16[1,1,32,128,128]{4,3,2,1,0:T(8,128)(2,1)}, u32[]{:S(2)}) copy-start(bf16[1,1,32,128,128]{4,3,2,1,0:T(8,128)(2,1)} %values.1) | copy-start | bytes 3145732
  4.9 0.9 %copy-start.9 = (bf16[256,256]{1,0:T(8,128)(2,1)S(1)}, bf16[256,256]{1,0:T(8,128)(2,1)}, u32[]{:S(2)}) copy-start(bf16[256,256]{1,0:T(8,128)(2,1)} %own.1) | copy-start | bytes 393220
  6.1 2.6 %copy-start = (bf16[1,1,32,128,128]{4,3,2,1,0:T(8,128)(2,1)}, bf16[1,1,32,128,128]{4,3,2,1,0:T(8,128)(2,1)S(1)}, u32[]{:S(2)}) copy-start(bf16[1,1,32,128,128]{4,3,2,1,0:T(8,128)(2,1)S(1)} %get-tuple-element.31.values) | copy-start | bytes 3145732
  7.4 1.3 %collective-permute-start.2 = (bf16[256,256]{1,0:T(8,128)(2,1)S(1)}, bf16[256,256]{1,0:T(8,128)(2,1)S(1)}, u32[]{:S(2)}, u32[]{:S(2)}) collective-permute-start(bf16[256,256]{1,0:T(8,128)(2,1)S(1)} %collective-permute-done.1.across), channel_id=1, source_target_pairs={{0,1},{1,0},{2,3},{3,2},{4,5},{5,4},{6,7},{7,6},{8,9},{9,8},{10,11... | collective-permute-start | bytes 393224 | tf_op jit(solution)/shard_map/ppermute | solution.py:46
  7.4 1.3 %copy-start.4 = (s32[1,1,32]{2,1,0:T(1,128)S(1)}, s32[1,1,32]{2,1,0:T(1,128)}, u32[]{:S(2)}) copy-start(s32[1,1,32]{2,1,0:T(1,128)} %target.3) | copy-start | bytes 388
  7.4 1.3 %copy-start.6 = (s32[1,1,32]{2,1,0:T(1,128)S(1)}, s32[1,1,32]{2,1,0:T(1,128)}, u32[]{:S(2)}) copy-start(s32[1,1,32]{2,1,0:T(1,128)} %source.3) | copy-start | bytes 388
  8.7 13.5 %copy-start.2 = (bf16[256,256]{1,0:T(8,128)(2,1)S(1)}, bf16[256,256]{1,0:T(8,128)(2,1)}, u32[]{:S(2)}) copy-start(bf16[256,256]{1,0:T(8,128)(2,1)} %weight.1) | copy-start | bytes 393220
  8.7 13.4 %copy-start.3 = (bf16[256,256]{1,0:T(8,128)(2,1)S(1)}, bf16[256,256]{1,0:T(8,128)(2,1)}, u32[]{:S(2)}) copy-start(bf16[256,256]{1,0:T(8,128)(2,1)} %cotangent.1) | copy-start | bytes 393220
  10.3 9.3 %collective-permute-start.3 = (bf16[256,256]{1,0:T(8,128)(2,1)S(1)}, bf16[256,256]{1,0:T(8,128)(2,1)S(1)}, u32[]{:S(2)}, u32[]{:S(2)}) collective-permute-start(bf16[256,256]{1,0:T(8,128)(2,1)S(1)} %get-tuple-element.34), channel_id=1, source_target_pairs={{0,4},{4,8},{8,12},{12,16},{16,20},{20,24},{24,28},{28,0},{1,5},{5... | collective-permute-start | bytes 393224 | tf_op jit(solution)/shard_map/ppermute | solution.py:41
  12.1 8.2 %collective-permute-start.4 = (bf16[256,256]{1,0:T(8,128)(2,1)S(1)}, bf16[256,256]{1,0:T(8,128)(2,1)S(1)}, u32[]{:S(2)}, u32[]{:S(2)}) collective-permute-start(bf16[256,256]{1,0:T(8,128)(2,1)S(1)} %get-tuple-element.35), channel_id=1, source_target_pairs={{0,8},{4,12},{8,16},{12,20},{16,24},{20,28},{24,0},{28,4},{1,9},{5... | collective-permute-start | bytes 393224 | tf_op jit(solution)/shard_map/ppermute | solution.py:41
  13.7 8.5 %collective-permute-start.5 = (bf16[256,256]{1,0:T(8,128)(2,1)S(1)}, bf16[256,256]{1,0:T(8,128)(2,1)S(1)}, u32[]{:S(2)}, u32[]{:S(2)}) collective-permute-start(bf16[256,256]{1,0:T(8,128)(2,1)S(1)} %get-tuple-element.36), channel_id=1, source_target_pairs={{0,24},{4,28},{8,0},{12,4},{16,8},{20,12},{24,16},{28,20},{1,25},{... | collective-permute-start | bytes 393224 | tf_op jit(solution)/shard_map/ppermute | solution.py:41
  15.9 6.3 %collective-permute-start.6 = (bf16[256,256]{1,0:T(8,128)(2,1)S(1)}, bf16[256,256]{1,0:T(8,128)(2,1)S(1)}, u32[]{:S(2)}, u32[]{:S(2)}) collective-permute-start(bf16[256,256]{1,0:T(8,128)(2,1)S(1)} %get-tuple-element.37), channel_id=1, source_target_pairs={{0,28},{4,0},{8,4},{12,8},{16,12},{20,16},{24,20},{28,24},{1,29},{... | collective-permute-start | bytes 393224 | tf_op jit(solution)/shard_map/ppermute | solution.py:41
  23.0 6.6 %collective-permute-start.13 = (bf16[72,256]{1,0:T(8,128)(2,1)S(1)}, bf16[72,256]{1,0:T(8,128)(2,1)S(1)}, u32[]{:S(2)}, u32[]{:S(2)}) collective-permute-start(bf16[72,256]{1,0:T(8,128)(2,1)S(1)} %get-tuple-element.50), channel_id=1, source_target_pairs={{0,1},{1,0},{2,3},{3,2},{4,5},{5,4},{6,7},{7,6},{8,9},{9,8},{10,11... | collective-permute-start | bytes 110600 | tf_op jit(solution)/shard_map/ppermute | solution.py:46
  23.1 9.2 %collective-permute-start.14 = (bf16[72,256]{1,0:T(8,128)(2,1)S(1)}, bf16[72,256]{1,0:T(8,128)(2,1)S(1)}, u32[]{:S(2)}, u32[]{:S(2)}) collective-permute-start(bf16[72,256]{1,0:T(8,128)(2,1)S(1)} %get-tuple-element.51), channel_id=1, source_target_pairs={{0,2},{1,3},{2,0},{3,1},{4,6},{5,7},{6,4},{7,5},{8,10},{9,11},{10,... | collective-permute-start | bytes 110600 | tf_op jit(solution)/shard_map/ppermute | solution.py:46
  24.6 7.7 %collective-permute-start.15 = (bf16[72,256]{1,0:T(8,128)(2,1)S(1)}, bf16[72,256]{1,0:T(8,128)(2,1)S(1)}, u32[]{:S(2)}, u32[]{:S(2)}) collective-permute-start(bf16[72,256]{1,0:T(8,128)(2,1)S(1)} %get-tuple-element.52), channel_id=1, source_target_pairs={{0,3},{1,2},{2,1},{3,0},{4,7},{5,6},{6,5},{7,4},{8,11},{9,10},{10,... | collective-permute-start | bytes 110600 | tf_op jit(solution)/shard_map/ppermute | solution.py:46
  25.0 11.7 %collective-permute-start.10 = (bf16[256,256]{1,0:T(8,128)(2,1)S(1)}, bf16[256,256]{1,0:T(8,128)(2,1)S(1)}, u32[]{:S(2)}, u32[]{:S(2)}) collective-permute-start(bf16[256,256]{1,0:T(8,128)(2,1)S(1)} %get-tuple-element.39.local), channel_id=1, source_target_pairs={{0,8},{4,12},{8,16},{12,20},{16,24},{20,28},{24,0},{28,4},{1,9},{5... | collective-permute-start | bytes 393224 | tf_op jit(solution)/shard_map/ppermute | solution.py:41
  26.6 12.3 %collective-permute-start.9 = (bf16[256,256]{1,0:T(8,128)(2,1)S(1)}, bf16[256,256]{1,0:T(8,128)(2,1)S(1)}, u32[]{:S(2)}, u32[]{:S(2)}) collective-permute-start(bf16[256,256]{1,0:T(8,128)(2,1)S(1)} %get-tuple-element.39.local), channel_id=1, source_target_pairs={{0,4},{4,8},{8,12},{12,16},{16,20},{20,24},{24,28},{28,0},{1,5},{5... | collective-permute-start | bytes 393224 | tf_op jit(solution)/shard_map/ppermute | solution.py:41
  29.6 9.3 %collective-permute-start.8 = (bf16[256,256]{1,0:T(8,128)(2,1)S(1)}, bf16[256,256]{1,0:T(8,128)(2,1)S(1)}, u32[]{:S(2)}, u32[]{:S(2)}) collective-permute-start(bf16[256,256]{1,0:T(8,128)(2,1)S(1)} %get-tuple-element.39.local), channel_id=1, source_target_pairs={{0,24},{4,28},{8,0},{12,4},{16,8},{20,12},{24,16},{28,20},{1,25},{... | collective-permute-start | bytes 393224 | tf_op jit(solution)/shard_map/ppermute | solution.py:41
  32.3 8.1 %collective-permute-start.7 = (bf16[256,256]{1,0:T(8,128)(2,1)S(1)}, bf16[256,256]{1,0:T(8,128)(2,1)S(1)}, u32[]{:S(2)}, u32[]{:S(2)}) collective-permute-start(bf16[256,256]{1,0:T(8,128)(2,1)S(1)} %get-tuple-element.39.local), channel_id=1, source_target_pairs={{0,28},{4,0},{8,4},{12,8},{16,12},{20,16},{24,20},{28,24},{1,29},{... | collective-permute-start | bytes 393224 | tf_op jit(solution)/shard_map/ppermute | solution.py:41
  32.3 8.1 %copy-start.1 = (bf16[1,1,32,128,128]{4,3,2,1,0:T(8,128)(2,1)S(1)}, bf16[1,1,32,128,128]{4,3,2,1,0:T(8,128)(2,1)}, u32[]{:S(2)}) copy-start(bf16[1,1,32,128,128]{4,3,2,1,0:T(8,128)(2,1)} %copy-done) | copy-start | bytes 3145732
  33.1 7.4 %copy-start.5 = (s32[1,1,32]{2,1,0:T(1,128)S(1)}, s32[1,1,32]{2,1,0:T(1,128)}, u32[]{:S(2)}) copy-start(s32[1,1,32]{2,1,0:T(1,128)} %target.3) | copy-start | bytes 388
  33.1 7.4 %copy-start.7 = (s32[1,1,32]{2,1,0:T(1,128)S(1)}, s32[1,1,32]{2,1,0:T(1,128)}, u32[]{:S(2)}) copy-start(s32[1,1,32]{2,1,0:T(1,128)} %source.3) | copy-start | bytes 388
  33.1 13.0 %all-to-all-start = ((bf16[8,72,256]{2,1,0:T(8,128)(2,1)}), bf16[8,72,256]{2,1,0:T(8,128)(2,1)S(1)}, u32[]{:S(2)}, u32[]{:S(2)}) async-start(bf16[8,72,256]{2,1,0:T(8,128)(2,1)} %weight_column_sum.1), calls=%async_computation | async-start | bytes 589824 | tf_op jit(solution)/shard_map/all_to_all | solution.py:338
  42.0 1.6 %collective-permute-start.11 = (bf16[2,256,256]{2,1,0:T(8,128)(2,1)S(1)}, bf16[2,256,256]{2,1,0:T(8,128)(2,1)S(1)}, u32[]{:S(2)}, u32[]{:S(2)}) collective-permute-start(bf16[2,256,256]{2,1,0:T(8,128)(2,1)S(1)} %get-tuple-element.42), channel_id=1, source_target_pairs={{0,1},{1,0},{2,3},{3,2},{4,5},{5,4},{6,7},{7,6},{8,9},{9,8},{10,11... | collective-permute-start | bytes 786440 | tf_op jit(solution)/shard_map/ppermute | solution.py:46
  43.6 5.6 %collective-permute-start.12 = (bf16[256,256]{1,0:T(8,128)(2,1)S(1)}, bf16[256,256]{1,0:T(8,128)(2,1)S(1)}, u32[]{:S(2)}, u32[]{:S(2)}) collective-permute-start(bf16[256,256]{1,0:T(8,128)(2,1)S(1)} %get-tuple-element.44), channel_id=1, source_target_pairs={{0,2},{1,3},{2,0},{3,1},{4,6},{5,7},{6,4},{7,5},{8,10},{9,11},{10,... | collective-permute-start | bytes 393224 | tf_op jit(solution)/shard_map/ppermute | solution.py:46
  46.2 3.8 %collective-permute-start.18 = (bf16[64,256]{1,0:T(8,128)(2,1)S(1)}, bf16[64,256]{1,0:T(8,128)(2,1)S(1)}, u32[]{:S(2)}, u32[]{:S(2)}) collective-permute-start(bf16[64,256]{1,0:T(8,128)(2,1)S(1)} %get-tuple-element.56.own), channel_id=1, source_target_pairs={{0,3},{1,2},{2,1},{3,0},{4,7},{5,6},{6,5},{7,4},{8,11},{9,10},{10,... | collective-permute-start | bytes 98312 | tf_op jit(solution)/shard_map/ppermute | solution.py:46
  46.3 4.0 %collective-permute-start.17 = (bf16[64,256]{1,0:T(8,128)(2,1)S(1)}, bf16[64,256]{1,0:T(8,128)(2,1)S(1)}, u32[]{:S(2)}, u32[]{:S(2)}) collective-permute-start(bf16[64,256]{1,0:T(8,128)(2,1)S(1)} %get-tuple-element.56.own), channel_id=1, source_target_pairs={{0,2},{1,3},{2,0},{3,1},{4,6},{5,7},{6,4},{7,5},{8,10},{9,11},{10,... | collective-permute-start | bytes 98312 | tf_op jit(solution)/shard_map/ppermute | solution.py:46
  47.8 2.5 %collective-permute-start.16 = (bf16[64,256]{1,0:T(8,128)(2,1)S(1)}, bf16[64,256]{1,0:T(8,128)(2,1)S(1)}, u32[]{:S(2)}, u32[]{:S(2)}) collective-permute-start(bf16[64,256]{1,0:T(8,128)(2,1)S(1)} %get-tuple-element.56.own), channel_id=1, source_target_pairs={{0,1},{1,0},{2,3},{3,2},{4,5},{5,4},{6,7},{7,6},{8,9},{9,8},{10,11... | collective-permute-start | bytes 98312 | tf_op jit(solution)/shard_map/ppermute | solution.py:46

commit v7 on v6

--- a/solution.py
+++ b/solution.py
@@ -15,7 +15,6 @@
 TAIL = 8
 FORWARD = ((1, None), (2, None), (-2, None), (-1, None))
 BACKWARD = ((-1, None), (-2, None), (1, None), (2, None))
-SLOT_GROUP = 32
 LONG = 10**11
 VMEM = pltpu.VMEM
 SMEM = pltpu.SMEM
@@ -64,11 +63,12 @@
 
 
 def for_slots(slot_total, live, step):
-    for start in range(0, slot_total, SLOT_GROUP):
+    split = slot_total * 3 // 4
+    for start, stop in ((0, split), (split, slot_total)):
 
         @pl.when(start < live)
         def _group():
-            for slot in range(start, min(start + SLOT_GROUP, slot_total)):
+            for slot in range(start, stop):
                 step(slot)
 
 

time: 51.3 us -> 51.2 us (level)
  transfers between devices with their start and end apart: 20 -> 20, of which waited for: 11 -> 12; matrix products, arithmetic and copies ran while one was open for 0% -> 0% of each run, Pallas kernels for 7% -> 6%
where the time goes in v7:
time: 51.2 us; the launch traced here: 50.9 us
  starting transfers between devices  26.4 us (52%)
  waiting for transfers between devices  14.7 us (29%)
  Pallas kernels  6.18 us (12%)
  local copies, waits for them, and re-layouts  2.17 us (4%)
  between operations  1.46 us (3%)
    ppermute x8, starting transfers between devices, routed(): return lax.ppermute(block, 'row', pairs)  14.3 us
    ppermute x8, waiting for transfers between devices, routed(): return lax.ppermute(block, 'row', pairs)  8.73 us
    ppermute x11, starting transfers between devices, swapped(): return lax.ppermute(block, axis, [(i, i ^ bit) for i in range(size)])  8.49 us
    ppermute x11, waiting for transfers between devices, swapped(): return lax.ppermute(block, axis, [(i, i ^ bit) for i in range(size)])  4.87 us
    all_to_all x1, starting transfers between devices, shards(): received = lax.all_to_all(message, 'row', 0, 0, tiled=True)  3.55 us
    unnamed x22, local copies, waits for them, and re-layouts  2.17 us
    pallas_call x1, Pallas kernels, shards(): call(backward_kernel, [tall, tall, jax.ShapeDtypeStruct((2, width, own_ro...  1.37 us
    pallas_call x1, Pallas kernels, shards(): call(forward_kernel, [wide] + [whole] * 4, [pltpu.VMEM((sources, BLK, wid...  1.36 us
  transfers between devices with their start and end apart: 20, of which 12 were waited for; matrix products, arithmetic and copies ran while one was open for 0% of the time, Pallas kernels for 6%

profile of v7, /device:TPU:0, one launch (start us, length us, event | category | flops | bytes accessed | tf_op | source)
XLA Modules:
  0.0 50.9 jit_solution(15125347832667966682)
XLA Ops:
  0.6 3.0 %collective-permute-start.1 = (bf16[256,256]{1,0:T(8,128)(2,1)}, bf16[256,256]{1,0:T(8,128)(2,1)S(1)}, u32[]{:S(2)}, u32[]{:S(2)}) collective-permute-start(bf16[256,256]{1,0:T(8,128)(2,1)} %own.1), channel_id=1, source_target_pairs={{0,2},{1,3},{2,0},{3,1},{4,6},{5,7},{6,4},{7,5},{8,10},{9,11},{10,... | collective-permute-start | bytes 393224 | tf_op jit(solution)/shard_map/ppermute | solution.py:45
  3.7 1.2 %copy-done.8 = bf16[1,1,32,128,128]{4,3,2,1,0:T(8,128)(2,1)S(1)} copy-done((bf16[1,1,32,128,128]{4,3,2,1,0:T(8,128)(2,1)S(1)}, bf16[1,1,32,128,128]{4,3,2,1,0:T(8,128)(2,1)}, u32[]{:S(2)}) %copy-start.8) | copy-done | bytes 1048600
  4.9 0.9 %copy-done.9 = bf16[256,256]{1,0:T(8,128)(2,1)S(1)} copy-done((bf16[256,256]{1,0:T(8,128)(2,1)S(1)}, bf16[256,256]{1,0:T(8,128)(2,1)}, u32[]{:S(2)}) %copy-start.9) | copy-done | bytes 131096
  6.7 0.6 %collective-permute-done.1.across = bf16[256,256]{1,0:T(8,128)(2,1)S(1)} collective-permute-done((bf16[256,256]{1,0:T(8,128)(2,1)}, bf16[256,256]{1,0:T(8,128)(2,1)S(1)}, u32[]{:S(2)}, u32[]{:S(2)}) %collective-permute-start.1) | collective-permute-done | bytes 131104 | tf_op jit(solution)/shard_map/ppermute | solution.py:45
  7.4 1.3 %collective-permute-done.2.far = bf16[256,256]{1,0:T(8,128)(2,1)S(1)} collective-permute-done((bf16[256,256]{1,0:T(8,128)(2,1)S(1)}, bf16[256,256]{1,0:T(8,128)(2,1)S(1)}, u32[]{:S(2)}, u32[]{:S(2)}) %collective-permute-start.2) | collective-permute-done | bytes 131104 | tf_op jit(solution)/shard_map/ppermute | solution.py:45
  8.7 1.4 %aggregate_terms.1 = (f32[256,256]{1,0:T(8,128)S(1)}, bf16[256,256]{1,0:T(8,128)(2,1)S(1)}, bf16[256,256]{1,0:T(8,128)(2,1)S(1)}, bf16[256,256]{1,0:T(8,128)(2,1)S(1)}, bf16[256,256]{1,0:T(8,128)(2,1)S(1)}) custom-call(s32[1,1]{1,0:T(1,128)S(6)} %copy.12.count, s32[1,1,32]{2,1,0:T(1,128)S(1)} %copy-done.4, s32[1,1,32]{2,1,0:T(1,128)S(1)} %copy-done.6, ...), custom_call_target="tpu_custom_call" | custom-call | flops 268435456 | bytes 1048576 | tf_op jit(solution)/shard_map/aggregate_terms/pallas_call | solution.py:267
  10.1 1.8 %collective-permute-start.3 = (bf16[256,256]{1,0:T(8,128)(2,1)S(1)}, bf16[256,256]{1,0:T(8,128)(2,1)S(1)}, u32[]{:S(2)}, u32[]{:S(2)}) collective-permute-start(bf16[256,256]{1,0:T(8,128)(2,1)S(1)} %get-tuple-element.34), channel_id=1, source_target_pairs={{0,4},{4,8},{8,12},{12,16},{16,20},{20,24},{24,28},{28,0},{1,5},{5... | collective-permute-start | bytes 393224 | tf_op jit(solution)/shard_map/ppermute | solution.py:40
  11.9 1.6 %collective-permute-start.4 = (bf16[256,256]{1,0:T(8,128)(2,1)S(1)}, bf16[256,256]{1,0:T(8,128)(2,1)S(1)}, u32[]{:S(2)}, u32[]{:S(2)}) collective-permute-start(bf16[256,256]{1,0:T(8,128)(2,1)S(1)} %get-tuple-element.35), channel_id=1, source_target_pairs={{0,8},{4,12},{8,16},{12,20},{16,24},{20,28},{24,0},{28,4},{1,9},{5... | collective-permute-start | bytes 393224 | tf_op jit(solution)/shard_map/ppermute | solution.py:40
  13.5 2.2 %collective-permute-start.5 = (bf16[256,256]{1,0:T(8,128)(2,1)S(1)}, bf16[256,256]{1,0:T(8,128)(2,1)S(1)}, u32[]{:S(2)}, u32[]{:S(2)}) collective-permute-start(bf16[256,256]{1,0:T(8,128)(2,1)S(1)} %get-tuple-element.36), channel_id=1, source_target_pairs={{0,24},{4,28},{8,0},{12,4},{16,8},{20,12},{24,16},{28,20},{1,25},{... | collective-permute-start | bytes 393224 | tf_op jit(solution)/shard_map/ppermute | solution.py:40
  15.8 1.3 %collective-permute-start.6 = (bf16[256,256]{1,0:T(8,128)(2,1)S(1)}, bf16[256,256]{1,0:T(8,128)(2,1)S(1)}, u32[]{:S(2)}, u32[]{:S(2)}) collective-permute-start(bf16[256,256]{1,0:T(8,128)(2,1)S(1)} %get-tuple-element.37), channel_id=1, source_target_pairs={{0,28},{4,0},{8,4},{12,8},{16,12},{20,16},{24,20},{28,24},{1,29},{... | collective-permute-start | bytes 393224 | tf_op jit(solution)/shard_map/ppermute | solution.py:40
  17.1 2.3 %collective-permute-done.3.first = bf16[256,256]{1,0:T(8,128)(2,1)S(1)} collective-permute-done((bf16[256,256]{1,0:T(8,128)(2,1)S(1)}, bf16[256,256]{1,0:T(8,128)(2,1)S(1)}, u32[]{:S(2)}, u32[]{:S(2)}) %collective-permute-start.3) | collective-permute-done | bytes 131104 | tf_op jit(solution)/shard_map/ppermute | solution.py:40
  19.4 0.7 %collective-permute-done.4.second = bf16[256,256]{1,0:T(8,128)(2,1)S(1)} collective-permute-done((bf16[256,256]{1,0:T(8,128)(2,1)S(1)}, bf16[256,256]{1,0:T(8,128)(2,1)S(1)}, u32[]{:S(2)}, u32[]{:S(2)}) %collective-permute-start.4) | collective-permute-done | bytes 131104 | tf_op jit(solution)/shard_map/ppermute | solution.py:40
  20.1 1.9 %collective-permute-done.5.third = bf16[256,256]{1,0:T(8,128)(2,1)S(1)} collective-permute-done((bf16[256,256]{1,0:T(8,128)(2,1)S(1)}, bf16[256,256]{1,0:T(8,128)(2,1)S(1)}, u32[]{:S(2)}, u32[]{:S(2)}) %collective-permute-start.5) | collective-permute-done | bytes 131104 | tf_op jit(solution)/shard_map/ppermute | solution.py:40
  22.0 0.6 %pointwise.1 = (bf16[256,256]{1,0:T(8,128)(2,1)S(1)}, bf16[256,256]{1,0:T(8,128)(2,1)S(1)}, bf16[256,256]{1,0:T(8,128)(2,1)S(1)}, bf16[256,256]{1,0:T(8,128)(2,1)S(1)}, f32[1,256]{1,0:T(1,128)S(1)}) custom-call(f32[256,256]{1,0:T(8,128)S(1)} %get-tuple-element.33.mine, bf16[256,256]{1,0:T(8,128)(2,1)S(1)} %collective-permute-done.3.first, ...), custom_call_target="tpu_custom_call" | custom-call | flops 100663296 | bytes 1048576 | tf_op jit(solution)/shard_map/pointwise/pallas_call | solution.py:281
  22.9 1.6 %collective-permute-start.14 = (bf16[72,256]{1,0:T(8,128)(2,1)S(1)}, bf16[72,256]{1,0:T(8,128)(2,1)S(1)}, u32[]{:S(2)}, u32[]{:S(2)}) collective-permute-start(bf16[72,256]{1,0:T(8,128)(2,1)S(1)} %get-tuple-element.51), channel_id=1, source_target_pairs={{0,2},{1,3},{2,0},{3,1},{4,6},{5,7},{6,4},{7,5},{8,10},{9,11},{10,... | collective-permute-start | bytes 110600 | tf_op jit(solution)/shard_map/ppermute | solution.py:45
  24.8 1.6 %collective-permute-start.10 = (bf16[256,256]{1,0:T(8,128)(2,1)S(1)}, bf16[256,256]{1,0:T(8,128)(2,1)S(1)}, u32[]{:S(2)}, u32[]{:S(2)}) collective-permute-start(bf16[256,256]{1,0:T(8,128)(2,1)S(1)} %get-tuple-element.39.local), channel_id=1, source_target_pairs={{0,8},{4,12},{8,16},{12,20},{16,24},{20,28},{24,0},{28,4},{1,9},{5... | collective-permute-start | bytes 393224 | tf_op jit(solution)/shard_map/ppermute | solution.py:40
  26.4 3.0 %collective-permute-start.9 = (bf16[256,256]{1,0:T(8,128)(2,1)S(1)}, bf16[256,256]{1,0:T(8,128)(2,1)S(1)}, u32[]{:S(2)}, u32[]{:S(2)}) collective-permute-start(bf16[256,256]{1,0:T(8,128)(2,1)S(1)} %get-tuple-element.39.local), channel_id=1, source_target_pairs={{0,4},{4,8},{8,12},{12,16},{16,20},{20,24},{24,28},{28,0},{1,5},{5... | collective-permute-start | bytes 393224 | tf_op jit(solution)/shard_map/ppermute | solution.py:40
  29.5 2.7 %collective-permute-start.8 = (bf16[256,256]{1,0:T(8,128)(2,1)S(1)}, bf16[256,256]{1,0:T(8,128)(2,1)S(1)}, u32[]{:S(2)}, u32[]{:S(2)}) collective-permute-start(bf16[256,256]{1,0:T(8,128)(2,1)S(1)} %get-tuple-element.39.local), channel_id=1, source_target_pairs={{0,24},{4,28},{8,0},{12,4},{16,8},{20,12},{24,16},{28,20},{1,25},{... | collective-permute-start | bytes 393224 | tf_op jit(solution)/shard_map/ppermute | solution.py:40
  32.2 0.7 %weight_column_sum.1 = bf16[8,72,256]{2,1,0:T(8,128)(2,1)} custom-call(f32[72,256]{1,0:T(8,128)S(1)} %get-tuple-element.49.mine, bf16[72,256]{1,0:T(8,128)(2,1)S(1)} %collective-permute-done.13.near, bf16[72,256]{1,0:T(8,128)(2,1)S(1)} %collective-permute-done.14.across, bf16[72,256]{1,0:T(8,128)(2,1)S(1)} %collective-permute-done.15.far), custom_call_target="tpu_custom_call" | custom-call | flops 99999997952 | bytes 1048576 | tf_op jit(solution)/shard_map/weight_column_sum/pallas_call | solution.py:301
  33.0 3.6 %all-to-all-start = ((bf16[8,72,256]{2,1,0:T(8,128)(2,1)}), bf16[8,72,256]{2,1,0:T(8,128)(2,1)S(1)}, u32[]{:S(2)}, u32[]{:S(2)}) async-start(bf16[8,72,256]{2,1,0:T(8,128)(2,1)} %weight_column_sum.1), calls=%async_computation | async-start | bytes 589824 | tf_op jit(solution)/shard_map/all_to_all | solution.py:338
  36.5 2.2 %collective-permute-done.9.third = bf16[256,256]{1,0:T(8,128)(2,1)S(1)} collective-permute-done((bf16[256,256]{1,0:T(8,128)(2,1)S(1)}, bf16[256,256]{1,0:T(8,128)(2,1)S(1)}, u32[]{:S(2)}, u32[]{:S(2)}) %collective-permute-start.9) | collective-permute-done | bytes 131104 | tf_op jit(solution)/shard_map/ppermute | solution.py:40
  38.8 1.5 %collective-permute-done.7.first = bf16[256,256]{1,0:T(8,128)(2,1)S(1)} collective-permute-done((bf16[256,256]{1,0:T(8,128)(2,1)S(1)}, bf16[256,256]{1,0:T(8,128)(2,1)S(1)}, u32[]{:S(2)}, u32[]{:S(2)}) %collective-permute-start.7) | collective-permute-done | bytes 131104 | tf_op jit(solution)/shard_map/ppermute | solution.py:40
  40.3 1.4 %source_terms.1 = (f32[256,256]{1,0:T(8,128)S(1)}, f32[256,256]{1,0:T(8,128)S(1)}, bf16[2,256,256]{2,1,0:T(8,128)(2,1)S(1)}) custom-call(s32[1,1]{1,0:T(1,128)S(6)} %copy.12.count, s32[1,1,32]{2,1,0:T(1,128)S(1)} %copy-done.5, s32[1,1,32]{2,1,0:T(1,128)S(1)} %copy-done.7, bf16[1,1,32,128,128]{4,3,2,1,0:T(8,128)(2,1)S(1)} %copy-done.1, ...), custom_call_target="tpu_custom_call" | custom-call | flops 99999997952 | bytes 1048576 | tf_op jit(solution)/shard_map/source_terms/pallas_call | solution.py:315
  41.8 1.5 %collective-permute-done.11.arrived = bf16[2,256,256]{2,1,0:T(8,128)(2,1)S(1)} collective-permute-done((bf16[2,256,256]{2,1,0:T(8,128)(2,1)S(1)}, bf16[2,256,256]{2,1,0:T(8,128)(2,1)S(1)}, u32[]{:S(2)}, u32[]{:S(2)}) %collective-permute-start.11) | collective-permute-done | bytes 262176 | tf_op jit(solution)/shard_map/ppermute | solution.py:45
  43.3 1.6 %collective-permute-start.12 = (bf16[256,256]{1,0:T(8,128)(2,1)S(1)}, bf16[256,256]{1,0:T(8,128)(2,1)S(1)}, u32[]{:S(2)}, u32[]{:S(2)}) collective-permute-start(bf16[256,256]{1,0:T(8,128)(2,1)S(1)} %get-tuple-element.44), channel_id=1, source_target_pairs={{0,2},{1,3},{2,0},{3,1},{4,6},{5,7},{6,4},{7,5},{8,10},{9,11},{10,... | collective-permute-start | bytes 393224 | tf_op jit(solution)/shard_map/ppermute | solution.py:45
  44.9 1.1 %all-to-all-done.received = bf16[8,72,256]{2,1,0:T(8,128)(2,1)S(1)} async-done(((bf16[8,72,256]{2,1,0:T(8,128)(2,1)}), bf16[8,72,256]{2,1,0:T(8,128)(2,1)S(1)}, u32[]{:S(2)}, u32[]{:S(2)}) %all-to-all-start) | async-done | bytes 294944 | tf_op jit(solution)/shard_map/all_to_all | solution.py:338
  46.1 1.5 %collective-permute-start.17 = (bf16[64,256]{1,0:T(8,128)(2,1)S(1)}, bf16[64,256]{1,0:T(8,128)(2,1)S(1)}, u32[]{:S(2)}, u32[]{:S(2)}) collective-permute-start(bf16[64,256]{1,0:T(8,128)(2,1)S(1)} %get-tuple-element.56.own), channel_id=1, source_target_pairs={{0,2},{1,3},{2,0},{3,1},{4,6},{5,7},{6,4},{7,5},{8,10},{9,11},{10,... | collective-permute-start | bytes 98312 | tf_op jit(solution)/shard_map/ppermute | solution.py:45
  47.6 0.3 collective-permute-start.16
  48.0 1.0 %collective-permute-done.12.arrived = bf16[256,256]{1,0:T(8,128)(2,1)S(1)} collective-permute-done((bf16[256,256]{1,0:T(8,128)(2,1)S(1)}, bf16[256,256]{1,0:T(8,128)(2,1)S(1)}, u32[]{:S(2)}, u32[]{:S(2)}) %collective-permute-start.12) | collective-permute-done | bytes 131104 | tf_op jit(solution)/shard_map/ppermute | solution.py:45
  48.9 0.8 %source_sum.1 = (bf16[256,256]{1,0:T(8,128)(2,1)}, bf16[256,256]{1,0:T(8,128)(2,1)}, f32[1,256]{1,0:T(1,128)}) custom-call(f32[256,256]{1,0:T(8,128)S(1)} %get-tuple-element.43.mine, bf16[256,256]{1,0:T(8,128)(2,1)S(1)} %collective-permute-done.12.arrived, bf16[256,256]{1,0:T(8,128)(2,1)S(1)} %get-tuple-element.45.output_in, ...), custom_call_target="tpu_custom_call" | custom-call | flops 99999997952 | bytes 1048576 | tf_op jit(solution)/shard_map/source_sum/pallas_call | solution.py:349
  49.8 0.4 collective-permute-done.17.across
  50.2 0.7 %weight_join.1 = f32[256,256]{1,0:T(8,128)} custom-call(bf16[64,256]{1,0:T(8,128)(2,1)S(1)} %get-tuple-element.56.own, bf16[64,256]{1,0:T(8,128)(2,1)S(1)} %collective-permute-done.16.near, bf16[64,256]{1,0:T(8,128)(2,1)S(1)} %collective-permute-done.17.across, bf16[64,256]{1,0:T(8,128)(2,1)S(1)} %collective-permute-done.18.far), custom_call_target="tpu_custom_call" | custom-call | flops 99999997952 | bytes 1048576 | tf_op jit(solution)/shard_map/weight_join/pallas_call | solution.py:357
  (41 shorter events, 1.3 us)
Async XLA Ops:
  0.6 3.0 %copy-start.10 = (f32[256]{0:T(256)S(1)}, f32[256]{0:T(256)}, u32[]{:S(2)}) copy-start(f32[256]{0:T(256)} %param.10) | copy-start | bytes 3076
  0.6 6.7 %collective-permute-start.1 = (bf16[256,256]{1,0:T(8,128)(2,1)}, bf16[256,256]{1,0:T(8,128)(2,1)S(1)}, u32[]{:S(2)}, u32[]{:S(2)}) collective-permute-start(bf16[256,256]{1,0:T(8,128)(2,1)} %own.1), channel_id=1, source_target_pairs={{0,2},{1,3},{2,0},{3,1},{4,6},{5,7},{6,4},{7,5},{8,10},{9,11},{10,... | collective-permute-start | bytes 393224 | tf_op jit(solution)/shard_map/ppermute | solution.py:45
  3.6 3.7 %collective-permute-start = (bf16[256,256]{1,0:T(8,128)(2,1)}, bf16[256,256]{1,0:T(8,128)(2,1)S(1)}, u32[]{:S(2)}, u32[]{:S(2)}) collective-permute-start(bf16[256,256]{1,0:T(8,128)(2,1)} %own.1), channel_id=1, source_target_pairs={{0,1},{1,0},{2,3},{3,2},{4,5},{5,4},{6,7},{7,6},{8,9},{9,8},{10,11... | collective-permute-start | bytes 393224 | tf_op jit(solution)/shard_map/ppermute | solution.py:45
  3.7 1.2 %copy-start.8 = (bf16[1,1,32,128,128]{4,3,2,1,0:T(8,128)(2,1)S(1)}, bf16[1,1,32,128,128]{4,3,2,1,0:T(8,128)(2,1)}, u32[]{:S(2)}) copy-start(bf16[1,1,32,128,128]{4,3,2,1,0:T(8,128)(2,1)} %values.1) | copy-start | bytes 3145732
  4.9 0.9 %copy-start.9 = (bf16[256,256]{1,0:T(8,128)(2,1)S(1)}, bf16[256,256]{1,0:T(8,128)(2,1)}, u32[]{:S(2)}) copy-start(bf16[256,256]{1,0:T(8,128)(2,1)} %own.1) | copy-start | bytes 393220
  6.1 2.6 %copy-start = (bf16[1,1,32,128,128]{4,3,2,1,0:T(8,128)(2,1)}, bf16[1,1,32,128,128]{4,3,2,1,0:T(8,128)(2,1)S(1)}, u32[]{:S(2)}) copy-start(bf16[1,1,32,128,128]{4,3,2,1,0:T(8,128)(2,1)S(1)} %get-tuple-element.31.values) | copy-start | bytes 3145732
  7.4 1.3 %collective-permute-start.2 = (bf16[256,256]{1,0:T(8,128)(2,1)S(1)}, bf16[256,256]{1,0:T(8,128)(2,1)S(1)}, u32[]{:S(2)}, u32[]{:S(2)}) collective-permute-start(bf16[256,256]{1,0:T(8,128)(2,1)S(1)} %collective-permute-done.1.across), channel_id=1, source_target_pairs={{0,1},{1,0},{2,3},{3,2},{4,5},{5,4},{6,7},{7,6},{8,9},{9,8},{10,11... | collective-permute-start | bytes 393224 | tf_op jit(solution)/shard_map/ppermute | solution.py:45
  7.4 1.3 %copy-start.4 = (s32[1,1,32]{2,1,0:T(1,128)S(1)}, s32[1,1,32]{2,1,0:T(1,128)}, u32[]{:S(2)}) copy-start(s32[1,1,32]{2,1,0:T(1,128)} %target.3) | copy-start | bytes 388
  7.4 1.3 %copy-start.6 = (s32[1,1,32]{2,1,0:T(1,128)S(1)}, s32[1,1,32]{2,1,0:T(1,128)}, u32[]{:S(2)}) copy-start(s32[1,1,32]{2,1,0:T(1,128)} %source.3) | copy-start | bytes 388
  8.7 13.3 %copy-start.2 = (bf16[256,256]{1,0:T(8,128)(2,1)S(1)}, bf16[256,256]{1,0:T(8,128)(2,1)}, u32[]{:S(2)}) copy-start(bf16[256,256]{1,0:T(8,128)(2,1)} %weight.1) | copy-start | bytes 393220
  8.7 13.3 %copy-start.3 = (bf16[256,256]{1,0:T(8,128)(2,1)S(1)}, bf16[256,256]{1,0:T(8,128)(2,1)}, u32[]{:S(2)}) copy-start(bf16[256,256]{1,0:T(8,128)(2,1)} %cotangent.1) | copy-start | bytes 393220
  10.1 9.3 %collective-permute-start.3 = (bf16[256,256]{1,0:T(8,128)(2,1)S(1)}, bf16[256,256]{1,0:T(8,128)(2,1)S(1)}, u32[]{:S(2)}, u32[]{:S(2)}) collective-permute-start(bf16[256,256]{1,0:T(8,128)(2,1)S(1)} %get-tuple-element.34), channel_id=1, source_target_pairs={{0,4},{4,8},{8,12},{12,16},{16,20},{20,24},{24,28},{28,0},{1,5},{5... | collective-permute-start | bytes 393224 | tf_op jit(solution)/shard_map/ppermute | solution.py:40
  11.9 8.2 %collective-permute-start.4 = (bf16[256,256]{1,0:T(8,128)(2,1)S(1)}, bf16[256,256]{1,0:T(8,128)(2,1)S(1)}, u32[]{:S(2)}, u32[]{:S(2)}) collective-permute-start(bf16[256,256]{1,0:T(8,128)(2,1)S(1)} %get-tuple-element.35), channel_id=1, source_target_pairs={{0,8},{4,12},{8,16},{12,20},{16,24},{20,28},{24,0},{28,4},{1,9},{5... | collective-permute-start | bytes 393224 | tf_op jit(solution)/shard_map/ppermute | solution.py:40
  13.5 8.5 %collective-permute-start.5 = (bf16[256,256]{1,0:T(8,128)(2,1)S(1)}, bf16[256,256]{1,0:T(8,128)(2,1)S(1)}, u32[]{:S(2)}, u32[]{:S(2)}) collective-permute-start(bf16[256,256]{1,0:T(8,128)(2,1)S(1)} %get-tuple-element.36), channel_id=1, source_target_pairs={{0,24},{4,28},{8,0},{12,4},{16,8},{20,12},{24,16},{28,20},{1,25},{... | collective-permute-start | bytes 393224 | tf_op jit(solution)/shard_map/ppermute | solution.py:40
  15.8 6.3 %collective-permute-start.6 = (bf16[256,256]{1,0:T(8,128)(2,1)S(1)}, bf16[256,256]{1,0:T(8,128)(2,1)S(1)}, u32[]{:S(2)}, u32[]{:S(2)}) collective-permute-start(bf16[256,256]{1,0:T(8,128)(2,1)S(1)} %get-tuple-element.37), channel_id=1, source_target_pairs={{0,28},{4,0},{8,4},{12,8},{16,12},{20,16},{24,20},{28,24},{1,29},{... | collective-permute-start | bytes 393224 | tf_op jit(solution)/shard_map/ppermute | solution.py:40
  22.9 6.6 %collective-permute-start.13 = (bf16[72,256]{1,0:T(8,128)(2,1)S(1)}, bf16[72,256]{1,0:T(8,128)(2,1)S(1)}, u32[]{:S(2)}, u32[]{:S(2)}) collective-permute-start(bf16[72,256]{1,0:T(8,128)(2,1)S(1)} %get-tuple-element.50), channel_id=1, source_target_pairs={{0,1},{1,0},{2,3},{3,2},{4,5},{5,4},{6,7},{7,6},{8,9},{9,8},{10,11... | collective-permute-start | bytes 110600 | tf_op jit(solution)/shard_map/ppermute | solution.py:45
  22.9 9.2 %collective-permute-start.14 = (bf16[72,256]{1,0:T(8,128)(2,1)S(1)}, bf16[72,256]{1,0:T(8,128)(2,1)S(1)}, u32[]{:S(2)}, u32[]{:S(2)}) collective-permute-start(bf16[72,256]{1,0:T(8,128)(2,1)S(1)} %get-tuple-element.51), channel_id=1, source_target_pairs={{0,2},{1,3},{2,0},{3,1},{4,6},{5,7},{6,4},{7,5},{8,10},{9,11},{10,... | collective-permute-start | bytes 110600 | tf_op jit(solution)/shard_map/ppermute | solution.py:45
  24.5 7.7 %collective-permute-start.15 = (bf16[72,256]{1,0:T(8,128)(2,1)S(1)}, bf16[72,256]{1,0:T(8,128)(2,1)S(1)}, u32[]{:S(2)}, u32[]{:S(2)}) collective-permute-start(bf16[72,256]{1,0:T(8,128)(2,1)S(1)} %get-tuple-element.52), channel_id=1, source_target_pairs={{0,3},{1,2},{2,1},{3,0},{4,7},{5,6},{6,5},{7,4},{8,11},{9,10},{10,... | collective-permute-start | bytes 110600 | tf_op jit(solution)/shard_map/ppermute | solution.py:45
  24.8 11.7 %collective-permute-start.10 = (bf16[256,256]{1,0:T(8,128)(2,1)S(1)}, bf16[256,256]{1,0:T(8,128)(2,1)S(1)}, u32[]{:S(2)}, u32[]{:S(2)}) collective-permute-start(bf16[256,256]{1,0:T(8,128)(2,1)S(1)} %get-tuple-element.39.local), channel_id=1, source_target_pairs={{0,8},{4,12},{8,16},{12,20},{16,24},{20,28},{24,0},{28,4},{1,9},{5... | collective-permute-start | bytes 393224 | tf_op jit(solution)/shard_map/ppermute | solution.py:40
  26.4 12.3 %collective-permute-start.9 = (bf16[256,256]{1,0:T(8,128)(2,1)S(1)}, bf16[256,256]{1,0:T(8,128)(2,1)S(1)}, u32[]{:S(2)}, u32[]{:S(2)}) collective-permute-start(bf16[256,256]{1,0:T(8,128)(2,1)S(1)} %get-tuple-element.39.local), channel_id=1, source_target_pairs={{0,4},{4,8},{8,12},{12,16},{16,20},{20,24},{24,28},{28,0},{1,5},{5... | collective-permute-start | bytes 393224 | tf_op jit(solution)/shard_map/ppermute | solution.py:40
  29.5 9.3 %collective-permute-start.8 = (bf16[256,256]{1,0:T(8,128)(2,1)S(1)}, bf16[256,256]{1,0:T(8,128)(2,1)S(1)}, u32[]{:S(2)}, u32[]{:S(2)}) collective-permute-start(bf16[256,256]{1,0:T(8,128)(2,1)S(1)} %get-tuple-element.39.local), channel_id=1, source_target_pairs={{0,24},{4,28},{8,0},{12,4},{16,8},{20,12},{24,16},{28,20},{1,25},{... | collective-permute-start | bytes 393224 | tf_op jit(solution)/shard_map/ppermute | solution.py:40
  32.2 8.1 %collective-permute-start.7 = (bf16[256,256]{1,0:T(8,128)(2,1)S(1)}, bf16[256,256]{1,0:T(8,128)(2,1)S(1)}, u32[]{:S(2)}, u32[]{:S(2)}) collective-permute-start(bf16[256,256]{1,0:T(8,128)(2,1)S(1)} %get-tuple-element.39.local), channel_id=1, source_target_pairs={{0,28},{4,0},{8,4},{12,8},{16,12},{20,16},{24,20},{28,24},{1,29},{... | collective-permute-start | bytes 393224 | tf_op jit(solution)/shard_map/ppermute | solution.py:40
  32.2 8.1 %copy-start.1 = (bf16[1,1,32,128,128]{4,3,2,1,0:T(8,128)(2,1)S(1)}, bf16[1,1,32,128,128]{4,3,2,1,0:T(8,128)(2,1)}, u32[]{:S(2)}) copy-start(bf16[1,1,32,128,128]{4,3,2,1,0:T(8,128)(2,1)} %copy-done) | copy-start | bytes 3145732
  32.9 7.4 %copy-start.5 = (s32[1,1,32]{2,1,0:T(1,128)S(1)}, s32[1,1,32]{2,1,0:T(1,128)}, u32[]{:S(2)}) copy-start(s32[1,1,32]{2,1,0:T(1,128)} %target.3) | copy-start | bytes 388
  32.9 7.4 %copy-start.7 = (s32[1,1,32]{2,1,0:T(1,128)S(1)}, s32[1,1,32]{2,1,0:T(1,128)}, u32[]{:S(2)}) copy-start(s32[1,1,32]{2,1,0:T(1,128)} %source.3) | copy-start | bytes 388
  33.0 13.0 %all-to-all-start = ((bf16[8,72,256]{2,1,0:T(8,128)(2,1)}), bf16[8,72,256]{2,1,0:T(8,128)(2,1)S(1)}, u32[]{:S(2)}, u32[]{:S(2)}) async-start(bf16[8,72,256]{2,1,0:T(8,128)(2,1)} %weight_column_sum.1), calls=%async_computation | async-start | bytes 589824 | tf_op jit(solution)/shard_map/all_to_all | solution.py:338
  41.7 1.6 %collective-permute-start.11 = (bf16[2,256,256]{2,1,0:T(8,128)(2,1)S(1)}, bf16[2,256,256]{2,1,0:T(8,128)(2,1)S(1)}, u32[]{:S(2)}, u32[]{:S(2)}) collective-permute-start(bf16[2,256,256]{2,1,0:T(8,128)(2,1)S(1)} %get-tuple-element.42), channel_id=1, source_target_pairs={{0,1},{1,0},{2,3},{3,2},{4,5},{5,4},{6,7},{7,6},{8,9},{9,8},{10,11... | collective-permute-start | bytes 786440 | tf_op jit(solution)/shard_map/ppermute | solution.py:45
  43.3 5.6 %collective-permute-start.12 = (bf16[256,256]{1,0:T(8,128)(2,1)S(1)}, bf16[256,256]{1,0:T(8,128)(2,1)S(1)}, u32[]{:S(2)}, u32[]{:S(2)}) collective-permute-start(bf16[256,256]{1,0:T(8,128)(2,1)S(1)} %get-tuple-element.44), channel_id=1, source_target_pairs={{0,2},{1,3},{2,0},{3,1},{4,6},{5,7},{6,4},{7,5},{8,10},{9,11},{10,... | collective-permute-start | bytes 393224 | tf_op jit(solution)/shard_map/ppermute | solution.py:45
  46.0 3.8 %collective-permute-start.18 = (bf16[64,256]{1,0:T(8,128)(2,1)S(1)}, bf16[64,256]{1,0:T(8,128)(2,1)S(1)}, u32[]{:S(2)}, u32[]{:S(2)}) collective-permute-start(bf16[64,256]{1,0:T(8,128)(2,1)S(1)} %get-tuple-element.56.own), channel_id=1, source_target_pairs={{0,3},{1,2},{2,1},{3,0},{4,7},{5,6},{6,5},{7,4},{8,11},{9,10},{10,... | collective-permute-start | bytes 98312 | tf_op jit(solution)/shard_map/ppermute | solution.py:45
  46.1 4.0 %collective-permute-start.17 = (bf16[64,256]{1,0:T(8,128)(2,1)S(1)}, bf16[64,256]{1,0:T(8,128)(2,1)S(1)}, u32[]{:S(2)}, u32[]{:S(2)}) collective-permute-start(bf16[64,256]{1,0:T(8,128)(2,1)S(1)} %get-tuple-element.56.own), channel_id=1, source_target_pairs={{0,2},{1,3},{2,0},{3,1},{4,6},{5,7},{6,4},{7,5},{8,10},{9,11},{10,... | collective-permute-start | bytes 98312 | tf_op jit(solution)/shard_map/ppermute | solution.py:45
  47.6 2.5 %collective-permute-start.16 = (bf16[64,256]{1,0:T(8,128)(2,1)S(1)}, bf16[64,256]{1,0:T(8,128)(2,1)S(1)}, u32[]{:S(2)}, u32[]{:S(2)}) collective-permute-start(bf16[64,256]{1,0:T(8,128)(2,1)S(1)} %get-tuple-element.56.own), channel_id=1, source_target_pairs={{0,1},{1,0},{2,3},{3,2},{4,5},{5,4},{6,7},{7,6},{8,9},{9,8},{10,11... | collective-permute-start | bytes 98312 | tf_op jit(solution)/shard_map/ppermute | solution.py:45

commit v8 on v7

--- a/solution.py
+++ b/solution.py
@@ -62,9 +62,11 @@
     )
 
 
-def for_slots(slot_total, live, step):
-    split = slot_total * 3 // 4
+def for_slots(slot_total, split, live, step):
     for start, stop in ((0, split), (split, slot_total)):
+
+        if start == stop:
+            continue
 
         @pl.when(start < live)
         def _group():
@@ -110,7 +112,7 @@
             values[0, 0, slot], table[place], preferred_element_type=jnp.float32
         )
 
-    for_slots(values.shape[2], live, step)
+    for_slots(values.shape[2], values.shape[2] * 3 // 4, live, step)
     row = lax.axis_index("row")
     offsets = [0] + [offset_at(route, row)[0] for route in FORWARD]
     for offset, out in zip(offsets, (mine, first, second, third, fourth)):
@@ -191,7 +193,7 @@
             table[target[0, 0, slot]], values[0, 0, slot], preferred_element_type=jnp.float32
         )
 
-    for_slots(values.shape[2], live, step)
+    for_slots(values.shape[2], values.shape[2], live, step)
     outs = (mine, leaving.at[0], across, leaving.at[1])
     for relative, out in enumerate(outs):
         for block in range(VB):

time: 51.2 us -> 51.2 us (level)
  transfers between devices with their start and end apart: 20 -> 20, of which waited for: 12 -> 11; matrix products, arithmetic and copies ran while one was open for 0% -> 0% of each run, Pallas kernels for 6% -> 7%
where the time goes in v8:
time: 51.2 us; the launch traced here: 50.9 us
  starting transfers between devices  26.4 us (52%)
  waiting for transfers between devices  14.6 us (29%)
  Pallas kernels  6.32 us (12%)
  local copies, waits for them, and re-layouts  2.17 us (4%)
  between operations  1.46 us (3%)
    ppermute x8, starting transfers between devices, routed(): return lax.ppermute(block, 'row', pairs)  14.3 us
    ppermute x8, waiting for transfers between devices, routed(): return lax.ppermute(block, 'row', pairs)  8.73 us
    ppermute x11, starting transfers between devices, swapped(): return lax.ppermute(block, axis, [(i, i ^ bit) for i in range(size)])  8.49 us
    ppermute x11, waiting for transfers between devices, swapped(): return lax.ppermute(block, axis, [(i, i ^ bit) for i in range(size)])  4.87 us
    all_to_all x1, starting transfers between devices, shards(): received = lax.all_to_all(message, 'row', 0, 0, tiled=True)  3.55 us
    unnamed x22, local copies, waits for them, and re-layouts  2.17 us
    pallas_call x1, Pallas kernels, shards(): call(backward_kernel, [tall, tall, jax.ShapeDtypeStruct((2, width, own_ro...  1.51 us
    pallas_call x1, Pallas kernels, shards(): call(forward_kernel, [wide] + [whole] * 4, [pltpu.VMEM((sources, BLK, wid...  1.36 us
  transfers between devices with their start and end apart: 20, of which 11 were waited for; matrix products, arithmetic and copies ran while one was open for 0% of the time, Pallas kernels for 7%

profile of v8, /device:TPU:0, one launch (start us, length us, event | category | flops | bytes accessed | tf_op | source)
XLA Modules:
  0.0 50.9 jit_solution(2896043731355399463)
XLA Ops:
  0.6 3.0 %collective-permute-start.1 = (bf16[256,256]{1,0:T(8,128)(2,1)}, bf16[256,256]{1,0:T(8,128)(2,1)S(1)}, u32[]{:S(2)}, u32[]{:S(2)}) collective-permute-start(bf16[256,256]{1,0:T(8,128)(2,1)} %own.1), channel_id=1, source_target_pairs={{0,2},{1,3},{2,0},{3,1},{4,6},{5,7},{6,4},{7,5},{8,10},{9,11},{10,... | collective-permute-start | bytes 393224 | tf_op jit(solution)/shard_map/ppermute | solution.py:45
  3.7 1.2 %copy-done.8 = bf16[1,1,32,128,128]{4,3,2,1,0:T(8,128)(2,1)S(1)} copy-done((bf16[1,1,32,128,128]{4,3,2,1,0:T(8,128)(2,1)S(1)}, bf16[1,1,32,128,128]{4,3,2,1,0:T(8,128)(2,1)}, u32[]{:S(2)}) %copy-start.8) | copy-done | bytes 1048600
  4.9 0.9 %copy-done.9 = bf16[256,256]{1,0:T(8,128)(2,1)S(1)} copy-done((bf16[256,256]{1,0:T(8,128)(2,1)S(1)}, bf16[256,256]{1,0:T(8,128)(2,1)}, u32[]{:S(2)}) %copy-start.9) | copy-done | bytes 131096
  6.7 0.6 %collective-permute-done.1.across = bf16[256,256]{1,0:T(8,128)(2,1)S(1)} collective-permute-done((bf16[256,256]{1,0:T(8,128)(2,1)}, bf16[256,256]{1,0:T(8,128)(2,1)S(1)}, u32[]{:S(2)}, u32[]{:S(2)}) %collective-permute-start.1) | collective-permute-done | bytes 131104 | tf_op jit(solution)/shard_map/ppermute | solution.py:45
  7.4 1.3 %collective-permute-done.2.far = bf16[256,256]{1,0:T(8,128)(2,1)S(1)} collective-permute-done((bf16[256,256]{1,0:T(8,128)(2,1)S(1)}, bf16[256,256]{1,0:T(8,128)(2,1)S(1)}, u32[]{:S(2)}, u32[]{:S(2)}) %collective-permute-start.2) | collective-permute-done | bytes 131104 | tf_op jit(solution)/shard_map/ppermute | solution.py:45
  8.7 1.4 %aggregate_terms.1 = (f32[256,256]{1,0:T(8,128)S(1)}, bf16[256,256]{1,0:T(8,128)(2,1)S(1)}, bf16[256,256]{1,0:T(8,128)(2,1)S(1)}, bf16[256,256]{1,0:T(8,128)(2,1)S(1)}, bf16[256,256]{1,0:T(8,128)(2,1)S(1)}) custom-call(s32[1,1]{1,0:T(1,128)S(6)} %copy.12.count, s32[1,1,32]{2,1,0:T(1,128)S(1)} %copy-done.4, s32[1,1,32]{2,1,0:T(1,128)S(1)} %copy-done.6, ...), custom_call_target="tpu_custom_call" | custom-call | flops 268435456 | bytes 1048576 | tf_op jit(solution)/shard_map/aggregate_terms/pallas_call | solution.py:269
  10.1 1.8 %collective-permute-start.3 = (bf16[256,256]{1,0:T(8,128)(2,1)S(1)}, bf16[256,256]{1,0:T(8,128)(2,1)S(1)}, u32[]{:S(2)}, u32[]{:S(2)}) collective-permute-start(bf16[256,256]{1,0:T(8,128)(2,1)S(1)} %get-tuple-element.34), channel_id=1, source_target_pairs={{0,4},{4,8},{8,12},{12,16},{16,20},{20,24},{24,28},{28,0},{1,5},{5... | collective-permute-start | bytes 393224 | tf_op jit(solution)/shard_map/ppermute | solution.py:40
  11.9 1.6 %collective-permute-start.4 = (bf16[256,256]{1,0:T(8,128)(2,1)S(1)}, bf16[256,256]{1,0:T(8,128)(2,1)S(1)}, u32[]{:S(2)}, u32[]{:S(2)}) collective-permute-start(bf16[256,256]{1,0:T(8,128)(2,1)S(1)} %get-tuple-element.35), channel_id=1, source_target_pairs={{0,8},{4,12},{8,16},{12,20},{16,24},{20,28},{24,0},{28,4},{1,9},{5... | collective-permute-start | bytes 393224 | tf_op jit(solution)/shard_map/ppermute | solution.py:40
  13.5 2.2 %collective-permute-start.5 = (bf16[256,256]{1,0:T(8,128)(2,1)S(1)}, bf16[256,256]{1,0:T(8,128)(2,1)S(1)}, u32[]{:S(2)}, u32[]{:S(2)}) collective-permute-start(bf16[256,256]{1,0:T(8,128)(2,1)S(1)} %get-tuple-element.36), channel_id=1, source_target_pairs={{0,24},{4,28},{8,0},{12,4},{16,8},{20,12},{24,16},{28,20},{1,25},{... | collective-permute-start | bytes 393224 | tf_op jit(solution)/shard_map/ppermute | solution.py:40
  15.8 1.3 %collective-permute-start.6 = (bf16[256,256]{1,0:T(8,128)(2,1)S(1)}, bf16[256,256]{1,0:T(8,128)(2,1)S(1)}, u32[]{:S(2)}, u32[]{:S(2)}) collective-permute-start(bf16[256,256]{1,0:T(8,128)(2,1)S(1)} %get-tuple-element.37), channel_id=1, source_target_pairs={{0,28},{4,0},{8,4},{12,8},{16,12},{20,16},{24,20},{28,24},{1,29},{... | collective-permute-start | bytes 393224 | tf_op jit(solution)/shard_map/ppermute | solution.py:40
  17.1 2.3 %collective-permute-done.3.first = bf16[256,256]{1,0:T(8,128)(2,1)S(1)} collective-permute-done((bf16[256,256]{1,0:T(8,128)(2,1)S(1)}, bf16[256,256]{1,0:T(8,128)(2,1)S(1)}, u32[]{:S(2)}, u32[]{:S(2)}) %collective-permute-start.3) | collective-permute-done | bytes 131104 | tf_op jit(solution)/shard_map/ppermute | solution.py:40
  19.4 0.7 %collective-permute-done.4.second = bf16[256,256]{1,0:T(8,128)(2,1)S(1)} collective-permute-done((bf16[256,256]{1,0:T(8,128)(2,1)S(1)}, bf16[256,256]{1,0:T(8,128)(2,1)S(1)}, u32[]{:S(2)}, u32[]{:S(2)}) %collective-permute-start.4) | collective-permute-done | bytes 131104 | tf_op jit(solution)/shard_map/ppermute | solution.py:40
  20.1 1.9 %collective-permute-done.5.third = bf16[256,256]{1,0:T(8,128)(2,1)S(1)} collective-permute-done((bf16[256,256]{1,0:T(8,128)(2,1)S(1)}, bf16[256,256]{1,0:T(8,128)(2,1)S(1)}, u32[]{:S(2)}, u32[]{:S(2)}) %collective-permute-start.5) | collective-permute-done | bytes 131104 | tf_op jit(solution)/shard_map/ppermute | solution.py:40
  22.0 0.6 %pointwise.1 = (bf16[256,256]{1,0:T(8,128)(2,1)S(1)}, bf16[256,256]{1,0:T(8,128)(2,1)S(1)}, bf16[256,256]{1,0:T(8,128)(2,1)S(1)}, bf16[256,256]{1,0:T(8,128)(2,1)S(1)}, f32[1,256]{1,0:T(1,128)S(1)}) custom-call(f32[256,256]{1,0:T(8,128)S(1)} %get-tuple-element.33.mine, bf16[256,256]{1,0:T(8,128)(2,1)S(1)} %collective-permute-done.3.first, ...), custom_call_target="tpu_custom_call" | custom-call | flops 100663296 | bytes 1048576 | tf_op jit(solution)/shard_map/pointwise/pallas_call | solution.py:283
  22.9 1.6 %collective-permute-start.14 = (bf16[72,256]{1,0:T(8,128)(2,1)S(1)}, bf16[72,256]{1,0:T(8,128)(2,1)S(1)}, u32[]{:S(2)}, u32[]{:S(2)}) collective-permute-start(bf16[72,256]{1,0:T(8,128)(2,1)S(1)} %get-tuple-element.51), channel_id=1, source_target_pairs={{0,2},{1,3},{2,0},{3,1},{4,6},{5,7},{6,4},{7,5},{8,10},{9,11},{10,... | collective-permute-start | bytes 110600 | tf_op jit(solution)/shard_map/ppermute | solution.py:45
  24.8 1.6 %collective-permute-start.10 = (bf16[256,256]{1,0:T(8,128)(2,1)S(1)}, bf16[256,256]{1,0:T(8,128)(2,1)S(1)}, u32[]{:S(2)}, u32[]{:S(2)}) collective-permute-start(bf16[256,256]{1,0:T(8,128)(2,1)S(1)} %get-tuple-element.39.local), channel_id=1, source_target_pairs={{0,8},{4,12},{8,16},{12,20},{16,24},{20,28},{24,0},{28,4},{1,9},{5... | collective-permute-start | bytes 393224 | tf_op jit(solution)/shard_map/ppermute | solution.py:40
  26.4 3.0 %collective-permute-start.9 = (bf16[256,256]{1,0:T(8,128)(2,1)S(1)}, bf16[256,256]{1,0:T(8,128)(2,1)S(1)}, u32[]{:S(2)}, u32[]{:S(2)}) collective-permute-start(bf16[256,256]{1,0:T(8,128)(2,1)S(1)} %get-tuple-element.39.local), channel_id=1, source_target_pairs={{0,4},{4,8},{8,12},{12,16},{16,20},{20,24},{24,28},{28,0},{1,5},{5... | collective-permute-start | bytes 393224 | tf_op jit(solution)/shard_map/ppermute | solution.py:40
  29.5 2.7 %collective-permute-start.8 = (bf16[256,256]{1,0:T(8,128)(2,1)S(1)}, bf16[256,256]{1,0:T(8,128)(2,1)S(1)}, u32[]{:S(2)}, u32[]{:S(2)}) collective-permute-start(bf16[256,256]{1,0:T(8,128)(2,1)S(1)} %get-tuple-element.39.local), channel_id=1, source_target_pairs={{0,24},{4,28},{8,0},{12,4},{16,8},{20,12},{24,16},{28,20},{1,25},{... | collective-permute-start | bytes 393224 | tf_op jit(solution)/shard_map/ppermute | solution.py:40
  32.2 0.7 %weight_column_sum.1 = bf16[8,72,256]{2,1,0:T(8,128)(2,1)} custom-call(f32[72,256]{1,0:T(8,128)S(1)} %get-tuple-element.49.mine, bf16[72,256]{1,0:T(8,128)(2,1)S(1)} %collective-permute-done.13.near, bf16[72,256]{1,0:T(8,128)(2,1)S(1)} %collective-permute-done.14.across, bf16[72,256]{1,0:T(8,128)(2,1)S(1)} %collective-permute-done.15.far), custom_call_target="tpu_custom_call" | custom-call | flops 99999997952 | bytes 1048576 | tf_op jit(solution)/shard_map/weight_column_sum/pallas_call | solution.py:303
  33.0 3.6 %all-to-all-start = ((bf16[8,72,256]{2,1,0:T(8,128)(2,1)}), bf16[8,72,256]{2,1,0:T(8,128)(2,1)S(1)}, u32[]{:S(2)}, u32[]{:S(2)}) async-start(bf16[8,72,256]{2,1,0:T(8,128)(2,1)} %weight_column_sum.1), calls=%async_computation | async-start | bytes 589824 | tf_op jit(solution)/shard_map/all_to_all | solution.py:340
  36.5 2.2 %collective-permute-done.9.third = bf16[256,256]{1,0:T(8,128)(2,1)S(1)} collective-permute-done((bf16[256,256]{1,0:T(8,128)(2,1)S(1)}, bf16[256,256]{1,0:T(8,128)(2,1)S(1)}, u32[]{:S(2)}, u32[]{:S(2)}) %collective-permute-start.9) | collective-permute-done | bytes 131104 | tf_op jit(solution)/shard_map/ppermute | solution.py:40
  38.8 1.5 %collective-permute-done.7.first = bf16[256,256]{1,0:T(8,128)(2,1)S(1)} collective-permute-done((bf16[256,256]{1,0:T(8,128)(2,1)S(1)}, bf16[256,256]{1,0:T(8,128)(2,1)S(1)}, u32[]{:S(2)}, u32[]{:S(2)}) %collective-permute-start.7) | collective-permute-done | bytes 131104 | tf_op jit(solution)/shard_map/ppermute | solution.py:40
  40.3 1.5 %source_terms.1 = (f32[256,256]{1,0:T(8,128)S(1)}, f32[256,256]{1,0:T(8,128)S(1)}, bf16[2,256,256]{2,1,0:T(8,128)(2,1)S(1)}) custom-call(s32[1,1]{1,0:T(1,128)S(6)} %copy.12.count, s32[1,1,32]{2,1,0:T(1,128)S(1)} %copy-done.5, s32[1,1,32]{2,1,0:T(1,128)S(1)} %copy-done.7, bf16[1,1,32,128,128]{4,3,2,1,0:T(8,128)(2,1)S(1)} %copy-done.1, ...), custom_call_target="tpu_custom_call" | custom-call | flops 99999997952 | bytes 1048576 | tf_op jit(solution)/shard_map/source_terms/pallas_call | solution.py:317
  41.9 1.5 %collective-permute-done.11.arrived = bf16[2,256,256]{2,1,0:T(8,128)(2,1)S(1)} collective-permute-done((bf16[2,256,256]{2,1,0:T(8,128)(2,1)S(1)}, bf16[2,256,256]{2,1,0:T(8,128)(2,1)S(1)}, u32[]{:S(2)}, u32[]{:S(2)}) %collective-permute-start.11) | collective-permute-done | bytes 262176 | tf_op jit(solution)/shard_map/ppermute | solution.py:45
  43.5 1.6 %collective-permute-start.12 = (bf16[256,256]{1,0:T(8,128)(2,1)S(1)}, bf16[256,256]{1,0:T(8,128)(2,1)S(1)}, u32[]{:S(2)}, u32[]{:S(2)}) collective-permute-start(bf16[256,256]{1,0:T(8,128)(2,1)S(1)} %get-tuple-element.44), channel_id=1, source_target_pairs={{0,2},{1,3},{2,0},{3,1},{4,6},{5,7},{6,4},{7,5},{8,10},{9,11},{10,... | collective-permute-start | bytes 393224 | tf_op jit(solution)/shard_map/ppermute | solution.py:45
  45.0 1.0 %all-to-all-done.received = bf16[8,72,256]{2,1,0:T(8,128)(2,1)S(1)} async-done(((bf16[8,72,256]{2,1,0:T(8,128)(2,1)}), bf16[8,72,256]{2,1,0:T(8,128)(2,1)S(1)}, u32[]{:S(2)}, u32[]{:S(2)}) %all-to-all-start) | async-done | bytes 294944 | tf_op jit(solution)/shard_map/all_to_all | solution.py:340
  46.1 1.5 %collective-permute-start.17 = (bf16[64,256]{1,0:T(8,128)(2,1)S(1)}, bf16[64,256]{1,0:T(8,128)(2,1)S(1)}, u32[]{:S(2)}, u32[]{:S(2)}) collective-permute-start(bf16[64,256]{1,0:T(8,128)(2,1)S(1)} %get-tuple-element.56.own), channel_id=1, source_target_pairs={{0,2},{1,3},{2,0},{3,1},{4,6},{5,7},{6,4},{7,5},{8,10},{9,11},{10,... | collective-permute-start | bytes 98312 | tf_op jit(solution)/shard_map/ppermute | solution.py:45
  47.6 0.3 collective-permute-start.16
  48.0 1.1 %collective-permute-done.12.arrived = bf16[256,256]{1,0:T(8,128)(2,1)S(1)} collective-permute-done((bf16[256,256]{1,0:T(8,128)(2,1)S(1)}, bf16[256,256]{1,0:T(8,128)(2,1)S(1)}, u32[]{:S(2)}, u32[]{:S(2)}) %collective-permute-start.12) | collective-permute-done | bytes 131104 | tf_op jit(solution)/shard_map/ppermute | solution.py:45
  49.1 0.8 %source_sum.1 = (bf16[256,256]{1,0:T(8,128)(2,1)}, bf16[256,256]{1,0:T(8,128)(2,1)}, f32[1,256]{1,0:T(1,128)}) custom-call(f32[256,256]{1,0:T(8,128)S(1)} %get-tuple-element.43.mine, bf16[256,256]{1,0:T(8,128)(2,1)S(1)} %collective-permute-done.12.arrived, bf16[256,256]{1,0:T(8,128)(2,1)S(1)} %get-tuple-element.45.output_in, ...), custom_call_target="tpu_custom_call" | custom-call | flops 99999997952 | bytes 1048576 | tf_op jit(solution)/shard_map/source_sum/pallas_call | solution.py:351
  49.8 0.3 collective-permute-done.17.across
  50.2 0.7 %weight_join.1 = f32[256,256]{1,0:T(8,128)} custom-call(bf16[64,256]{1,0:T(8,128)(2,1)S(1)} %get-tuple-element.56.own, bf16[64,256]{1,0:T(8,128)(2,1)S(1)} %collective-permute-done.16.near, bf16[64,256]{1,0:T(8,128)(2,1)S(1)} %collective-permute-done.17.across, bf16[64,256]{1,0:T(8,128)(2,1)S(1)} %collective-permute-done.18.far), custom_call_target="tpu_custom_call" | custom-call | flops 99999997952 | bytes 1048576 | tf_op jit(solution)/shard_map/weight_join/pallas_call | solution.py:359
  (41 shorter events, 1.2 us)
Async XLA Ops:
  0.6 3.0 %copy-start.10 = (f32[256]{0:T(256)S(1)}, f32[256]{0:T(256)}, u32[]{:S(2)}) copy-start(f32[256]{0:T(256)} %param.10) | copy-start | bytes 3076
  0.6 6.7 %collective-permute-start.1 = (bf16[256,256]{1,0:T(8,128)(2,1)}, bf16[256,256]{1,0:T(8,128)(2,1)S(1)}, u32[]{:S(2)}, u32[]{:S(2)}) collective-permute-start(bf16[256,256]{1,0:T(8,128)(2,1)} %own.1), channel_id=1, source_target_pairs={{0,2},{1,3},{2,0},{3,1},{4,6},{5,7},{6,4},{7,5},{8,10},{9,11},{10,... | collective-permute-start | bytes 393224 | tf_op jit(solution)/shard_map/ppermute | solution.py:45
  3.6 3.7 %collective-permute-start = (bf16[256,256]{1,0:T(8,128)(2,1)}, bf16[256,256]{1,0:T(8,128)(2,1)S(1)}, u32[]{:S(2)}, u32[]{:S(2)}) collective-permute-start(bf16[256,256]{1,0:T(8,128)(2,1)} %own.1), channel_id=1, source_target_pairs={{0,1},{1,0},{2,3},{3,2},{4,5},{5,4},{6,7},{7,6},{8,9},{9,8},{10,11... | collective-permute-start | bytes 393224 | tf_op jit(solution)/shard_map/ppermute | solution.py:45
  3.7 1.2 %copy-start.8 = (bf16[1,1,32,128,128]{4,3,2,1,0:T(8,128)(2,1)S(1)}, bf16[1,1,32,128,128]{4,3,2,1,0:T(8,128)(2,1)}, u32[]{:S(2)}) copy-start(bf16[1,1,32,128,128]{4,3,2,1,0:T(8,128)(2,1)} %values.1) | copy-start | bytes 3145732
  4.9 0.9 %copy-start.9 = (bf16[256,256]{1,0:T(8,128)(2,1)S(1)}, bf16[256,256]{1,0:T(8,128)(2,1)}, u32[]{:S(2)}) copy-start(bf16[256,256]{1,0:T(8,128)(2,1)} %own.1) | copy-start | bytes 393220
  6.1 2.6 %copy-start = (bf16[1,1,32,128,128]{4,3,2,1,0:T(8,128)(2,1)}, bf16[1,1,32,128,128]{4,3,2,1,0:T(8,128)(2,1)S(1)}, u32[]{:S(2)}) copy-start(bf16[1,1,32,128,128]{4,3,2,1,0:T(8,128)(2,1)S(1)} %get-tuple-element.31.values) | copy-start | bytes 3145732
  7.4 1.3 %collective-permute-start.2 = (bf16[256,256]{1,0:T(8,128)(2,1)S(1)}, bf16[256,256]{1,0:T(8,128)(2,1)S(1)}, u32[]{:S(2)}, u32[]{:S(2)}) collective-permute-start(bf16[256,256]{1,0:T(8,128)(2,1)S(1)} %collective-permute-done.1.across), channel_id=1, source_target_pairs={{0,1},{1,0},{2,3},{3,2},{4,5},{5,4},{6,7},{7,6},{8,9},{9,8},{10,11... | collective-permute-start | bytes 393224 | tf_op jit(solution)/shard_map/ppermute | solution.py:45
  7.4 1.3 %copy-start.4 = (s32[1,1,32]{2,1,0:T(1,128)S(1)}, s32[1,1,32]{2,1,0:T(1,128)}, u32[]{:S(2)}) copy-start(s32[1,1,32]{2,1,0:T(1,128)} %target.3) | copy-start | bytes 388
  7.4 1.3 %copy-start.6 = (s32[1,1,32]{2,1,0:T(1,128)S(1)}, s32[1,1,32]{2,1,0:T(1,128)}, u32[]{:S(2)}) copy-start(s32[1,1,32]{2,1,0:T(1,128)} %source.3) | copy-start | bytes 388
  8.7 13.3 %copy-start.2 = (bf16[256,256]{1,0:T(8,128)(2,1)S(1)}, bf16[256,256]{1,0:T(8,128)(2,1)}, u32[]{:S(2)}) copy-start(bf16[256,256]{1,0:T(8,128)(2,1)} %weight.1) | copy-start | bytes 393220
  8.7 13.3 %copy-start.3 = (bf16[256,256]{1,0:T(8,128)(2,1)S(1)}, bf16[256,256]{1,0:T(8,128)(2,1)}, u32[]{:S(2)}) copy-start(bf16[256,256]{1,0:T(8,128)(2,1)} %cotangent.1) | copy-start | bytes 393220
  10.1 9.3 %collective-permute-start.3 = (bf16[256,256]{1,0:T(8,128)(2,1)S(1)}, bf16[256,256]{1,0:T(8,128)(2,1)S(1)}, u32[]{:S(2)}, u32[]{:S(2)}) collective-permute-start(bf16[256,256]{1,0:T(8,128)(2,1)S(1)} %get-tuple-element.34), channel_id=1, source_target_pairs={{0,4},{4,8},{8,12},{12,16},{16,20},{20,24},{24,28},{28,0},{1,5},{5... | collective-permute-start | bytes 393224 | tf_op jit(solution)/shard_map/ppermute | solution.py:40
  11.9 8.2 %collective-permute-start.4 = (bf16[256,256]{1,0:T(8,128)(2,1)S(1)}, bf16[256,256]{1,0:T(8,128)(2,1)S(1)}, u32[]{:S(2)}, u32[]{:S(2)}) collective-permute-start(bf16[256,256]{1,0:T(8,128)(2,1)S(1)} %get-tuple-element.35), channel_id=1, source_target_pairs={{0,8},{4,12},{8,16},{12,20},{16,24},{20,28},{24,0},{28,4},{1,9},{5... | collective-permute-start | bytes 393224 | tf_op jit(solution)/shard_map/ppermute | solution.py:40
  13.5 8.5 %collective-permute-start.5 = (bf16[256,256]{1,0:T(8,128)(2,1)S(1)}, bf16[256,256]{1,0:T(8,128)(2,1)S(1)}, u32[]{:S(2)}, u32[]{:S(2)}) collective-permute-start(bf16[256,256]{1,0:T(8,128)(2,1)S(1)} %get-tuple-element.36), channel_id=1, source_target_pairs={{0,24},{4,28},{8,0},{12,4},{16,8},{20,12},{24,16},{28,20},{1,25},{... | collective-permute-start | bytes 393224 | tf_op jit(solution)/shard_map/ppermute | solution.py:40
  15.8 6.3 %collective-permute-start.6 = (bf16[256,256]{1,0:T(8,128)(2,1)S(1)}, bf16[256,256]{1,0:T(8,128)(2,1)S(1)}, u32[]{:S(2)}, u32[]{:S(2)}) collective-permute-start(bf16[256,256]{1,0:T(8,128)(2,1)S(1)} %get-tuple-element.37), channel_id=1, source_target_pairs={{0,28},{4,0},{8,4},{12,8},{16,12},{20,16},{24,20},{28,24},{1,29},{... | collective-permute-start | bytes 393224 | tf_op jit(solution)/shard_map/ppermute | solution.py:40
  22.9 6.6 %collective-permute-start.13 = (bf16[72,256]{1,0:T(8,128)(2,1)S(1)}, bf16[72,256]{1,0:T(8,128)(2,1)S(1)}, u32[]{:S(2)}, u32[]{:S(2)}) collective-permute-start(bf16[72,256]{1,0:T(8,128)(2,1)S(1)} %get-tuple-element.50), channel_id=1, source_target_pairs={{0,1},{1,0},{2,3},{3,2},{4,5},{5,4},{6,7},{7,6},{8,9},{9,8},{10,11... | collective-permute-start | bytes 110600 | tf_op jit(solution)/shard_map/ppermute | solution.py:45
  22.9 9.2 %collective-permute-start.14 = (bf16[72,256]{1,0:T(8,128)(2,1)S(1)}, bf16[72,256]{1,0:T(8,128)(2,1)S(1)}, u32[]{:S(2)}, u32[]{:S(2)}) collective-permute-start(bf16[72,256]{1,0:T(8,128)(2,1)S(1)} %get-tuple-element.51), channel_id=1, source_target_pairs={{0,2},{1,3},{2,0},{3,1},{4,6},{5,7},{6,4},{7,5},{8,10},{9,11},{10,... | collective-permute-start | bytes 110600 | tf_op jit(solution)/shard_map/ppermute | solution.py:45
  24.5 7.7 %collective-permute-start.15 = (bf16[72,256]{1,0:T(8,128)(2,1)S(1)}, bf16[72,256]{1,0:T(8,128)(2,1)S(1)}, u32[]{:S(2)}, u32[]{:S(2)}) collective-permute-start(bf16[72,256]{1,0:T(8,128)(2,1)S(1)} %get-tuple-element.52), channel_id=1, source_target_pairs={{0,3},{1,2},{2,1},{3,0},{4,7},{5,6},{6,5},{7,4},{8,11},{9,10},{10,... | collective-permute-start | bytes 110600 | tf_op jit(solution)/shard_map/ppermute | solution.py:45
  24.8 11.7 %collective-permute-start.10 = (bf16[256,256]{1,0:T(8,128)(2,1)S(1)}, bf16[256,256]{1,0:T(8,128)(2,1)S(1)}, u32[]{:S(2)}, u32[]{:S(2)}) collective-permute-start(bf16[256,256]{1,0:T(8,128)(2,1)S(1)} %get-tuple-element.39.local), channel_id=1, source_target_pairs={{0,8},{4,12},{8,16},{12,20},{16,24},{20,28},{24,0},{28,4},{1,9},{5... | collective-permute-start | bytes 393224 | tf_op jit(solution)/shard_map/ppermute | solution.py:40
  26.4 12.3 %collective-permute-start.9 = (bf16[256,256]{1,0:T(8,128)(2,1)S(1)}, bf16[256,256]{1,0:T(8,128)(2,1)S(1)}, u32[]{:S(2)}, u32[]{:S(2)}) collective-permute-start(bf16[256,256]{1,0:T(8,128)(2,1)S(1)} %get-tuple-element.39.local), channel_id=1, source_target_pairs={{0,4},{4,8},{8,12},{12,16},{16,20},{20,24},{24,28},{28,0},{1,5},{5... | collective-permute-start | bytes 393224 | tf_op jit(solution)/shard_map/ppermute | solution.py:40
  29.5 9.3 %collective-permute-start.8 = (bf16[256,256]{1,0:T(8,128)(2,1)S(1)}, bf16[256,256]{1,0:T(8,128)(2,1)S(1)}, u32[]{:S(2)}, u32[]{:S(2)}) collective-permute-start(bf16[256,256]{1,0:T(8,128)(2,1)S(1)} %get-tuple-element.39.local), channel_id=1, source_target_pairs={{0,24},{4,28},{8,0},{12,4},{16,8},{20,12},{24,16},{28,20},{1,25},{... | collective-permute-start | bytes 393224 | tf_op jit(solution)/shard_map/ppermute | solution.py:40
  32.2 8.1 %collective-permute-start.7 = (bf16[256,256]{1,0:T(8,128)(2,1)S(1)}, bf16[256,256]{1,0:T(8,128)(2,1)S(1)}, u32[]{:S(2)}, u32[]{:S(2)}) collective-permute-start(bf16[256,256]{1,0:T(8,128)(2,1)S(1)} %get-tuple-element.39.local), channel_id=1, source_target_pairs={{0,28},{4,0},{8,4},{12,8},{16,12},{20,16},{24,20},{28,24},{1,29},{... | collective-permute-start | bytes 393224 | tf_op jit(solution)/shard_map/ppermute | solution.py:40
  32.2 8.1 %copy-start.1 = (bf16[1,1,32,128,128]{4,3,2,1,0:T(8,128)(2,1)S(1)}, bf16[1,1,32,128,128]{4,3,2,1,0:T(8,128)(2,1)}, u32[]{:S(2)}) copy-start(bf16[1,1,32,128,128]{4,3,2,1,0:T(8,128)(2,1)} %copy-done) | copy-start | bytes 3145732
  32.9 7.4 %copy-start.5 = (s32[1,1,32]{2,1,0:T(1,128)S(1)}, s32[1,1,32]{2,1,0:T(1,128)}, u32[]{:S(2)}) copy-start(s32[1,1,32]{2,1,0:T(1,128)} %target.3) | copy-start | bytes 388
  32.9 7.4 %copy-start.7 = (s32[1,1,32]{2,1,0:T(1,128)S(1)}, s32[1,1,32]{2,1,0:T(1,128)}, u32[]{:S(2)}) copy-start(s32[1,1,32]{2,1,0:T(1,128)} %source.3) | copy-start | bytes 388
  33.0 13.0 %all-to-all-start = ((bf16[8,72,256]{2,1,0:T(8,128)(2,1)}), bf16[8,72,256]{2,1,0:T(8,128)(2,1)S(1)}, u32[]{:S(2)}, u32[]{:S(2)}) async-start(bf16[8,72,256]{2,1,0:T(8,128)(2,1)} %weight_column_sum.1), calls=%async_computation | async-start | bytes 589824 | tf_op jit(solution)/shard_map/all_to_all | solution.py:340
  41.8 1.6 %collective-permute-start.11 = (bf16[2,256,256]{2,1,0:T(8,128)(2,1)S(1)}, bf16[2,256,256]{2,1,0:T(8,128)(2,1)S(1)}, u32[]{:S(2)}, u32[]{:S(2)}) collective-permute-start(bf16[2,256,256]{2,1,0:T(8,128)(2,1)S(1)} %get-tuple-element.42), channel_id=1, source_target_pairs={{0,1},{1,0},{2,3},{3,2},{4,5},{5,4},{6,7},{7,6},{8,9},{9,8},{10,11... | collective-permute-start | bytes 786440 | tf_op jit(solution)/shard_map/ppermute | solution.py:45
  43.5 5.6 %collective-permute-start.12 = (bf16[256,256]{1,0:T(8,128)(2,1)S(1)}, bf16[256,256]{1,0:T(8,128)(2,1)S(1)}, u32[]{:S(2)}, u32[]{:S(2)}) collective-permute-start(bf16[256,256]{1,0:T(8,128)(2,1)S(1)} %get-tuple-element.44), channel_id=1, source_target_pairs={{0,2},{1,3},{2,0},{3,1},{4,6},{5,7},{6,4},{7,5},{8,10},{9,11},{10,... | collective-permute-start | bytes 393224 | tf_op jit(solution)/shard_map/ppermute | solution.py:45
  46.0 3.8 %collective-permute-start.18 = (bf16[64,256]{1,0:T(8,128)(2,1)S(1)}, bf16[64,256]{1,0:T(8,128)(2,1)S(1)}, u32[]{:S(2)}, u32[]{:S(2)}) collective-permute-start(bf16[64,256]{1,0:T(8,128)(2,1)S(1)} %get-tuple-element.56.own), channel_id=1, source_target_pairs={{0,3},{1,2},{2,1},{3,0},{4,7},{5,6},{6,5},{7,4},{8,11},{9,10},{10,... | collective-permute-start | bytes 98312 | tf_op jit(solution)/shard_map/ppermute | solution.py:45
  46.1 4.0 %collective-permute-start.17 = (bf16[64,256]{1,0:T(8,128)(2,1)S(1)}, bf16[64,256]{1,0:T(8,128)(2,1)S(1)}, u32[]{:S(2)}, u32[]{:S(2)}) collective-permute-start(bf16[64,256]{1,0:T(8,128)(2,1)S(1)} %get-tuple-element.56.own), channel_id=1, source_target_pairs={{0,2},{1,3},{2,0},{3,1},{4,6},{5,7},{6,4},{7,5},{8,10},{9,11},{10,... | collective-permute-start | bytes 98312 | tf_op jit(solution)/shard_map/ppermute | solution.py:45
  47.6 2.5 %collective-permute-start.16 = (bf16[64,256]{1,0:T(8,128)(2,1)S(1)}, bf16[64,256]{1,0:T(8,128)(2,1)S(1)}, u32[]{:S(2)}, u32[]{:S(2)}) collective-permute-start(bf16[64,256]{1,0:T(8,128)(2,1)S(1)} %get-tuple-element.56.own), channel_id=1, source_target_pairs={{0,1},{1,0},{2,3},{3,2},{4,5},{5,4},{6,7},{7,6},{8,9},{9,8},{10,11... | collective-permute-start | bytes 98312 | tf_op jit(solution)/shard_map/ppermute | solution.py:45
